TPU v7x, 128 devices: a whole 4x4x4 slice. The times are simulated.
128 devices in a mesh: seq: 32 (over x_hi, z, y), row: 4 (over x_lo, core).
Axes of the slice: x: 4 (x_hi: 2, x_lo: 2; x = x_hi * 2 + x_lo), y: 4, z: 4, core: 2. Of those that a mesh axis runs over, the one named last changes fastest.
Arguments:
- activations: bfloat16 [256, 256, 1024], P('seq', 'row'), may hold values from -6 to 6
- noise_embed: bfloat16 [256, 1024], P('seq'), may hold values from -6 to 6
- frame_position: int32 [256], P('seq'), may hold values from 0 to 7, as said below
- cotangent: bfloat16 [256, 256, 1024], P('seq', 'row'), may hold values from -6 to 6
- ada_weight: bfloat16 [1024, 6144], P('row'), may hold values from -0.1875 to 0.1875
- ada_bias: bfloat16 [6144], P('row'), may hold values from -3 to 3
- qkv_weight: bfloat16 [1024, 3072], P('row'), may hold values from -0.1875 to 0.1875
- qkv_bias: bfloat16 [3072], P('row'), may hold values from -3 to 3
- out_weight: bfloat16 [1024, 1024], P('row'), may hold values from -0.75 to 0.75
- out_bias: bfloat16 [1024], P('row'), may hold values from -3 to 3
- up_weight: bfloat16 [1024, 4096], P('row'), may hold values from -0.1875 to 0.1875
- up_bias: bfloat16 [4096], P('row'), may hold values from -3 to 3
- down_weight: bfloat16 [4096, 1024], P('row'), may hold values from -0.09375 to 0.09375
- down_bias: bfloat16 [1024], P('row'), may hold values from -3 to 3
Outputs:
- layer_output: bfloat16 [256, 256, 1024], P('seq', 'row')
- input_grad: float32 [256, 256, 1024], P('seq', 'row')
- embed_grad: float32 [256, 1024], P('seq')
- ada_weight_grad: float32 [1024, 6144], P('row')
- ada_bias_grad: float32 [6144], P('row')
- qkv_weight_grad: float32 [1024, 3072], P('row')
- qkv_bias_grad: float32 [3072], P('row')
- out_weight_grad: float32 [1024, 1024], P('row')
- out_bias_grad: float32 [1024], P('row')
- up_weight_grad: float32 [1024, 4096], P('row')
- up_bias_grad: float32 [4096], P('row')
- down_weight_grad: float32 [4096, 1024], P('row')
- down_bias_grad: float32 [1024], P('row')
Inputs may be any that keep to these rules, and one draw needn't show every extreme that they name: frame_position[f] is the place of frame f in its clip: 0 where a clip begins, else one more than at frame f - 1; a clip holds 1 to 8 frames, and frames 0 to 7 form one clip.
All inputs are finite; a program needn't handle non-finite values.
Results may differ from a plain program's by a relative error of at most 0.028.
The roundings to bfloat16 on the way count: a program that leaves them out, or rounds other values in their place, can miss the bound.
Values may be sent and summed in bfloat16 or wider, within the bound.
No kernel may reach another device: no remote copies, remote signals or barrier semaphores. Data moves between devices by JAX's collectives and lax.ppermute only.
A program may use at most 320 MiB of HBM per device.

v0:
```python
import math

import jax
import jax.numpy as jnp
from jax import lax
from jax.sharding import PartitionSpec as P

H = 16
HD = 64
GRID = 16
MOST = 8


def shifted(value, axis, steps):
    count = lax.axis_size(axis)
    leading, last = (max(0, -steps), min(count, count - steps))
    return lax.ppermute(value, axis, [(source, source + steps) for source in range(leading, last)])


def layer_norm(values):
    center = values - jnp.mean(values, axis=-1, keepdims=True)
    spread = jnp.mean(center * center, axis=-1, keepdims=True)
    return center * lax.rsqrt(spread + 1e-06)


def modulate(values, shifts, scales):
    return layer_norm(values) * (1.0 + scales) + shifts


def gelu_tanh(values):
    return jax.nn.gelu(values, approximate=True)


def rotary_angles(frame_place, patch_row, patch_col, half_dim):
    pair_index = jnp.arange(half_dim).astype(jnp.float32)
    quarter = half_dim // 2
    eighth = half_dim // 4
    in_frame = pair_index < quarter
    in_row = jnp.logical_and(pair_index >= quarter, pair_index < quarter + eighth)
    offset = jnp.where(
        in_frame, pair_index, jnp.where(in_row, pair_index - quarter, pair_index - quarter - eighth)
    )
    length = jnp.where(in_frame, 1.0 * quarter, 1.0 * eighth)
    frequency = jnp.exp(-math.log(10000.0) * offset / length)
    position = jnp.where(
        in_frame, frame_place[:, None], jnp.where(in_row, patch_row[:, None], patch_col[:, None])
    )
    angle_table = position * frequency
    return (jnp.cos(angle_table)[:, None, :], jnp.sin(angle_table)[:, None, :])


def rotate(values, cosine, sine):
    half_dim = values.shape[-1] // 2
    front_half = values[..., :half_dim]
    back_half = values[..., half_dim:]
    return jnp.concatenate(
        [front_half * cosine - back_half * sine, front_half * sine + back_half * cosine], axis=-1
    )


def block_mask(
    seq_index, frame_count, first_frame, block_frames, key_frames, places, row_count, patch_count
):
    query_frame = seq_index * frame_count + first_frame + jnp.arange(block_frames, dtype=jnp.int32)
    key_frame = (
        (seq_index - 1) * frame_count
        + frame_count
        + first_frame
        - (MOST - 1)
        + jnp.arange(key_frames, dtype=jnp.int32)
    )
    frame_gap = query_frame[:, None] - key_frame[None, :]
    frame_ok = (frame_gap >= 0) & (frame_gap <= places[:, None]) & (key_frame[None, :] >= 0)
    return jnp.repeat(jnp.repeat(frame_ok, row_count, axis=0), patch_count, axis=1)


def attention_plan(span, row_rep, patch_count, frame_count):
    local_heads = span // HD
    group_size = math.gcd(local_heads, max(1, 128 // HD))
    group_total = local_heads // group_size
    columns = group_size * HD
    block_frames = min(frame_count, max(1, 512 // row_rep))
    key_frames = MOST - 1 + block_frames
    return (
        group_size,
        group_total,
        columns,
        block_frames,
        key_frames,
        block_frames * row_rep,
        key_frames * patch_count,
        frame_count // block_frames,
    )


def per_device(
    activations,
    noise_embed,
    frame_position,
    cotangent,
    ada_weight,
    ada_bias,
    qkv_weight,
    qkv_bias,
    out_weight,
    out_bias,
    up_weight,
    up_bias,
    down_weight,
    down_bias,
):
    frame_count, row_count, width = activations.shape
    token_count = frame_count * row_count
    seq_index = lax.axis_index("seq")
    row_index = lax.axis_index("row")
    scale_factor = HD ** (-0.5)
    ada_w, ada_b, qkv_w, qkv_b, out_w, out_b, up_w, up_b, down_w, down_b = (
        lax.all_gather(ada_weight, "row", axis=0, tiled=True),
        lax.all_gather(ada_bias, "row", axis=0, tiled=True),
        lax.all_gather(qkv_weight, "row", axis=0, tiled=True),
        lax.all_gather(qkv_bias, "row", axis=0, tiled=True),
        lax.all_gather(out_weight, "row", axis=0, tiled=True),
        lax.all_gather(out_bias, "row", axis=0, tiled=True),
        lax.all_gather(up_weight, "row", axis=0, tiled=True),
        lax.all_gather(up_bias, "row", axis=0, tiled=True),
        lax.all_gather(down_weight, "row", axis=0, tiled=True),
        lax.all_gather(down_bias, "row", axis=0, tiled=True),
    )
    embedding = noise_embed.astype(jnp.float32)
    silu_value, silu_back = jax.vjp(jax.nn.silu, embedding)
    silu_embed = silu_value.astype(jnp.bfloat16)
    modulation = jnp.dot(silu_embed, ada_w, preferred_element_type=jnp.float32) + ada_b.astype(
        jnp.float32
    )
    modulation_parts = [
        modulation[:, None, segment * width : (segment + 1) * width] for segment in range(6)
    ]
    shift_one, scale_one, gate_one, shift_two, scale_two, gate_two = modulation_parts
    inputs = activations.astype(jnp.float32)
    first_value, first_back = jax.vjp(modulate, inputs, shift_one, scale_one)
    hidden_one = first_value.astype(jnp.bfloat16).reshape(token_count, width)
    projected = jnp.dot(hidden_one, qkv_w, preferred_element_type=jnp.float32) + qkv_b.astype(
        jnp.float32
    )
    patch_index = row_index * row_count + jnp.arange(row_count, dtype=jnp.int32)
    patch_row = jnp.tile(patch_index // GRID, frame_count).astype(jnp.float32)
    patch_col = jnp.tile(patch_index % GRID, frame_count).astype(jnp.float32)
    frame_place = jnp.repeat(frame_position, row_count).astype(jnp.float32)
    cosine, sine = rotary_angles(frame_place, patch_row, patch_col, HD // 2)
    queries = (
        rotate(projected[:, :width].reshape(token_count, H, HD), cosine, sine)
        .astype(jnp.bfloat16)
        .reshape(token_count, width)
    )
    keys_now = (
        rotate(projected[:, width : 2 * width].reshape(token_count, H, HD), cosine, sine)
        .astype(jnp.bfloat16)
        .reshape(frame_count, row_count, width)
    )
    values_now = (
        projected[:, 2 * width :].astype(jnp.bfloat16).reshape(frame_count, row_count, width)
    )
    earlier_keys, earlier_values = shifted((keys_now, values_now), "seq", 1)
    key_window = jnp.concatenate([earlier_keys, keys_now], axis=0)
    value_window = jnp.concatenate([earlier_values, values_now], axis=0)
    key_full, value_full = (
        lax.all_gather(key_window, "row", axis=1, tiled=True),
        lax.all_gather(value_window, "row", axis=1, tiled=True),
    )
    span = queries.shape[1]
    patch_count = key_full.shape[1]
    (
        group_size,
        group_total,
        columns,
        block_frames,
        key_frames,
        block_rows,
        key_rows,
        block_total,
    ) = attention_plan(span, row_count, patch_count, frame_count)

    def block_inputs(block_index):
        first_frame = block_index * block_frames
        key_start = frame_count + first_frame - (MOST - 1)
        key_block = lax.dynamic_slice_in_dim(key_full, key_start, key_frames, 0).reshape(
            key_rows, span
        )
        value_block = lax.dynamic_slice_in_dim(value_full, key_start, key_frames, 0).reshape(
            key_rows, span
        )
        allowed = block_mask(
            seq_index,
            frame_count,
            first_frame,
            block_frames,
            key_frames,
            frame_position,
            row_count,
            patch_count,
        )
        return (first_frame, key_start, queries, key_block, value_block, allowed)

    def head_slices(query_block, key_block, value_block, group_index):
        column_start = group_index * columns
        query_part = lax.dynamic_slice_in_dim(query_block, column_start, columns, 1).reshape(
            block_rows, group_size, HD
        )
        key_part = lax.dynamic_slice_in_dim(key_block, column_start, columns, 1).reshape(
            key_rows, group_size, HD
        )
        value_part = lax.dynamic_slice_in_dim(value_block, column_start, columns, 1).reshape(
            key_rows, group_size, HD
        )
        return (query_part, key_part, value_part)

    def masked_scores(query_part, key_part, allowed):
        scores = (
            jnp.einsum("qhd,khd->hqk", query_part, key_part, preferred_element_type=jnp.float32)
            * scale_factor
        )
        return jnp.where(allowed[None], scores, -1e30)

    def attend(block_index):
        first_frame, key_start, query_block, key_block, value_block, allowed = block_inputs(
            block_index
        )

        def one_group(group_index):
            query_part, key_part, value_part = head_slices(
                query_block, key_block, value_block, group_index
            )
            scores = masked_scores(query_part, key_part, allowed)
            largest = jnp.max(scores, axis=-1, keepdims=True)
            exponent = jnp.exp(scores - largest)
            row_total = jnp.sum(exponent, axis=-1, keepdims=True)
            softmax_weights = exponent / row_total
            mixture = jnp.einsum(
                "hqk,khd->qhd",
                softmax_weights.astype(jnp.bfloat16),
                value_part,
                preferred_element_type=jnp.float32,
            )
            return (mixture.reshape(block_rows, columns), (largest + jnp.log(row_total))[..., 0])

        mixture, group_lse = lax.map(one_group, jnp.arange(group_total))
        return (jnp.transpose(mixture, (1, 0, 2)).reshape(block_rows, span), group_lse)

    attended_blocks, log_totals = lax.map(attend, jnp.arange(block_total))
    attended_local = attended_blocks.reshape(frame_count * row_count, span).astype(jnp.bfloat16)
    branch = (
        jnp.dot(attended_local, out_w, preferred_element_type=jnp.float32)
        + out_b.astype(jnp.float32)
    ).reshape(frame_count, row_count, width)
    middle = inputs + gate_one * branch
    second_value, second_back = jax.vjp(modulate, middle, shift_two, scale_two)
    hidden_two = second_value.astype(jnp.bfloat16).reshape(token_count, width)
    upward = jnp.dot(hidden_two, up_w, preferred_element_type=jnp.float32) + up_b.astype(
        jnp.float32
    )
    gelu_value, gelu_back = jax.vjp(gelu_tanh, upward)
    activated = gelu_value.astype(jnp.bfloat16)
    downward = (
        jnp.dot(activated, down_w, preferred_element_type=jnp.float32) + down_b.astype(jnp.float32)
    ).reshape(frame_count, row_count, width)
    layer_output = (middle + gate_two * downward).astype(jnp.bfloat16)
    ada_w, ada_b, qkv_w, qkv_b, out_w, out_b, up_w, up_b, down_w, down_b = (
        lax.all_gather(ada_weight, "row", axis=0, tiled=True),
        lax.all_gather(ada_bias, "row", axis=0, tiled=True),
        lax.all_gather(qkv_weight, "row", axis=0, tiled=True),
        lax.all_gather(qkv_bias, "row", axis=0, tiled=True),
        lax.all_gather(out_weight, "row", axis=0, tiled=True),
        lax.all_gather(out_bias, "row", axis=0, tiled=True),
        lax.all_gather(up_weight, "row", axis=0, tiled=True),
        lax.all_gather(up_bias, "row", axis=0, tiled=True),
        lax.all_gather(down_weight, "row", axis=0, tiled=True),
        lax.all_gather(down_bias, "row", axis=0, tiled=True),
    )
    cotangent_full = cotangent.astype(jnp.float32)
    down_grad = (gate_two * cotangent_full).astype(jnp.bfloat16).reshape(token_count, width)
    gate_two_grad = jnp.sum(cotangent_full * downward, axis=1)
    down_weight_part = jnp.einsum(
        "tf,td->fd", activated, down_grad, preferred_element_type=jnp.float32
    )
    down_bias_part = jnp.sum(down_grad.astype(jnp.float32), axis=0)
    (up_grad_full,) = gelu_back(
        jnp.einsum("td,fd->tf", down_grad, down_w, preferred_element_type=jnp.float32)
    )
    up_grad = up_grad_full.astype(jnp.bfloat16)
    up_weight_part = jnp.einsum(
        "td,tf->df", hidden_two, up_grad, preferred_element_type=jnp.float32
    )
    up_bias_part = jnp.sum(up_grad.astype(jnp.float32), axis=0)
    hidden_two_grad = jnp.einsum(
        "tf,df->td", up_grad, up_w, preferred_element_type=jnp.float32
    ).reshape(frame_count, row_count, width)
    middle_norm_grad, shift_two_grad, scale_two_grad = second_back(hidden_two_grad)
    middle_grad = cotangent_full + middle_norm_grad
    branch_grad = (gate_one * middle_grad).astype(jnp.bfloat16).reshape(token_count, width)
    gate_one_grad = jnp.sum(middle_grad * branch, axis=1)
    out_weight_part = jnp.einsum(
        "td,te->de", attended_local, branch_grad, preferred_element_type=jnp.float32
    )
    out_bias_part = jnp.sum(branch_grad.astype(jnp.float32), axis=0)
    attended_grad = jnp.einsum(
        "te,de->td", branch_grad, out_w, preferred_element_type=jnp.float32
    ).astype(jnp.bfloat16)

    def attend_back(block_index, loop_state):
        query_total, key_total, value_total = loop_state
        first_frame, key_start, query_block, key_block, value_block, allowed = block_inputs(
            block_index
        )
        block_lse = log_totals[block_index]

        def one_group(group_index):
            query_part, key_part, value_part = head_slices(
                query_block, key_block, value_block, group_index
            )
            grad_part = lax.dynamic_slice_in_dim(
                attended_grad, group_index * columns, columns, 1
            ).reshape(block_rows, group_size, HD)
            scores = masked_scores(query_part, key_part, allowed)
            softmax_again = jnp.exp(scores - block_lse[group_index][:, :, None])
            soft_grad = jnp.einsum(
                "qhd,khd->hqk", grad_part, value_part, preferred_element_type=jnp.float32
            )
            weighted_sum = jnp.sum(softmax_again * soft_grad, axis=-1, keepdims=True)
            score_grad = (softmax_again * (soft_grad - weighted_sum)).astype(jnp.bfloat16)
            query_grad = (
                jnp.einsum("hqk,khd->qhd", score_grad, key_part, preferred_element_type=jnp.float32)
                * scale_factor
            )
            key_grad = (
                jnp.einsum(
                    "hqk,qhd->khd", score_grad, query_part, preferred_element_type=jnp.float32
                )
                * scale_factor
            )
            value_grad = jnp.einsum(
                "hqk,qhd->khd",
                softmax_again.astype(jnp.bfloat16),
                grad_part,
                preferred_element_type=jnp.float32,
            )
            return (
                query_grad.reshape(block_rows, columns),
                key_grad.reshape(key_rows, columns),
                value_grad.reshape(key_rows, columns),
            )

        query_parts, key_parts, value_parts = lax.map(one_group, jnp.arange(group_total))
        query_piece = jnp.transpose(query_parts, (1, 0, 2)).reshape(block_rows, span)
        key_piece = jnp.transpose(key_parts, (1, 0, 2)).reshape(key_frames, patch_count, span)
        value_piece = jnp.transpose(value_parts, (1, 0, 2)).reshape(key_frames, patch_count, span)
        query_total = query_piece
        key_current = lax.dynamic_slice_in_dim(key_total, key_start, key_frames, 0)
        key_total = lax.dynamic_update_slice_in_dim(
            key_total, key_current + key_piece, key_start, 0
        )
        value_current = lax.dynamic_slice_in_dim(value_total, key_start, key_frames, 0)
        value_total = lax.dynamic_update_slice_in_dim(
            value_total, value_current + value_piece, key_start, 0
        )
        return (query_total, key_total, value_total)

    query_start = jnp.zeros((frame_count * row_count, span), jnp.float32)
    key_zero = jnp.zeros((2 * frame_count, patch_count, span), jnp.float32)
    value_zero = jnp.zeros((2 * frame_count, patch_count, span), jnp.float32)
    query_total, key_total, value_total = lax.fori_loop(
        0, block_total, attend_back, (query_start, key_zero, value_zero)
    )
    key_sums, value_sums = (
        lax.psum_scatter(
            key_total.astype(jnp.bfloat16), "row", scatter_dimension=1, tiled=True
        ).astype(jnp.float32),
        lax.psum_scatter(
            value_total.astype(jnp.bfloat16), "row", scatter_dimension=1, tiled=True
        ).astype(jnp.float32),
    )
    returned_keys, returned_values = (
        shifted(key_sums[:frame_count].astype(jnp.bfloat16), "seq", -1).astype(jnp.float32),
        shifted(value_sums[:frame_count].astype(jnp.bfloat16), "seq", -1).astype(jnp.float32),
    )
    key_own = (key_sums[frame_count:] + returned_keys).reshape(token_count, width)
    value_own = (value_sums[frame_count:] + returned_values).reshape(token_count, width)
    query_pre = rotate(query_total.reshape(token_count, H, HD), cosine, -sine).reshape(
        token_count, width
    )
    key_pre = rotate(key_own.reshape(token_count, H, HD), cosine, -sine).reshape(token_count, width)
    projected_grad = jnp.concatenate([query_pre, key_pre, value_own], axis=1).astype(jnp.bfloat16)
    qkv_weight_part = jnp.einsum(
        "td,te->de", hidden_one, projected_grad, preferred_element_type=jnp.float32
    )
    qkv_bias_part = jnp.sum(projected_grad.astype(jnp.float32), axis=0)
    hidden_one_grad = jnp.einsum(
        "te,de->td", projected_grad, qkv_w, preferred_element_type=jnp.float32
    ).reshape(frame_count, row_count, width)
    input_norm_grad, shift_one_grad, scale_one_grad = first_back(hidden_one_grad)
    input_grad = middle_grad + input_norm_grad
    modulation_grad = jnp.concatenate(
        [
            shift_one_grad[:, 0],
            scale_one_grad[:, 0],
            gate_one_grad,
            shift_two_grad[:, 0],
            scale_two_grad[:, 0],
            gate_two_grad,
        ],
        axis=1,
    )
    ada_weight_part = jnp.einsum(
        "fd,fe->de",
        silu_embed.astype(jnp.float32),
        modulation_grad,
        precision=lax.Precision.HIGHEST,
    )
    ada_bias_part = jnp.sum(modulation_grad, axis=0)
    silu_grad_part = jnp.einsum(
        "fe,de->fd", modulation_grad, ada_w.astype(jnp.float32), precision=lax.Precision.HIGHEST
    )
    silu_grad = lax.psum(silu_grad_part.astype(jnp.bfloat16), "row").astype(jnp.float32)
    (embed_grad,) = silu_back(silu_grad)
    owned = (
        lax.psum_scatter(
            ada_weight_part.astype(jnp.bfloat16), "row", scatter_dimension=0, tiled=True
        ).astype(jnp.float32),
        lax.psum_scatter(
            ada_bias_part.astype(jnp.bfloat16), "row", scatter_dimension=0, tiled=True
        ).astype(jnp.float32),
        lax.psum_scatter(
            qkv_weight_part.astype(jnp.bfloat16), "row", scatter_dimension=0, tiled=True
        ).astype(jnp.float32),
        lax.psum_scatter(
            qkv_bias_part.astype(jnp.bfloat16), "row", scatter_dimension=0, tiled=True
        ).astype(jnp.float32),
        lax.psum_scatter(
            out_weight_part.astype(jnp.bfloat16), "row", scatter_dimension=0, tiled=True
        ).astype(jnp.float32),
        lax.psum_scatter(
            out_bias_part.astype(jnp.bfloat16), "row", scatter_dimension=0, tiled=True
        ).astype(jnp.float32),
        lax.psum_scatter(
            up_weight_part.astype(jnp.bfloat16), "row", scatter_dimension=0, tiled=True
        ).astype(jnp.float32),
        lax.psum_scatter(
            up_bias_part.astype(jnp.bfloat16), "row", scatter_dimension=0, tiled=True
        ).astype(jnp.float32),
        lax.psum_scatter(
            down_weight_part.astype(jnp.bfloat16), "row", scatter_dimension=0, tiled=True
        ).astype(jnp.float32),
        lax.psum_scatter(
            down_bias_part.astype(jnp.bfloat16), "row", scatter_dimension=0, tiled=True
        ).astype(jnp.float32),
    )
    totals = (
        lax.psum(owned[0].astype(jnp.bfloat16), "seq").astype(jnp.float32),
        lax.psum(owned[1].astype(jnp.bfloat16), "seq").astype(jnp.float32),
        lax.psum(owned[2].astype(jnp.bfloat16), "seq").astype(jnp.float32),
        lax.psum(owned[3].astype(jnp.bfloat16), "seq").astype(jnp.float32),
        lax.psum(owned[4].astype(jnp.bfloat16), "seq").astype(jnp.float32),
        lax.psum(owned[5].astype(jnp.bfloat16), "seq").astype(jnp.float32),
        lax.psum(owned[6].astype(jnp.bfloat16), "seq").astype(jnp.float32),
        lax.psum(owned[7].astype(jnp.bfloat16), "seq").astype(jnp.float32),
        lax.psum(owned[8].astype(jnp.bfloat16), "seq").astype(jnp.float32),
        lax.psum(owned[9].astype(jnp.bfloat16), "seq").astype(jnp.float32),
    )
    return (
        layer_output,
        input_grad,
        embed_grad,
        totals[0],
        totals[1],
        totals[2],
        totals[3],
        totals[4],
        totals[5],
        totals[6],
        totals[7],
        totals[8],
        totals[9],
    )


def solution(mesh):
    in_specs = (
        P("seq", "row", None),
        P("seq", None),
        P("seq"),
        P("seq", "row", None),
        P("row", None),
        P("row"),
        P("row", None),
        P("row"),
        P("row", None),
        P("row"),
        P("row", None),
        P("row"),
        P("row", None),
        P("row"),
    )
    out_specs = (
        P("seq", "row", None),
        P("seq", "row", None),
        P("seq", None),
        P("row", None),
        P("row"),
        P("row", None),
        P("row"),
        P("row", None),
        P("row"),
        P("row", None),
        P("row"),
        P("row", None),
        P("row"),
    )
    return jax.shard_map(
        per_device, mesh=mesh, in_specs=in_specs, out_specs=out_specs, check_vma=False
    )
```

profile of v0, /device:TPU:6, one launch (start us, length us, event | category | flops | bytes accessed | tf_op | source)
XLA Modules:
  0.0 2132.7 jit_solution(12973560310825122768)
XLA Ops:
  19.9 106.7 %all-gather.12.cloned.1.call-done = bf16[1024,6144]{1,0:T(8,128)(2,1)} async-done(((bf16[256,6144]{1,0:T(8,128)(2,1)}), bf16[1024,6144]{1,0:T(8,128)(2,1)}) %all-gather.12.cloned.1.call-update) | async-done | bytes 12582928 | tf_op jit(solution)/shard_map/all_gather | solution.py:118
  134.7 58.6 %all-gather.14.cloned.1.call-done = bf16[1024,3072]{1,0:T(8,128)(2,1)} async-done(((bf16[256,3072]{1,0:T(8,128)(2,1)}), bf16[1024,3072]{1,0:T(8,128)(2,1)}) %all-gather.14.cloned.1.call-update) | async-done | bytes 6291472 | tf_op jit(solution)/shard_map/all_gather | solution.py:120
  205.1 30.1 %collective-permute-done = bf16[8,64,1024]{2,1,0:T(8,128)(2,1)S(1)} collective-permute-done((bf16[8,64,1024]{2,1,0:T(8,128)(2,1)S(1)}, bf16[8,64,1024]{2,1,0:T(8,128)(2,1)S(1)}, u32[]{:S(2)}, u32[]{:S(2)}) %collective-permute-start) | collective-permute-done | bytes 1048608 | tf_op jit(solution)/shard_map/ppermute | solution.py:17
  256.1 53.9 %collective-permute-done.1 = bf16[8,64,1024]{2,1,0:T(8,128)(2,1)S(1)} collective-permute-done((bf16[8,64,1024]{2,1,0:T(8,128)(2,1)S(1)}, bf16[8,64,1024]{2,1,0:T(8,128)(2,1)S(1)}, u32[]{:S(2)}, u32[]{:S(2)}) %collective-permute-start.1) | collective-permute-done | bytes 1048608 | tf_op jit(solution)/shard_map/ppermute | solution.py:17
  342.6 11.2 copy.87
  353.8 63.7 %all-gather.18.cloned.1.call-done = bf16[16,256,1024]{2,1,0:T(8,128)(2,1)} async-done(((bf16[16,64,1024]{2,1,0:T(8,128)(2,1)}), bf16[16,256,1024]{2,1,0:T(8,128)(2,1)}) %all-gather.18.cloned.1.call-update) | async-done | bytes 8388624 | tf_op jit(solution)/shard_map/all_gather | solution.py:167
  435.8 196.1 %while.51 = (s32[]{:T(128)}, bf16[8,512,128]{1,2,0:T(8,128)(2,1)}, f32[8,2,512]{2,1,0:T(2,128)}, s32[8]{0:T(128)S(1)}, bf16[3840,1024]{0,1:T(8,128)(2,1)}, /*ind...) while((s32[]{:T(128)}, bf16[8,512,128]{1,2,0:T(8,128)(2,1)}, ...), condition=%wide.region_5.6_spmd.clone.clone, body=%wide.region_2.5_spmd.clone.sunk.clone | while | flops 1053817856 | bytes 73572032 | solution.py:246
  647.7 24.4 %fusion.55 = (bf16[4096]{0:T(1024)(128)(2,1)}, bf16[512,4096]{1,0:T(8,128)(2,1)}) fusion(f32[512,4096]{1,0:T(8,128)} %fusion.63, f32[4096]{0:T(1024)S(1)} %copy-done.57, bf16[512,1024]{1,0:T(8,128)(2,1)} %bitcast.246, bf16[4096,1024]{1,0:T(8,128)(2,1)} %all-gather.24.cloned.1.call-done), kind=kOutput, calls=%fused_computation.159 | convolution fusion | flops 4341100544 | bytes 22044672 | tf_op jit(solution)/shard_map/td,fd->tf/dot_general | solution.py:287
  697.4 414.1 %while.52 = (s32[]{:T(128)}, f32[8,512,128]{1,2,0:T(8,128)}, bf16[8,3840,128]{1,2,0:T(8,128)(2,1)}, bf16[8,3840,128]{1,2,0:T(8,128)(2,1)}, s32[8]{0:T(128)S(1)},...) while((s32[]{:T(128)}, f32[8,512,128]{1,2,0:T(8,128)}, ...), condition=%wide.region_12.13_spmd.clone.clone, body=%wide.region_10.12_spmd.clone.sunk.clone | while | flops 2553019392 | bytes 153579696 | solution.py:352
  718.1 11.1 multiply_reduce_fusion.6
  769.8 11.1 multiply_reduce_fusion.6
  821.5 11.1 multiply_reduce_fusion.6
  976.7 11.1 multiply_reduce_fusion.6
  1028.4 11.1 multiply_reduce_fusion.6
  1080.1 11.1 multiply_reduce_fusion.6
  1111.5 13.8 reshape.567
  1125.3 12.1 copy.99
  1145.3 14.0 reshape.566
  1159.2 12.2 copy.98
  1183.6 13.4 convolution_convert_fusion.1
  1207.2 19.5 reduce-scatter.10.cloned.1.call-done
  1235.9 92.8 %reduce-scatter.8.cloned.1.call-done = bf16[16,64,1024]{2,1,0:T(8,128)(2,1)} async-done(((bf16[16,256,1024]{2,1,0:T(8,128)(2,1)}), bf16[16,64,1024]{2,1,0:T(8,128)(2,1)}) %reduce-scatter.8.cloned.1.call-update) | async-done | bytes 2097168 | tf_op jit(solution)/shard_map/reduce_scatter | solution.py:374
  1335.2 37.7 %collective-permute-done.2 = bf16[8,64,1024]{2,1,0:T(8,128)(2,1)} collective-permute-done((bf16[8,64,1024]{2,1,0:T(8,128)(2,1)}, bf16[8,64,1024]{2,1,0:T(8,128)(2,1)}, u32[]{:S(2)}, u32[]{:S(2)}) %collective-permute-start.2) | collective-permute-done | bytes 1048608 | tf_op jit(solution)/shard_map/ppermute | solution.py:17
  1416.7 12.4 convolution_convert_fusion
  1429.6 20.3 reduce-scatter.20.cloned.1.call-done
  1449.9 82.5 %reduce-scatter.18.cloned.1.call-done = bf16[256,4096]{1,0:T(8,128)(2,1)} async-done(((bf16[1024,4096]{1,0:T(8,128)(2,1)}), bf16[256,4096]{1,0:T(8,128)(2,1)}) %reduce-scatter.18.cloned.1.call-update) | async-done | bytes 2097168 | tf_op jit(solution)/shard_map/reduce_scatter | solution.py:443
  1532.4 66.6 %reduce-scatter.14.cloned.1.call-done = bf16[256,3072]{1,0:T(8,128)(2,1)} async-done(((bf16[1024,3072]{1,0:T(8,128)(2,1)}), bf16[256,3072]{1,0:T(8,128)(2,1)}) %reduce-scatter.14.cloned.1.call-update) | async-done | bytes 1572880 | tf_op jit(solution)/shard_map/reduce_scatter | solution.py:431
  1598.9 116.5 %reduce-scatter.12.cloned.1.call-done = bf16[256,6144]{1,0:T(8,128)(2,1)} async-done(((bf16[1024,6144]{1,0:T(8,128)(2,1)}), bf16[256,6144]{1,0:T(8,128)(2,1)}) %reduce-scatter.12.cloned.1.call-update) | async-done | bytes 3145744 | tf_op jit(solution)/shard_map/reduce_scatter | solution.py:425
  1720.4 12.7 convolution_convert_fusion.6
  1733.1 12.3 all-reduce.9
  1745.7 97.8 %all-reduce.7 = (bf16[1536]{0:T(1024)(128)(2,1)S(1)}, bf16[768]{0:T(1024)(128)(2,1)S(1)}, bf16[256]{0:T(256)(128)(2,1)S(1)}, bf16[1024]{0:T(1024)(128)(2,1)S(1)}, bf16[256]{0:T(256)(128)(2,1)S(1)}) all-reduce(bf16[1536]{0:T(1024)(128)(2,1)S(1)} %dynamic-slice.2, ...), channel_id=1, replica_groups=mesh['seq'=32,'row'=4] {'seq'}, use_global_device_ids=true, to_apply=%region_28.29 | all-reduce | flops 3840 | bytes 15360 | tf_op jit(solution)/shard_map/psum | solution.py:458
  1847.1 263.8 %all-reduce.12.cloned.1.call-done = (bf16[256,6144]{1,0:T(8,128)(2,1)}, bf16[256,3072]{1,0:T(8,128)(2,1)}, bf16[256,1024]{1,0:T(8,128)(2,1)}, bf16[256,4096]{1,0:T(8,128)(2,1)}, bf16[1024,1024]{1,0:T(8,128)(2,1)}) async-done(((bf16[256,6144]{1,0:T(8,128)(2,1)}, bf16[256,3072]{1,0:T(8,128)(2,1)}, bf16[256,1024]{1,0:T(8,128)(2,1)}, bf16[256,4096]{1,0:T(8,128)(2,1)}, bf16[1024,1024]{1,0:T(8,128)(2,1)}), ...) | async-done | bytes 9437200 | tf_op jit(solution)/shard_map/psum | solution.py:457
  (622 shorter events, 771.4 us)
Async XLA Ops:
  7.2 119.4 %copy-start.43 = (bf16[8,1024]{1,0:T(8,128)(2,1)S(1)}, bf16[8,1024]{1,0:T(8,128)(2,1)}, u32[]{:S(2)}) copy-start(bf16[8,1024]{1,0:T(8,128)(2,1)} %param.19) | copy-start | bytes 49156
  7.2 119.4 %all-gather.12.cloned.1.call-start = ((), (), s32[]{:S(2)}) async-start(), calls=%async_computation.7 | async-start | bytes 15728640 | tf_op jit(solution)/shard_map/all_gather | solution.py:118
  8.0 185.4 %all-gather.14.cloned.1.call-start = ((), (), s32[]{:S(2)}) async-start(), calls=%async_computation.8 | async-start | bytes 7864320 | tf_op jit(solution)/shard_map/all_gather | solution.py:120
  8.7 326.3 %all-gather.16.cloned.1.call-start = ((), (), s32[]{:S(2)}) async-start(), calls=%async_computation.9 | async-start | bytes 10485760 | tf_op jit(solution)/shard_map/all_gather | solution.py:168
  19.4 114.1 %copy-start.45 = (f32[8,64]{1,0:T(8,128)}, f32[8,64]{1,0:T(8,128)S(1)}, u32[]{:S(2)}) copy-start(f32[8,64]{1,0:T(8,128)S(1)} %broadcast_multiply_fusion.1) | copy-start | bytes 6148
  19.9 106.8 %copy-start.55 = (f32[8,64]{1,0:T(8,128)}, f32[8,64]{1,0:T(8,128)S(1)}, u32[]{:S(2)}) copy-start(f32[8,64]{1,0:T(8,128)S(1)} %fusion.27) | copy-start | bytes 6148
  19.9 113.7 %copy-start.51 = (f32[8,64]{1,0:T(8,128)}, f32[8,64]{1,0:T(8,128)S(1)}, u32[]{:S(2)}) copy-start(f32[8,64]{1,0:T(8,128)S(1)} %fusion.43) | copy-start | bytes 6148
  133.6 198.5 %copy-start.40 = (f32[8,1024]{1,0:T(8,128)}, f32[8,1024]{1,0:T(8,128)S(1)}, u32[]{:S(2)}) copy-start(f32[8,1024]{1,0:T(8,128)S(1)} %get-tuple-element.403) | copy-start | bytes 98308
  134.7 64.1 %copy-start.30 = (bf16[8,64,1024]{2,1,0:T(8,128)(2,1)}, bf16[8,64,1024]{2,1,0:T(8,128)(2,1)S(1)}, u32[]{:S(2)}) copy-start(bf16[8,64,1024]{2,1,0:T(8,128)(2,1)S(1)} %fusion.25) | copy-start | bytes 3145732
  201.6 35.2 %copy-start.66 = (s32[8]{0:T(128)S(1)}, s32[8]{0:T(128)}, u32[]{:S(2)}) copy-start(s32[8]{0:T(128)} %param.20) | copy-start | bytes 100
  201.7 33.5 %collective-permute-start = (bf16[8,64,1024]{2,1,0:T(8,128)(2,1)S(1)}, bf16[8,64,1024]{2,1,0:T(8,128)(2,1)S(1)}, u32[]{:S(2)}, u32[]{:S(2)}) collective-permute-start(bf16[8,64,1024]{2,1,0:T(8,128)(2,1)S(1)} %bitcast.237), channel_id=1, source_target_pairs={{0,4},{4,8},{8,12},{12,16},{16,20},{20,24},{24,28},{28,32},{32,36}... | collective-permute-start | bytes 3145736 | tf_op jit(solution)/shard_map/ppermute | solution.py:17
  236.7 180.7 %all-gather.18.cloned.1.call-start = ((), (), s32[]{:S(2)}) async-start(), calls=%async_computation.10 | async-start | bytes 10485760 | tf_op jit(solution)/shard_map/all_gather | solution.py:167
  254.1 55.8 %collective-permute-start.1 = (bf16[8,64,1024]{2,1,0:T(8,128)(2,1)S(1)}, bf16[8,64,1024]{2,1,0:T(8,128)(2,1)S(1)}, u32[]{:S(2)}, u32[]{:S(2)}) collective-permute-start(bf16[8,64,1024]{2,1,0:T(8,128)(2,1)S(1)} %copy.97), channel_id=1, source_target_pairs={{0,4},{4,8},{8,12},{12,16},{16,20},{20,24},{24,28},{28,32},{32,36}... | collective-permute-start | bytes 3145736 | tf_op jit(solution)/shard_map/ppermute | solution.py:17
  311.4 20.6 copy-start.9
  311.5 22.5 %copy-start.22 = (bf16[512,16,32]{0,2,1:T(8,128)(2,1)S(1)}, bf16[512,16,32]{0,2,1:T(8,128)(2,1)}, u32[]{:S(2)}) copy-start(bf16[512,16,32]{0,2,1:T(8,128)(2,1)} %get-tuple-element.411) | copy-start | bytes 1572868
  311.5 22.5 %copy-start.23 = (bf16[512,16,32]{0,2,1:T(8,128)(2,1)S(1)}, bf16[512,16,32]{0,2,1:T(8,128)(2,1)}, u32[]{:S(2)}) copy-start(bf16[512,16,32]{0,2,1:T(8,128)(2,1)} %get-tuple-element.412) | copy-start | bytes 1572868
  311.5 320.4 %all-gather.20.cloned.1.call-start = ((), (), s32[]{:S(2)}) async-start(), calls=%async_computation.11 | async-start | bytes 2621440 | tf_op jit(solution)/shard_map/all_gather | solution.py:122
  312.1 325.2 %all-gather.22.cloned.1.call-start = ((), (), s32[]{:S(2)}) async-start(), calls=%async_computation.12 | async-start | bytes 10485760 | tf_op jit(solution)/shard_map/all_gather | solution.py:124
  312.7 335.1 %all-gather.24.cloned.1.call-start = ((), (), s32[]{:S(2)}) async-start(), calls=%async_computation.13 | async-start | bytes 10485760 | tf_op jit(solution)/shard_map/all_gather | solution.py:126
  313.4 913.4 %reduce-scatter.10.cloned.1.call-start = ((), (), s32[]{:S(2)}) async-start(), calls=%async_computation.15 | async-start | bytes 10485760 | tf_op jit(solution)/shard_map/reduce_scatter | solution.py:377
  435.8 196.1 %copy-start.50 = (f32[4,1,256]{2,1,0:T(1,128)S(1)}, f32[4,1,256]{2,1,0:T(1,128)}, u32[]{:S(2)}) copy-start(f32[4,1,256]{2,1,0:T(1,128)} %convert_element_type.274) | copy-start | bytes 12292
  647.7 24.4 %copy-start.68 = (bf16[1024,4096]{1,0:T(8,128)(2,1)S(1)}, bf16[1024,4096]{1,0:T(8,128)(2,1)}, u32[]{:S(2)}) copy-start(bf16[1024,4096]{1,0:T(8,128)(2,1)} %all-gather.22.cloned.1.call-done) | copy-start | bytes 25165828
  1145.2 183.4 %reduce-scatter.8.cloned.1.call-start = ((), (), s32[]{:S(2)}) async-start(), calls=%async_computation.14 | async-start | bytes 10485760 | tf_op jit(solution)/shard_map/reduce_scatter | solution.py:374
  1179.4 250.2 %reduce-scatter.16.cloned.1.call-start = ((), (), s32[]{:S(2)}) async-start(), calls=%async_computation.18 | async-start | bytes 2621440 | tf_op jit(solution)/shard_map/reduce_scatter | solution.py:437
  1183.6 266.3 %reduce-scatter.20.cloned.1.call-start = ((), (), s32[]{:S(2)}) async-start(), calls=%async_computation.20 | async-start | bytes 10485760 | tf_op jit(solution)/shard_map/reduce_scatter | solution.py:449
  1197.0 335.3 %reduce-scatter.18.cloned.1.call-start = ((), (), s32[]{:S(2)}) async-start(), calls=%async_computation.19 | async-start | bytes 10485760 | tf_op jit(solution)/shard_map/reduce_scatter | solution.py:443
  1207.2 391.7 %reduce-scatter.14.cloned.1.call-start = ((), (), s32[]{:S(2)}) async-start(), calls=%async_computation.17 | async-start | bytes 7864320 | tf_op jit(solution)/shard_map/reduce_scatter | solution.py:431
  1226.8 106.1 %copy-start.20 = (bf16[16,64,1024]{2,1,0:T(8,128)(2,1)S(1)}, bf16[16,64,1024]{2,1,0:T(8,128)(2,1)}, u32[]{:S(2)}) copy-start(bf16[16,64,1024]{2,1,0:T(8,128)(2,1)} %reduce-scatter.10.cloned.1.call-done) | copy-start | bytes 6291460
  1228.2 104.6 %collective-permute-start.3 = (bf16[8,64,1024]{2,1,0:T(8,128)(2,1)S(1)}, bf16[8,64,1024]{2,1,0:T(8,128)(2,1)}, u32[]{:S(2)}, u32[]{:S(2)}) collective-permute-start(bf16[8,64,1024]{2,1,0:T(8,128)(2,1)S(1)} %slice.117), channel_id=1, source_target_pairs={{4,0},{8,4},{12,8},{16,12},{20,16},{24,20},{28,24},{32,28},{36,32}... | collective-permute-start | bytes 3145736 | tf_op jit(solution)/shard_map/ppermute | solution.py:17
  1330.9 42.0 %collective-permute-start.2 = (bf16[8,64,1024]{2,1,0:T(8,128)(2,1)}, bf16[8,64,1024]{2,1,0:T(8,128)(2,1)}, u32[]{:S(2)}, u32[]{:S(2)}) collective-permute-start(bf16[8,64,1024]{2,1,0:T(8,128)(2,1)} %slice.113), channel_id=1, source_target_pairs={{4,0},{8,4},{12,8},{16,12},{20,16},{24,20},{28,24},{32,28},{36,32}... | collective-permute-start | bytes 3145736 | tf_op jit(solution)/shard_map/ppermute | solution.py:17
  1403.8 311.7 %reduce-scatter.12.cloned.1.call-start = ((), (), s32[]{:S(2)}) async-start(), calls=%async_computation.16 | async-start | bytes 15728640 | tf_op jit(solution)/shard_map/reduce_scatter | solution.py:425
  1429.2 681.6 %all-reduce.12.cloned.1.call-start = ((), (), s32[]{:S(2)}) async-start(), calls=%async_computation.21 | async-start | bytes 18874368 | tf_op jit(solution)/shard_map/psum | solution.py:457
  (110 other events, 637.7 us)
Sparse Core Ops, SparseCore 0:
  9.7 116.8 all-gather.11
  128.3 65.0 all-gather.13
  236.8 76.2 all-gather.15
  315.2 102.2 all-gather.17
  419.0 30.8 all-gather.19
  451.4 81.3 all-gather.21
  534.4 82.2 all-gather.23
  1145.3 81.3 reduce-scatter.9
  1229.2 99.3 reduce-scatter.7
  1330.9 41.3 reduce-scatter.15
  1374.9 74.9 reduce-scatter.19
  1452.3 79.9 reduce-scatter.17
  1535.5 63.4 reduce-scatter.13
  1601.4 113.9 reduce-scatter.11
  1718.4 392.3 all-reduce.11
where the time goes:
time: 2150 us; the launch traced here: 2130 us
  waiting for transfers between devices  1020 us (47%)
  matrix products  416 us (19%)
  local copies, waits for them, and re-layouts  354 us (16%)
  other arithmetic  150 us (7%)
  blocking collectives  136 us (6%)
  loops' own time  27.5 us (1%)
    psum x1, waiting for transfers between devices, per_device(): lax.psum(owned[0].astype(jnp.bfloat16), 'seq').astype(jnp.float32)  264 us
    dot_general x16, matrix products, masked_scores(): jnp.einsum('qhd,khd->hqk', query_part, key_part, preferred_element_type=j...  132 us
    ppermute x4, waiting for transfers between devices, shifted(): lax.ppermute(value, axis, [(source, source + steps) for source in range(l...  122 us
    reduce_scatter x1, waiting for transfers between devices, per_device(): lax.psum_scatter(ada_weight_part.astype(jnp.bfloat16), 'row', scatter_dim...  117 us
    all_gather x1, waiting for transfers between devices, per_device(): lax.all_gather(ada_weight, 'row', axis=0, tiled=True)  107 us
    psum x1, blocking collectives, per_device(): lax.psum(owned[1].astype(jnp.bfloat16), 'seq').astype(jnp.float32)  97.8 us
    reduce_scatter x1, waiting for transfers between devices, per_device(): lax.psum_scatter(key_total.astype(jnp.bfloat16), 'row', scatter_dimension...  92.8 us
    reduce_scatter x1, waiting for transfers between devices, per_device(): lax.psum_scatter(up_weight_part.astype(jnp.bfloat16), 'row', scatter_dime...  82.5 us
  transfers between devices with their start and end apart: 19, of which 13 were waited for; matrix products, arithmetic and copies ran while one was open for 19% of the time, Pallas kernels for 0%

commit v1 on v0

v1 whole, which is shorter than its diff:
```python
import math

import jax
import jax.numpy as jnp
from jax import lax
from jax.experimental import pallas as pl
from jax.experimental.pallas import tpu as pltpu
from jax.sharding import Mesh, PartitionSpec as P

F32 = jnp.float32
BF16 = jnp.bfloat16
HD = 64
GRID = 16
FPD = 8
PR = 64
D = 1024
FF = 4096
HC = 256
TOK = 256
PREV = 7
AXES = ("xh", "z", "y", "xl", "c")
CORE, DIRECT, OTHER, FAR = 1, 2, 66, 64
MB = 1024 * 1024


def swap(value, mask):
    return lax.ppermute(value, AXES, [(i, i ^ mask) for i in range(128)])


def shift(value, steps):
    first, last = max(0, -4 * steps), min(128, 128 - 4 * steps)
    return lax.ppermute(value, AXES, [(i, i + 4 * steps) for i in range(first, last)])


def after(value, *others):
    return lax.optimization_barrier((value,) + others)[0]


def nt(left, right):
    return lax.dot_general(left, right, (((1,), (1,)), ((), ())), preferred_element_type=F32)


def tn(left, right):
    return lax.dot_general(left, right, (((0,), (0,)), ((), ())), preferred_element_type=F32)


def nn(left, right):
    return jnp.dot(left, right, preferred_element_type=F32)


def norm(values):
    center = values - jnp.mean(values, axis=-1, keepdims=True)
    spread = jnp.mean(center * center, axis=-1, keepdims=True)
    rate = lax.rsqrt(spread + 1e-06)
    return center * rate, rate


def norm_back(normal, rate, grad):
    mean_grad = jnp.mean(grad, axis=-1, keepdims=True)
    mean_both = jnp.mean(grad * normal, axis=-1, keepdims=True)
    return rate * (grad - mean_grad - normal * mean_both)


def turn(values, cosine, sine):
    lanes = lax.broadcasted_iota(jnp.int32, values.shape, 1)
    other = jnp.where(
        lanes % HD < HD // 2, pltpu.roll(values, HC - HD // 2, 1), pltpu.roll(values, HD // 2, 1)
    )
    return values * cosine + other * sine


def params(mib):
    return pltpu.CompilerParams(
        dimension_semantics=("arbitrary",), vmem_limit_bytes=mib * MB
    )


def cost(flops, moved, exps=0):
    return pl.CostEstimate(flops=int(flops), bytes_accessed=int(moved), transcendentals=int(exps))


def whole(shape):
    return pl.BlockSpec(shape, lambda i, *_: (0,) * len(shape))


def columns(row, j):
    return pl.ds(pl.multiple_of((row ^ j) * HC, HC), HC)


def project_kernel(with_query, row_ref, x0, x1, x2, x3, sh, sc, w0, w1, w2, w3, b, cp, sp, cf, sf, *outs):
    row = row_ref[0]
    if with_query:
        h_ref, q_ref, k_ref, v_ref = outs
        first = 0
    else:
        k_ref, v_ref, h_ref = outs
        first = HC
    x = jnp.concatenate([r[0] for r in (x0, x1, x2, x3)], axis=0).astype(F32)
    normal, _ = norm(x)
    hidden = (normal * (1.0 + sc[0]) + sh[0]).astype(BF16)
    where = (0,) if with_query else ()
    h_ref[where + (slice(None), slice(None))] = hidden
    total = b[:, first:]
    for j, w in enumerate((w0, w1, w2, w3)):
        total = total + nn(h_ref[where + (slice(None), columns(row, j))], w[:, first:])
    cosine = cp[...] + cf[0]
    sine = sp[...] + sf[0]
    if with_query:
        q_ref[0] = (turn(total[:, :HC], cosine, sine).astype(BF16).astype(F32) * 0.125).astype(BF16)
        total = total[:, HC:]
    k_ref[0] = turn(total[:, :HC], cosine, sine).astype(BF16)
    v_ref[0] = total[:, HC:].astype(BF16)


def project(with_query, row, xs, mod, weights, bias, tables):
    cp, sp, cf, sf = tables
    frames = xs[0].shape[0]
    segment = 0 if with_query else 6
    base = 0 if with_query else FPD - frames
    x_spec = pl.BlockSpec((1, PR, D), lambda f, *_: (f, 0, 0))
    mod_spec = lambda s: pl.BlockSpec((1, 1, D), lambda f, *_: (f + base, 0, s))
    frame_table = pl.BlockSpec((1, 1, HC), lambda f, *_: (f, 0, 0))
    out_spec = pl.BlockSpec((1, TOK, HC), lambda f, *_: (f, 0, 0))
    out = jax.ShapeDtypeStruct((frames, TOK, HC), BF16)
    if with_query:
        out_specs = [pl.BlockSpec((1, TOK, D), lambda f, *_: (f, 0, 0)), out_spec, out_spec, out_spec]
        out_shape = [jax.ShapeDtypeStruct((frames, TOK, D), BF16), out, out, out]
        scratch = []
    else:
        out_specs = [out_spec, out_spec]
        out_shape = [out, out]
        scratch = [pltpu.VMEM((TOK, D), BF16)]
    return pl.pallas_call(
        lambda *refs: project_kernel(with_query, *refs),
        out_shape=out_shape,
        grid_spec=pltpu.PrefetchScalarGridSpec(
            num_scalar_prefetch=1,
            grid=(frames,),
            in_specs=[x_spec] * 4
            + [mod_spec(segment), mod_spec(segment + 1)]
            + [whole((HC, 3 * HC))] * 4
            + [whole((1, 3 * HC)), whole((TOK, HC)), whole((TOK, HC)), frame_table, frame_table],
            out_specs=out_specs,
            scratch_shapes=scratch,
        ),
        compiler_params=params(32),
        cost_estimate=cost(2 * frames * TOK * D * 3 * HC, frames * TOK * D * 4 + 4 * MB),
        name="project_own" if with_query else "project_prev",
    )(row, *xs, mod, mod, *weights, bias, cp, sp, cf, sf)


def head_lanes():
    return lax.broadcasted_iota(jnp.int32, (TOK, HC), 1) // HD


def attend_kernel(pos_ref, q, k, v, kp, vp, o0, o1, o2, o3, lse, qs, scores, acc, top, low):
    f = pl.program_id(0)
    place = pos_ref[f]
    lanes = head_lanes()
    query = q[0]
    for h in range(4):
        qs[pl.ds(h * TOK, TOK), :] = jnp.where(lanes == h, query, jnp.zeros_like(query))
    top[...] = jnp.full_like(top, -1e30)
    low[...] = jnp.zeros_like(low)
    acc[...] = jnp.zeros_like(acc)
    before = jnp.maximum(place - f, 0)
    start = jnp.maximum(f - place, 0)

    def score(keys, slot):
        for h in range(4):
            rows = pl.ds(h * TOK, TOK)
            s = nt(qs[rows, :], keys)
            scores[slot, rows, :] = s
            top[rows, :] = jnp.maximum(top[rows, :], jnp.maximum(s[:, :128], s[:, 128:]))

    def mix(values, slot):
        for h in range(4):
            rows = pl.ds(h * TOK, TOK)
            p = jnp.exp(scores[slot, rows, :] - jnp.concatenate([top[rows, :]] * 2, axis=1))
            low[rows, :] = low[rows, :] + (p[:, :128] + p[:, 128:])
            acc[rows, :] = acc[rows, :] + nn(p.astype(BF16), values)

    def run(step):
        def prev(i, _):
            at = PREV - before + i
            step(kp[at] if step is score else vp[at], i)
            return 0

        def own(g, _):
            step(k[g] if step is score else v[g], g - f + place)
            return 0

        lax.fori_loop(0, before, prev, 0)
        lax.fori_loop(start, f + 1, own, 0)

    run(score)
    for h in range(4):
        rows = pl.ds(h * TOK, TOK)
        top[rows, :] = jnp.broadcast_to(jnp.max(top[rows, :], axis=1, keepdims=True), (TOK, 128))
    run(mix)
    result = jnp.zeros((TOK, HC), F32)
    logs = jnp.zeros((TOK, 128), F32)
    narrow = lax.broadcasted_iota(jnp.int32, (TOK, 128), 1)
    for h in range(4):
        rows = pl.ds(h * TOK, TOK)
        total = jnp.sum(low[rows, :], axis=1, keepdims=True)
        result = jnp.where(lanes == h, acc[rows, :] / total, result)
        logs = jnp.where(narrow == h, top[rows, :] + jnp.log(total), logs)
    lse[0] = logs.T[:8]
    result = result.astype(BF16)
    for j, o in enumerate((o0, o1, o2, o3)):
        o[0] = result[j * PR : (j + 1) * PR]


def attend(places, q, k, v, kp, vp):
    block = pl.BlockSpec((1, TOK, HC), lambda f, *_: (f, 0, 0))
    piece = pl.BlockSpec((1, PR, HC), lambda f, *_: (f, 0, 0))
    return pl.pallas_call(
        attend_kernel,
        out_shape=[jax.ShapeDtypeStruct((FPD, PR, HC), BF16)] * 4
        + [jax.ShapeDtypeStruct((FPD, 8, TOK), F32)],
        grid_spec=pltpu.PrefetchScalarGridSpec(
            num_scalar_prefetch=1,
            grid=(FPD,),
            in_specs=[block]
            + [whole((FPD, TOK, HC))] * 2
            + [whole((PREV, TOK, HC))] * 2,
            out_specs=[piece] * 4 + [pl.BlockSpec((1, 8, TOK), lambda f, *_: (f, 0, 0))],
            scratch_shapes=[
                pltpu.VMEM((4 * TOK, HC), BF16),
                pltpu.VMEM((8, 4 * TOK, TOK), F32),
                pltpu.VMEM((4 * TOK, HC), F32),
                pltpu.VMEM((4 * TOK, 128), F32),
                pltpu.VMEM((4 * TOK, 128), F32),
            ],
        ),
        compiler_params=params(40),
        cost_estimate=cost(36 * 4 * 2 * 2 * TOK**3, 6 * MB, 36 * 4 * TOK * TOK),
        name="attend",
    )(places, q, k, v, kp, vp)


def attend_back_kernel(
    pos_ref, q, k, v, kp, vp, g0, g1, g2, g3, o0, o1, o2, o3, lse, cp, sp, cf, sf,
    dq, dk, dv, dkp, dvp,
    qs, gs, ks, pl_scr, dl_scr, ds_scr, dq_acc, dkp_acc, dvp_acc,
):
    f = pl.program_id(0)
    place = pos_ref[f]
    lanes = head_lanes()

    @pl.when(f == 0)
    def _():
        for ref in (dk, dv, dkp_acc, dvp_acc):
            ref[...] = jnp.zeros_like(ref)

    query = q[0]
    grad = jnp.concatenate([r[0] for r in (g0, g1, g2, g3)], axis=0)
    mixed = jnp.concatenate([r[0] for r in (o0, o1, o2, o3)], axis=0)
    for h in range(4):
        rows = pl.ds(h * TOK, TOK)
        qs[rows, :] = jnp.where(lanes == h, query, jnp.zeros_like(query))
        gs[rows, :] = jnp.where(lanes == h, grad, jnp.zeros_like(grad))
    both = grad.astype(F32) * mixed.astype(F32)
    pick = (
        lax.broadcasted_iota(jnp.int32, (8, HC), 1) // HD
        == lax.broadcasted_iota(jnp.int32, (8, HC), 0)
    ).astype(F32)
    delta = lax.dot_general(
        pick, both, (((1,), (1,)), ((), ())),
        preferred_element_type=F32, precision=lax.Precision.HIGHEST,
    )
    logs = lse[0]
    dq_acc[...] = jnp.zeros_like(dq_acc)

    def step(keys, values, dk_ref, dv_ref, at):
        for h in range(4):
            rows = pl.ds(h * TOK, TOK)
            ks[rows, :] = jnp.where(lanes == h, keys, jnp.zeros_like(keys))
            p = jnp.exp(nt(keys, qs[rows, :]) - logs[h : h + 1])
            ds = (p * (nt(values, gs[rows, :]) - delta[h : h + 1])).astype(BF16)
            pl_scr[:, rows] = p.astype(BF16)
            dl_scr[:, rows] = ds
            ds_scr[rows, :] = ds
        dv_ref[at] = dv_ref[at] + nn(pl_scr[...], gs[...])
        dk_ref[at] = dk_ref[at] + nn(dl_scr[...], qs[...])
        dq_acc[...] = dq_acc[...] + tn(ds_scr[...], ks[...])

    before = jnp.maximum(place - f, 0)
    start = jnp.maximum(f - place, 0)

    def prev(i, _):
        at = PREV - before + i
        step(kp[at], vp[at], dkp_acc, dvp_acc, at)
        return 0

    def own(g, _):
        step(k[g], v[g], dk, dv, g)
        return 0

    lax.fori_loop(0, before, prev, 0)
    lax.fori_loop(start, f + 1, own, 0)
    dq[0] = turn(dq_acc[...] * 0.125, cp[...] + cf[0], -(sp[...] + sf[0])).astype(BF16)

    @pl.when(f == FPD - 1)
    def _():
        dkp[...] = dkp_acc[...].astype(BF16)
        dvp[...] = dvp_acc[...].astype(BF16)


def attend_back(places, q, k, v, kp, vp, grads, mixed, lse, tables):
    cp, sp, cf, sf = tables
    block = pl.BlockSpec((1, TOK, HC), lambda f, *_: (f, 0, 0))
    piece = pl.BlockSpec((1, PR, HC), lambda f, *_: (f, 0, 0))
    frame_table = pl.BlockSpec((1, 1, HC), lambda f, *_: (f, 0, 0))
    return pl.pallas_call(
        attend_back_kernel,
        out_shape=[
            jax.ShapeDtypeStruct((FPD, TOK, HC), BF16),
            jax.ShapeDtypeStruct((FPD, TOK, HC), F32),
            jax.ShapeDtypeStruct((FPD, TOK, HC), F32),
            jax.ShapeDtypeStruct((PREV, TOK, HC), BF16),
            jax.ShapeDtypeStruct((PREV, TOK, HC), BF16),
        ],
        grid_spec=pltpu.PrefetchScalarGridSpec(
            num_scalar_prefetch=1,
            grid=(FPD,),
            in_specs=[block]
            + [whole((FPD, TOK, HC))] * 2
            + [whole((PREV, TOK, HC))] * 2
            + [piece] * 8
            + [pl.BlockSpec((1, 8, TOK), lambda f, *_: (f, 0, 0))]
            + [whole((TOK, HC))] * 2
            + [frame_table] * 2,
            out_specs=[block]
            + [whole((FPD, TOK, HC))] * 2
            + [whole((PREV, TOK, HC))] * 2,
            scratch_shapes=[
                pltpu.VMEM((4 * TOK, HC), BF16),
                pltpu.VMEM((4 * TOK, HC), BF16),
                pltpu.VMEM((4 * TOK, HC), BF16),
                pltpu.VMEM((TOK, 4 * TOK), BF16),
                pltpu.VMEM((TOK, 4 * TOK), BF16),
                pltpu.VMEM((4 * TOK, TOK), BF16),
                pltpu.VMEM((TOK, HC), F32),
                pltpu.VMEM((PREV, TOK, HC), F32),
                pltpu.VMEM((PREV, TOK, HC), F32),
            ],
        ),
        compiler_params=params(44),
        cost_estimate=cost(36 * 4 * 5 * 2 * TOK**3, 16 * MB, 36 * 4 * TOK * TOK),
        name="attend_back",
    )(places, q, k, v, kp, vp, *grads, *mixed, lse, cp, sp, cf, sf)


HALF = 4


def flat(ref):
    return ref[...].reshape(HALF * PR, ref.shape[-1])


def frames_of(value):
    return value.reshape(HALF, PR, value.shape[-1])


def mid_kernel(o0, o1, o2, o3, w0, w1, w2, w3, ob, x, cot, g1, s2, c2, g2, branch, middle, hidden, down, dsum):
    total = ob[...]
    for o, w in zip((o0, o1, o2, o3), (w0, w1, w2, w3)):
        total = total + nn(flat(o), w[...])
    branched = frames_of(total)
    branch[...] = branched
    mid = x[...].astype(F32) + g1[...] * branched
    middle[...] = mid
    normal, _ = norm(mid)
    hidden[...] = (normal * (1.0 + c2[...]) + s2[...]).astype(BF16)
    grad = (g2[...] * cot[...].astype(F32)).astype(BF16)
    down[...] = grad
    sums = jnp.sum(grad.astype(F32).reshape(HALF * PR, D), axis=0, keepdims=True)

    @pl.when(pl.program_id(0) == 0)
    def _():
        dsum[...] = jnp.zeros_like(dsum)

    dsum[...] = dsum[...] + sums


def half_spec(width):
    return pl.BlockSpec((HALF, PR, width), lambda i, *_: (i, 0, 0))


def segment_spec(segment):
    return pl.BlockSpec((HALF, 1, D), lambda i, *_: (i, 0, segment))


def mid(pieces, weights, bias, x, cot, mod):
    return pl.pallas_call(
        mid_kernel,
        out_shape=[
            jax.ShapeDtypeStruct((FPD, PR, D), F32),
            jax.ShapeDtypeStruct((FPD, PR, D), F32),
            jax.ShapeDtypeStruct((FPD, PR, D), BF16),
            jax.ShapeDtypeStruct((FPD, PR, D), BF16),
            jax.ShapeDtypeStruct((1, D), F32),
        ],
        grid=(FPD // HALF,),
        in_specs=[half_spec(HC)] * 4
        + [whole((HC, D))] * 4
        + [whole((1, D)), half_spec(D), half_spec(D)]
        + [segment_spec(s) for s in (2, 3, 4, 5)],
        out_specs=[half_spec(D)] * 4 + [whole((1, D))],
        compiler_params=params(40),
        cost_estimate=cost(2 * 512 * D * D, 12 * MB),
        name="mid",
    )(*pieces, *weights, bias, x, cot, mod, mod, mod, mod)


def mid_back_kernel(hg, middle, branch, cot, g1, c2, w0, w1, w2, w3, mg, bg, a0, a1, a2, a3, sh, sc, ga, osum):
    grad = hg[...]
    normal, rate = norm(middle[...])
    sh[...] = jnp.sum(grad, axis=1, keepdims=True)
    sc[...] = jnp.sum(grad * normal, axis=1, keepdims=True)
    total = cot[...].astype(F32) + norm_back(normal, rate, grad * (1.0 + c2[...]))
    mg[...] = total
    ga[...] = jnp.sum(total * branch[...], axis=1, keepdims=True)
    low = (g1[...] * total).astype(BF16)
    bg[...] = low
    low = low.reshape(HALF * PR, D)
    sums = jnp.sum(low.astype(F32), axis=0, keepdims=True)

    @pl.when(pl.program_id(0) == 0)
    def _():
        osum[...] = jnp.zeros_like(osum)

    osum[...] = osum[...] + sums
    for a, w in zip((a0, a1, a2, a3), (w0, w1, w2, w3)):
        a[...] = frames_of(nt(low, w[...]).astype(BF16))


def mid_back(hg, middle, branch, cot, mod, weights):
    frame_sum = pl.BlockSpec((HALF, 1, D), lambda i, *_: (i, 0, 0))
    return pl.pallas_call(
        mid_back_kernel,
        out_shape=[
            jax.ShapeDtypeStruct((FPD, PR, D), F32),
            jax.ShapeDtypeStruct((FPD, PR, D), BF16),
        ]
        + [jax.ShapeDtypeStruct((FPD, PR, HC), BF16)] * 4
        + [jax.ShapeDtypeStruct((FPD, 1, D), F32)] * 3
        + [jax.ShapeDtypeStruct((1, D), F32)],
        grid=(FPD // HALF,),
        in_specs=[half_spec(D)] * 4
        + [segment_spec(2), segment_spec(4)]
        + [whole((HC, D))] * 4,
        out_specs=[half_spec(D)] * 2 + [half_spec(HC)] * 4 + [frame_sum] * 3 + [whole((1, D))],
        compiler_params=params(40),
        cost_estimate=cost(2 * 512 * D * D, 12 * MB),
        name="mid_back",
    )(hg, middle, branch, cot, mod, mod, *weights)


NB = 512
STEPS = FF // NB
PER = D // NB
TOKENS = FPD * PR


def up_column(t, row):
    return (row ^ (t // PER)) * PER + t % PER


def own_step(j):
    return lambda t: jnp.clip(t - j * PER, 0, PER - 1)


def down_spec(j):
    return pl.BlockSpec((NB, D), lambda t, row: (own_step(j)(t), 0))


def pick_down(d0, d1, d2, d3):
    j = pl.program_id(0) // PER
    return jnp.where(
        j < 2, jnp.where(j == 0, d0[...], d1[...]), jnp.where(j == 2, d2[...], d3[...])
    )


def feed_kernel(row_ref, h2, dg, u0, u1, u2, u3, ub, d0, d1, d2, d3, act, upg, hg, usum):
    row = row_ref[0]
    ups = (u0, u1, u2, u3)
    down = pick_down(d0, d1, d2, d3)
    u = ub[...]
    for j, w in enumerate(ups):
        u = u + nn(h2[:, columns(row, j)], w[...])
    rate = math.sqrt(2.0 / math.pi)
    square = u * u
    wave = jnp.tanh(rate * (u + 0.044715 * (u * square)))
    act[...] = (0.5 * u * (1.0 + wave)).astype(BF16)
    slope = 0.5 * (1.0 + wave) + 0.5 * u * (1.0 - wave * wave) * (
        rate * (1.0 + 3.0 * 0.044715 * square)
    )
    grad = (nt(dg[...], down) * slope).astype(BF16)
    upg[...] = grad
    usum[...] = jnp.sum(grad.astype(F32), axis=0, keepdims=True)

    @pl.when(pl.program_id(0) == 0)
    def _():
        hg[...] = jnp.zeros_like(hg)

    for j, w in enumerate(ups):
        hg[:, columns(row, j)] = hg[:, columns(row, j)] + nt(grad, w[...])


def feed(row, h2, dg, ups, up_bias, downs):
    tok = whole((TOKENS, D))
    block = pl.BlockSpec((TOKENS, NB), lambda t, row: (0, t))
    bias = pl.BlockSpec((1, NB), lambda t, row: (0, up_column(t, row[0])))
    return pl.pallas_call(
        feed_kernel,
        out_shape=[
            jax.ShapeDtypeStruct((TOKENS, FF), BF16),
            jax.ShapeDtypeStruct((TOKENS, FF), BF16),
            jax.ShapeDtypeStruct((TOKENS, D), F32),
            jax.ShapeDtypeStruct((1, FF), F32),
        ],
        grid_spec=pltpu.PrefetchScalarGridSpec(
            num_scalar_prefetch=1,
            grid=(STEPS,),
            in_specs=[tok, tok]
            + [pl.BlockSpec((HC, NB), lambda t, row: (0, up_column(t, row[0])))] * 4
            + [bias]
            + [down_spec(j) for j in range(4)],
            out_specs=[block, block, tok, bias],
        ),
        compiler_params=params(44),
        cost_estimate=cost(3 * 2 * TOKENS * D * FF, 30 * MB, TOKENS * FF),
        name="feed",
    )(row, h2, dg, *ups, up_bias, *downs)


def feed_back_kernel(row_ref, h2, dg, act, upg, d0, d1, d2, d3, dn, w0, w1, w2, w3, e0, e1, e2, e3):
    row = row_ref[0]
    j_now = pl.program_id(0) // PER
    down = pick_down(d0, d1, d2, d3)
    active = act[...]

    @pl.when(pl.program_id(0) == 0)
    def _():
        dn[...] = jnp.zeros_like(dn)

    dn[...] = dn[...] + nn(active, down)
    part = tn(active, dg[...]).astype(BF16)
    for j, e in enumerate((e0, e1, e2, e3)):

        @pl.when(j_now == j)
        def _():
            e[...] = part

    grad = upg[...]
    for j, w in enumerate((w0, w1, w2, w3)):
        w[0] = tn(h2[:, columns(row, j)], grad).astype(BF16)


def feed_back(row, h2, dg, act, upg, downs):
    tok = whole((TOKENS, D))
    block = pl.BlockSpec((TOKENS, NB), lambda t, row: (0, t))
    up_out = pl.BlockSpec(
        (1, HC, NB), lambda t, row: (up_column(t, row[0]) // PER, 0, up_column(t, row[0]) % PER)
    )
    return pl.pallas_call(
        feed_back_kernel,
        out_shape=[jax.ShapeDtypeStruct((TOKENS, D), F32)]
        + [jax.ShapeDtypeStruct((4, HC, D), BF16)] * 4
        + [jax.ShapeDtypeStruct((D, D), BF16)] * 4,
        grid_spec=pltpu.PrefetchScalarGridSpec(
            num_scalar_prefetch=1,
            grid=(STEPS,),
            in_specs=[tok, tok, block, block] + [down_spec(j) for j in range(4)],
            out_specs=[tok] + [up_out] * 4 + [down_spec(j) for j in range(4)],
        ),
        compiler_params=params(48),
        cost_estimate=cost(3 * 2 * TOKENS * D * FF, 40 * MB),
        name="feed_back",
    )(row, h2, dg, act, upg, *downs)


def project_back_kernel(row_ref, dq, dk, dv, rk, rv, w0, w1, w2, w3, cp, sp, cf, sf, dp, h0, h1, h2, h3, bsum):
    row = row_ref[0]
    f = pl.program_id(0)
    later = (f > 0).astype(F32)
    keys = dk[0] + later * rk[0].astype(F32)
    values = dv[0] + later * rv[0].astype(F32)
    dp[0, :, :HC] = dq[0]
    dp[0, :, HC : 2 * HC] = turn(keys, cp[...] + cf[0], -(sp[...] + sf[0])).astype(BF16)
    dp[0, :, 2 * HC :] = values.astype(BF16)
    grad = dp[0]
    sums = jnp.sum(grad.astype(F32), axis=0, keepdims=True)

    @pl.when(f == 0)
    def _():
        bsum[...] = jnp.zeros_like(bsum)

    bsum[...] = bsum[...] + sums
    for j, w in enumerate((w0, w1, w2, w3)):
        part = nt(grad, w[...]).astype(BF16)
        for i, h in enumerate((h0, h1, h2, h3)):
            h[0, :, columns(row, j)] = part[i * PR : (i + 1) * PR]


def project_back(row, dq, dk, dv, rk, rv, weights, tables):
    cp, sp, cf, sf = tables
    block = pl.BlockSpec((1, TOK, HC), lambda f, *_: (f, 0, 0))
    late = pl.BlockSpec((1, TOK, HC), lambda f, *_: (jnp.maximum(f - 1, 0), 0, 0))
    frame_table = pl.BlockSpec((1, 1, HC), lambda f, *_: (f, 0, 0))
    return pl.pallas_call(
        project_back_kernel,
        out_shape=[jax.ShapeDtypeStruct((FPD, TOK, 3 * HC), BF16)]
        + [jax.ShapeDtypeStruct((FPD, PR, D), BF16)] * 4
        + [jax.ShapeDtypeStruct((1, 3 * HC), F32)],
        grid_spec=pltpu.PrefetchScalarGridSpec(
            num_scalar_prefetch=1,
            grid=(FPD,),
            in_specs=[block] * 3
            + [late] * 2
            + [whole((HC, 3 * HC))] * 4
            + [whole((TOK, HC))] * 2
            + [frame_table] * 2,
            out_specs=[pl.BlockSpec((1, TOK, 3 * HC), lambda f, *_: (f, 0, 0))]
            + [pl.BlockSpec((1, PR, D), lambda f, *_: (f, 0, 0))] * 4
            + [whole((1, 3 * HC))],
        ),
        compiler_params=params(32),
        cost_estimate=cost(2 * FPD * TOK * D * 3 * HC, 14 * MB),
        name="project_back",
    )(row, dq, dk, dv, rk, rv, *weights, cp, sp, cf, sf)


def weight_kernel(row_ref, h, dp, w):
    w[0] = tn(h[...], dp[...]).astype(BF16)


def project_weight(row, hidden, dproj):
    tokens = FPD * TOK
    return pl.pallas_call(
        weight_kernel,
        out_shape=jax.ShapeDtypeStruct((4, HC, 3 * HC), BF16),
        grid_spec=pltpu.PrefetchScalarGridSpec(
            num_scalar_prefetch=1,
            grid=(4,),
            in_specs=[
                pl.BlockSpec((tokens, HC), lambda j, row: (0, row[0] ^ j)),
                whole((tokens, 3 * HC)),
            ],
            out_specs=pl.BlockSpec((1, HC, 3 * HC), lambda j, row: (j, 0, 0)),
        ),
        compiler_params=params(32),
        cost_estimate=cost(2 * tokens * D * 3 * HC, 9 * MB),
        name="project_weight",
    )(row, hidden.reshape(tokens, D), dproj.reshape(tokens, 3 * HC))


def input_back_kernel(x, near, far, c1, mg, out, sh, sc):
    grad = near[...] + far[...].astype(F32)
    normal, rate = norm(x[...].astype(F32))
    sh[...] = jnp.sum(grad, axis=1, keepdims=True)
    sc[...] = jnp.sum(grad * normal, axis=1, keepdims=True)
    out[...] = mg[...] + norm_back(normal, rate, grad * (1.0 + c1[...]))


def input_back(x, near, far, mod, mg):
    frame_sum = pl.BlockSpec((HALF, 1, D), lambda i, *_: (i, 0, 0))
    return pl.pallas_call(
        input_back_kernel,
        out_shape=[jax.ShapeDtypeStruct((FPD, PR, D), F32)]
        + [jax.ShapeDtypeStruct((FPD, 1, D), F32)] * 2,
        grid=(FPD // HALF,),
        in_specs=[half_spec(D)] * 3 + [segment_spec(1), half_spec(D)],
        out_specs=[half_spec(D)] + [frame_sum] * 2,
        compiler_params=params(32),
        cost_estimate=cost(20 * 512 * D, 10 * MB),
        name="input_back",
    )(x, near, far, mod, mg)


def row_sum(value):
    value = value + swap(value, CORE)
    return value + swap(value, DIRECT)


def row_pieces(value):
    return [value, swap(value, CORE), swap(value, DIRECT), swap(value, DIRECT ^ CORE)]


def seq_gather(value):
    value = jnp.stack([value, swap(value, FAR)])
    value = jnp.concatenate([value] + [swap(value, m) for m in (16, 32, 48)])
    return jnp.concatenate([value] + [swap(value, m) for m in (4, 8, 12)])


def by_row(pieces, row):
    a, b, c, d = pieces
    odd, high = row % 2 == 1, row >= 2
    a, b = jnp.where(odd, b, a), jnp.where(odd, a, b)
    c, d = jnp.where(odd, d, c), jnp.where(odd, c, d)
    return jnp.stack(
        [
            jnp.where(high, c, a),
            jnp.where(high, d, b),
            jnp.where(high, a, c),
            jnp.where(high, b, d),
        ]
    )


def angle_tables(row, places):
    index = jnp.arange(HC) % (HD // 2)
    quarter, eighth = HD // 4, HD // 8
    in_frame = index < quarter
    in_row = (index >= quarter) & (index < quarter + eighth)
    offset = jnp.where(
        in_frame, index, jnp.where(in_row, index - quarter, index - quarter - eighth)
    ).astype(F32)
    length = jnp.where(in_frame, 1.0 * quarter, 1.0 * eighth)
    frequency = jnp.exp(-math.log(10000.0) * offset / length)
    sign = jnp.where(jnp.arange(HC) % HD < HD // 2, -1.0, 1.0)
    slot = jnp.arange(TOK, dtype=jnp.int32)
    patch = ((slot // PR) ^ row) * PR + slot % PR
    position = jnp.where(in_row, (patch // GRID)[:, None], (patch % GRID)[:, None]).astype(F32)
    angle = position * frequency
    cp = jnp.where(in_frame, 0.0, jnp.cos(angle))
    sp = jnp.where(in_frame, 0.0, jnp.sin(angle) * sign)

    def frame_table(place):
        angle = place.astype(F32)[:, None] * frequency
        cf = jnp.where(in_frame, jnp.cos(angle), 0.0)
        sf = jnp.where(in_frame, jnp.sin(angle) * sign, 0.0)
        return cf[:, None, :], sf[:, None, :]

    return cp, sp, frame_table


def per_device(
    activations,
    noise_embed,
    frame_position,
    cotangent,
    ada_weight,
    ada_bias,
    qkv_weight,
    qkv_bias,
    out_weight,
    out_bias,
    up_weight,
    up_bias,
    down_weight,
    down_bias,
):
    row = lax.axis_index(("xl", "c"))
    row_arg = row.astype(jnp.int32).reshape(1)

    x0 = activations
    x2 = swap(x0, DIRECT)
    x1 = swap(x0, CORE)
    x3 = swap(x2, CORE)
    before = shift(activations[1:], 1)
    p0 = after(before, x2)
    p2 = swap(p0, DIRECT)
    p1 = swap(p0, CORE)
    p3 = swap(p2, CORE)

    heads = qkv_weight.reshape(HC, 3, 4, HC)
    masks = (0, CORE, OTHER, OTHER ^ CORE)
    qkv_pieces = []
    for j in range(4):
        piece = lax.dynamic_index_in_dim(heads, row ^ j, 2, keepdims=False).reshape(HC, 3 * HC)
        qkv_pieces.append(piece if j == 0 else swap(piece, masks[j]))

    pack = jnp.concatenate([ada_bias, qkv_bias, out_bias, up_bias, down_bias])[None]
    full = by_row(row_pieces(pack), row)[:, 0].astype(F32)
    ada_b = full[:, :1536].reshape(1, 6 * D)
    qkv_b = full[:, 1536:2304].reshape(3, 4, HC)
    qkv_b = lax.dynamic_index_in_dim(qkv_b, row, 1, keepdims=False).reshape(1, 3 * HC)
    out_b = full[:, 2304:2560].reshape(1, D)
    up_b = full[:, 2560:3584].reshape(1, FF)
    down_b = full[:, 3584:].reshape(1, D)

    embed = noise_embed.astype(F32)
    silu = jax.nn.silu(embed).astype(BF16)
    silu_own = lax.dynamic_slice_in_dim(silu, row * HC, HC, 1)
    silu_prev = shift(silu_own, 1)
    part = jnp.concatenate(
        [
            jnp.dot(silu_own, ada_weight, preferred_element_type=F32),
            jnp.dot(silu_prev, ada_weight[:, : 2 * D], preferred_element_type=F32),
        ],
        axis=1,
    )
    modulation = row_sum(part) + jnp.concatenate([ada_b, ada_b[:, : 2 * D]], axis=1)
    mod = modulation[:, None, :]

    cp, sp, frame_table = angle_tables(row, frame_position)
    own_tables = (cp, sp) + frame_table(frame_position)
    prev_tables = (cp, sp) + frame_table(shift(frame_position.astype(F32)[1:], 1))

    late = lambda value: after(value, p2)
    out_own = late(out_weight)
    up_own = late(up_weight)
    down_own = late(down_weight)
    outs2 = swap(out_own, OTHER)
    ups2 = jnp.concatenate([swap(up_own[:96], DIRECT), swap(up_own[96:], OTHER)])
    downs2 = jnp.concatenate([swap(down_own[:384], DIRECT), swap(down_own[384:], OTHER)])
    outs = [out_weight, swap(out_own, CORE), outs2, swap(outs2, CORE)]
    ups = [up_weight, swap(up_own, CORE), ups2, swap(ups2, CORE)]
    downs = [down_weight, swap(down_own, CORE), downs2, swap(downs2, CORE)]

    hidden1, q, k, v = project(True, row_arg, (x0, x1, x2, x3), mod, qkv_pieces, qkv_b, own_tables)
    kp, vp = project(False, row_arg, (p0, p1, p2, p3), mod, qkv_pieces, qkv_b, prev_tables)
    *mixed, lse = attend(frame_position, q, k, v, kp, vp)
    turned = [mixed[0]] + [swap(mixed[j], (0, CORE, DIRECT, DIRECT ^ CORE)[j]) for j in (1, 2, 3)]
    branch, middle, hidden2, down_grad, down_sum = mid(turned, outs, out_b, x0, cotangent, mod)
    h2 = hidden2.reshape(TOKENS, D)
    dg = down_grad.reshape(TOKENS, D)
    act, upg, hg, up_sum = feed(row_arg, h2, dg, ups, up_b, downs)
    mg, bg, *rest = mid_back(hg.reshape(FPD, PR, D), middle, branch, cotangent, mod, outs)
    ag, (shift2, scale2, gate1, out_sum) = rest[:4], rest[4:]
    back = [ag[0]] + [swap(ag[j], (0, CORE, DIRECT, DIRECT ^ CORE)[j]) for j in (1, 2, 3)]

    dn, *grads = feed_back(row_arg, h2, dg, act, upg, downs)
    up_parts, down_parts = grads[:4], grads[4:]
    downward = (dn + down_b).reshape(FPD, PR, D)
    layer_output = (middle + mod[:, :, 5 * D : 6 * D] * downward).astype(BF16)
    gate2 = jnp.sum(cotangent.astype(F32) * downward, axis=1)
    out_parts = [
        tn(t.reshape(TOKENS, HC), bg.reshape(TOKENS, D)).astype(BF16) for t in turned
    ]

    def core_sum(parts, j):
        own = parts[j].astype(F32)
        return (own + swap(parts[j + 1], CORE).astype(F32)).astype(BF16)

    packed = jnp.stack(
        [
            jnp.concatenate(
                [
                    core_sum(up_parts, j).reshape(D, D),
                    core_sum(down_parts, j),
                    core_sum(out_parts, j),
                ]
            )
            for j in (0, 2)
        ]
    )
    scattered = lax.psum_scatter(packed, ("z", "y"), scatter_dimension=1, tiled=True)
    share = scattered[0].astype(F32) + swap(scattered[1], DIRECT).astype(F32)
    share = (share + swap(share.astype(BF16), FAR).astype(F32)).astype(BF16)
    totals = lax.all_gather(share, ("z", "y"), axis=0, tiled=True)
    up_total = totals[:D].reshape(4, HC, D).transpose(1, 0, 2).reshape(HC, FF).astype(F32)
    down_total = totals[D : 2 * D].astype(F32)
    out_total = totals[2 * D :].astype(F32)

    dq, dk, dv, dkp, dvp = attend_back(
        frame_position, q, k, v, kp, vp, back, mixed, lse, own_tables
    )
    rk, rv = shift(dkp, -1), shift(dvp, -1)
    dproj, *pieces, qkv_sum = project_back(row_arg, dq, dk, dv, rk, rv, qkv_pieces, own_tables)
    near0 = pieces[0].astype(F32) + swap(pieces[1], CORE).astype(F32)
    near2 = pieces[2].astype(F32) + swap(pieces[3], CORE).astype(F32)
    far = swap(near2.astype(BF16), DIRECT)
    input_grad, shift1, scale1 = input_back(x0, near0, far, mod, mg)

    qkv_parts = project_weight(row_arg, hidden1, dproj)
    qkv_parts = lax.psum_scatter(qkv_parts, ("z", "y"), scatter_dimension=1, tiled=True)
    qkv_parts = (
        qkv_parts.astype(F32) + swap(qkv_parts, FAR).astype(F32)
    ).astype(BF16)
    qkv_turned = [qkv_parts[0]] + [
        swap(qkv_parts[j], (0, CORE, DIRECT, DIRECT ^ CORE)[j]) for j in (1, 2, 3)
    ]
    qkv_share = by_row(qkv_turned, row).reshape(4, 16, 3, HC).transpose(1, 2, 0, 3)
    qkv_total = lax.all_gather(
        qkv_share.reshape(16, 3 * D), ("z", "y"), axis=0, tiled=True
    ).astype(F32)

    early = jnp.concatenate(
        [
            gate1[:, 0],
            shift2[:, 0],
            scale2[:, 0],
            gate2,
            jnp.concatenate([down_sum, up_sum, out_sum], axis=1).reshape(FPD, 768),
        ],
        axis=1,
    )
    early = row_sum(early)
    early_all = seq_gather(early.astype(BF16))
    qkv_sum = lax.dynamic_update_slice(
        jnp.zeros((3, 4, HC), F32), qkv_sum.reshape(3, 1, HC), (0, row, 0)
    )
    final = jnp.concatenate([shift1[:, 0], scale1[:, 0], qkv_sum.reshape(FPD, 384)], axis=1)
    final = row_sum(final)
    final_all = seq_gather(final.astype(BF16))
    silu_all = seq_gather(silu_own).reshape(256, HC)

    mod_all = jnp.concatenate([final_all[:, :, : 2 * D], early_all[:, :, : 4 * D]], axis=2)
    mod_all = mod_all.reshape(256, 6 * D)
    ada_total = tn(silu_all, mod_all)
    ada_sum = jnp.sum(mod_all.astype(F32), axis=0)
    ada_sum = lax.dynamic_slice_in_dim(ada_sum, row * 1536, 1536)
    bias_sum = jnp.sum(early_all[:, :, 4 * D :].astype(F32), axis=0).reshape(6144)
    down_sum = lax.dynamic_slice_in_dim(bias_sum, row * HC, HC)
    up_sum = lax.dynamic_slice_in_dim(bias_sum, D + row * D, D)
    out_sum = lax.dynamic_slice_in_dim(bias_sum, 5 * D + row * HC, HC)
    qkv_sum = jnp.sum(final_all[:, :, 2 * D :].astype(F32), axis=0).reshape(3 * D)
    qkv_sum = lax.dynamic_slice_in_dim(qkv_sum, row * 768, 768)

    mod_own = jnp.concatenate([final[:, : 2 * D], early[:, : 4 * D]], axis=1).astype(BF16)
    silu_grad = nt(mod_own, ada_weight)
    silu_grad = by_row(row_pieces(silu_grad), row).transpose(1, 0, 2).reshape(FPD, D)
    gate = jax.nn.sigmoid(embed)
    embed_grad = silu_grad * (gate * (1.0 + embed * (1.0 - gate)))

    return (
        layer_output,
        input_grad,
        embed_grad,
        ada_total,
        ada_sum,
        qkv_total,
        qkv_sum,
        out_total,
        out_sum,
        up_total,
        up_sum,
        down_total,
        down_sum,
    )


def solution(mesh):
    fine = Mesh(mesh.devices.reshape(2, 4, 4, 2, 2), AXES)
    seq, row = ("xh", "z", "y"), ("xl", "c")
    token, weight, vector = P(seq, row, None), P(row, None), P(row)
    in_specs = (token, P(seq, None), P(seq), token) + (weight, vector) * 5
    out_specs = (token, token, P(seq, None)) + (weight, vector) * 5
    return jax.shard_map(
        per_device, mesh=fine, in_specs=in_specs, out_specs=out_specs, check_vma=False
    )
```

time: 2150 us -> 747 us (0.35)
  waiting for transfers between devices: 1020 us -> 329 us
  matrix products: 416 us -> 17.2 us
  local copies, waits for them, and re-layouts: 354 us -> 72.3 us
  Pallas kernels: 0 us -> 169 us
  blocking collectives: 136 us -> 0 us
  other arithmetic: 150 us -> 61.3 us
  starting transfers between devices: 16 us -> 74.5 us
  loops' own time: 27.5 us -> 0 us
    dot_general x71 -> x8, matrix products: 416 us -> 17.2 us  [the longest x5 10.5 us: tn(): lax.dot_general(left, right, (((0,), (0,)), ((), ())), preferred_element_...]
    reduce_scatter x7 -> x2, waiting for transfers between devices: 398 us -> 74.3 us  [the longest x1 47.9 us: per_device(): lax.psum_scatter(packed, ('z', 'y'), scatter_dimension=1, tiled=True)]
    psum x1 -> x0, waiting for transfers between devices: 264 us -> none  [per_device(): lax.psum(owned[0].astype(jnp.bfloat16), 'seq').astype(jnp.float32)]
    all_gather x7 -> x2, waiting for transfers between devices: 229 us -> 6.66 us  [the longest x1 6.66 us: per_device(): totals = lax.all_gather(share, ('z', 'y'), axis=0, tiled=True)]
    pallas_call x0 -> x11, Pallas kernels: none -> 169 us  [the longest x1 43.6 us: attend_back(): pl.pallas_call(attend_back_kernel, out_shape=[jax.ShapeDtypeStruct((FPD,...]
    ppermute x4 -> x79, waiting for transfers between devices: 122 us -> 248 us  [the longest x74 174 us: swap(): return lax.ppermute(value, AXES, [(i, i ^ mask) for i in range(128)])]
    psum x2 -> x0, blocking collectives: 110 us -> none  [the longest x1 97.8 us: per_device(): lax.psum(owned[1].astype(jnp.bfloat16), 'seq').astype(jnp.float32)]
    dynamic_slice x74 -> x6, local copies, waits for them, and re-layouts: 103 us -> 3.65 us  [the longest x1 1.04 us: per_device(): lax.dynamic_index_in_dim(heads, row ^ j, 2, keepdims=False)]
  transfers between devices with their start and end apart: 19 -> 83, of which waited for: 13 -> 35; matrix products, arithmetic and copies ran while one was open for 19% -> 16% of each run, Pallas kernels for 0% -> 19%
where the time goes in v1:
time: 747 us; the launch traced here: 739 us
  waiting for transfers between devices  329 us (44%)
  Pallas kernels  169 us (23%)
  starting transfers between devices  74.5 us (10%)
  local copies, waits for them, and re-layouts  72.3 us (10%)
  other arithmetic  61.3 us (8%)
  matrix products  17.2 us (2%)
  between operations  15.4 us (2%)
    ppermute x74, waiting for transfers between devices, swap(): return lax.ppermute(value, AXES, [(i, i ^ mask) for i in range(128)])  174 us
    ppermute x5, waiting for transfers between devices, shift(): lax.ppermute(value, AXES, [(i, i + 4 * steps) for i in range(first, last)])  74.1 us
    ppermute x74, starting transfers between devices, swap(): return lax.ppermute(value, AXES, [(i, i ^ mask) for i in range(128)])  60.2 us
    reduce_scatter x1, waiting for transfers between devices, per_device(): lax.psum_scatter(packed, ('z', 'y'), scatter_dimension=1, tiled=True)  47.9 us
    pallas_call x1, Pallas kernels, attend_back(): pl.pallas_call(attend_back_kernel, out_shape=[jax.ShapeDtypeStruct((FPD,...  43.6 us
    unnamed x121, local copies, waits for them, and re-layouts  31.8 us
    pallas_call x1, Pallas kernels, attend(): pl.pallas_call(attend_kernel, out_shape=[jax.ShapeDtypeStruct((FPD, PR, H...  29.8 us
    pallas_call x1, Pallas kernels, feed_back(): pl.pallas_call(feed_back_kernel, out_shape=[jax.ShapeDtypeStruct((TOKENS,...  26.8 us
  transfers between devices with their start and end apart: 83, of which 35 were waited for; matrix products, arithmetic and copies ran while one was open for 16% of the time, Pallas kernels for 19%

profile of v1, /device:TPU:6, one launch (start us, length us, event | category | flops | bytes accessed | tf_op | source)
XLA Modules:
  0.0 738.7 jit_solution(5400042658864130473)
XLA Ops:
  48.3 39.0 %collective-permute-done.12.refs_1_ = bf16[7,64,1024]{2,1,0:T(8,128)(2,1)} collective-permute-done((bf16[7,64,1024]{2,1,0:T(8,128)(2,1)}, bf16[7,64,1024]{2,1,0:T(8,128)(2,1)}, u32[]{:S(2)}, u32[]{:S(2)}) %collective-permute-start.12) | collective-permute-done | bytes 917536 | tf_op jit(solution)/shard_map/ppermute | solution.py:32
  89.4 24.9 %collective-permute-done.14.refs_3_ = bf16[7,64,1024]{2,1,0:T(8,128)(2,1)} collective-permute-done((bf16[7,64,1024]{2,1,0:T(8,128)(2,1)}, bf16[7,64,1024]{2,1,0:T(8,128)(2,1)}, u32[]{:S(2)}, u32[]{:S(2)}) %collective-permute-start.14) | collective-permute-done | bytes 917536 | tf_op jit(solution)/shard_map/ppermute | solution.py:27
  124.4 11.1 %project_own.1 = (bf16[8,256,1024]{2,1,0:T(8,128)(2,1)S(1)}, bf16[8,256,256]{2,1,0:T(8,128)(2,1)S(1)}, bf16[8,256,256]{2,1,0:T(8,128)(2,1)S(1)}, bf16[8,256,256]{2,1,0:T(8,128)(2,1)S(1)}) custom-call(s32[1]{0:T(128)} %bitcast.refs_0_.row_ref, bf16[8,64,1024]{2,1,0:T(8,128)(2,1)S(1)} %copy-done.1, bf16[8,64,1024]{2,1,0:T(8,128)(2,1)S(1)} %collective-permute-done.refs_2_, ...), custom_call_target="tpu_custom_call" | custom-call | flops 3221225472 | bytes 12582912 | tf_op jit(solution)/shard_map/project_own/pallas_call | solution.py:133
  137.6 16.5 %collective-permute-done.24 = bf16[96,4096]{1,0:T(8,128)(2,1)S(1)} collective-permute-done((bf16[96,4096]{1,0:T(8,128)(2,1)S(1)}, bf16[96,4096]{1,0:T(8,128)(2,1)S(1)}, u32[]{:S(2)}, u32[]{:S(2)}) %collective-permute-start.24) | collective-permute-done | bytes 786464 | tf_op jit(solution)/shard_map/ppermute | solution.py:27
  157.9 22.7 %collective-permute-done.29 = bf16[640,1024]{1,0:T(8,128)(2,1)S(1)} collective-permute-done((bf16[640,1024]{1,0:T(8,128)(2,1)S(1)}, bf16[640,1024]{1,0:T(8,128)(2,1)S(1)}, u32[]{:S(2)}, u32[]{:S(2)}) %collective-permute-start.29) | collective-permute-done | bytes 1310752 | tf_op jit(solution)/shard_map/ppermute | solution.py:27
  182.4 8.1 %collective-permute-done.21.w2 = bf16[256,1024]{1,0:T(8,128)(2,1)S(1)} collective-permute-done((bf16[256,1024]{1,0:T(8,128)(2,1)S(1)}, bf16[256,1024]{1,0:T(8,128)(2,1)S(1)}, u32[]{:S(2)}, u32[]{:S(2)}) %collective-permute-start.21) | collective-permute-done | bytes 524320 | tf_op jit(solution)/shard_map/ppermute | solution.py:27
  190.9 8.6 %project_prev.1 = (bf16[7,256,256]{2,1,0:T(8,128)(2,1)S(1)}, bf16[7,256,256]{2,1,0:T(8,128)(2,1)S(1)}) custom-call(s32[1]{0:T(128)} %bitcast.refs_0_.row_ref, bf16[7,64,1024]{2,1,0:T(8,128)(2,1)} %collective-permute-done.12.refs_1_, bf16[7,64,1024]{2,1,0:T(8,128)(2,1)S(1)} %collective-permute-done.13.refs_2_, ...), custom_call_target="tpu_custom_call" | custom-call | flops 2818572288 | bytes 11534336 | tf_op jit(solution)/shard_map/project_prev/pallas_call | solution.py:133
  199.8 29.8 %attend.1 = (bf16[8,64,256]{2,1,0:T(8,128)(2,1)S(1)}, bf16[8,64,256]{2,1,0:T(8,128)(2,1)S(1)}, bf16[8,64,256]{2,1,0:T(8,128)(2,1)S(1)}, bf16[8,64,256]{2,1,0:T(8,128)(2,1)S(1)}, f32[8,8,256]{2,1,0:T(8,128)S(1)}) custom-call(s32[8]{0:T(128)S(1)} %copy-done.17, bf16[8,256,256]{2,1,0:T(8,128)(2,1)S(1)} %get-tuple-element.70.q, ...), custom_call_target="tpu_custom_call" | custom-call | flops 9663676416 | bytes 6291456 | tf_op jit(solution)/shard_map/attend/pallas_call | solution.py:218
  231.3 8.6 %collective-permute-done.18.o2 = bf16[8,64,256]{2,1,0:T(8,128)(2,1)S(1)} collective-permute-done((bf16[8,64,256]{2,1,0:T(8,128)(2,1)S(1)}, bf16[8,64,256]{2,1,0:T(8,128)(2,1)S(1)}, u32[]{:S(2)}, u32[]{:S(2)}) %collective-permute-start.18) | collective-permute-done | bytes 262176 | tf_op jit(solution)/shard_map/ppermute | solution.py:27
  239.9 8.3 %collective-permute-done.19.o3 = bf16[8,64,256]{2,1,0:T(8,128)(2,1)S(1)} collective-permute-done((bf16[8,64,256]{2,1,0:T(8,128)(2,1)S(1)}, bf16[8,64,256]{2,1,0:T(8,128)(2,1)S(1)}, u32[]{:S(2)}, u32[]{:S(2)}) %collective-permute-start.19) | collective-permute-done | bytes 262176 | tf_op jit(solution)/shard_map/ppermute | solution.py:27
  255.3 25.5 %feed.1 = (bf16[512,4096]{1,0:T(8,128)(2,1)}, bf16[512,4096]{1,0:T(8,128)(2,1)}, f32[512,1024]{1,0:T(8,128)S(1)}, f32[1,4096]{1,0:T(1,128)S(1)}) custom-call(s32[1]{0:T(128)} %bitcast.refs_0_.row_ref, bf16[512,1024]{1,0:T(8,128)(2,1)S(1)} %bitcast.176, bf16[512,1024]{1,0:T(8,128)(2,1)S(1)} %bitcast.178, bf16[256,4096]{1,0:T(8,128)(2,1)} %u0.1, ...), custom_call_target="tpu_custom_call" | custom-call | flops 12884901888 | bytes 31457280 | tf_op jit(solution)/shard_map/feed/pallas_call | solution.py:517
  289.7 26.8 %feed_back.1 = (f32[512,1024]{1,0:T(8,128)S(1)}, bf16[4,256,1024]{2,1,0:T(8,128)(2,1)}, bf16[4,256,1024]{2,1,0:T(8,128)(2,1)}, bf16[4,256,1024]{2,1,0:T(8,128)(2...) custom-call(s32[1]{0:T(128)} %bitcast.refs_0_.row_ref, ...), custom_call_target="tpu_custom_call" | custom-call | flops 12884901888 | bytes 41943040 | tf_op jit(solution)/shard_map/feed_back/pallas_call | solution.py:569
  320.6 43.6 %attend_back.1 = (bf16[8,256,256]{2,1,0:T(8,128)(2,1)S(1)}, f32[8,256,256]{2,1,0:T(8,128)}, f32[8,256,256]{2,1,0:T(8,128)}, bf16[7,256,256]{2,1,0:T(8,128)(2,1)S(1)}, bf16[7,256,256]{2,1,0:T(8,128)(2,1)S(1)}) custom-call(s32[8]{0:T(128)S(1)} %copy-done.17, bf16[8,256,256]{2,1,0:T(8,128)(2,1)S(1)} %copy-done.27, bf16[8,256,256]{2,1,0:T(8,128)(2,1)S(1)} %copy-done.29, ...), custom_call_target="tpu_custom_call" | custom-call | flops 24159191040 | bytes 16777216 | tf_op jit(solution)/shard_map/attend_back/pallas_call | solution.py:316
  369.4 19.9 %collective-permute-done.34.rk = bf16[7,256,256]{2,1,0:T(8,128)(2,1)S(1)} collective-permute-done((bf16[7,256,256]{2,1,0:T(8,128)(2,1)S(1)}, bf16[7,256,256]{2,1,0:T(8,128)(2,1)S(1)}, u32[]{:S(2)}, u32[]{:S(2)}) %collective-permute-start.34) | collective-permute-done | bytes 917536 | tf_op jit(solution)/shard_map/ppermute | solution.py:32
  393.1 15.2 %collective-permute-done.35.rv = bf16[7,256,256]{2,1,0:T(8,128)(2,1)S(1)} collective-permute-done((bf16[7,256,256]{2,1,0:T(8,128)(2,1)S(1)}, bf16[7,256,256]{2,1,0:T(8,128)(2,1)S(1)}, u32[]{:S(2)}, u32[]{:S(2)}) %collective-permute-start.35) | collective-permute-done | bytes 917536 | tf_op jit(solution)/shard_map/ppermute | solution.py:32
  408.3 9.5 %project_back.1 = (bf16[8,256,768]{2,1,0:T(8,128)(2,1)S(1)}, bf16[8,64,1024]{2,1,0:T(8,128)(2,1)S(1)}, bf16[8,64,1024]{2,1,0:T(8,128)(2,1)}, bf16[8,64,1024]{2,1...) custom-call(s32[1]{0:T(128)} %bitcast.refs_0_.row_ref, ...), custom_call_target="tpu_custom_call" | custom-call | flops 3221225472 | bytes 14680064 | tf_op jit(solution)/shard_map/project_back/pallas_call | solution.py:614
  442.4 8.4 %pad_maximum_fusion = bf16[2,2304,1024]{2,1,0:T(8,128)(2,1)} fusion(bf16[1,2304,1024]{2,1,0:T(8,128)(2,1)} %maximum_bitcast_fusion.1, bf16[1,2304,1024]{2,1,0:T(8,128)(2,1)} %maximum_bitcast_fusion), kind=kLoop, calls=%fused_computation | loop fusion | flops 4718592 | bytes 18874368 | tf_op jit(solution)/shard_map/stack | solution.py:840
  456.2 5.8 collective-permute-done.42
  463.4 5.3 collective-permute-done.60
  474.1 26.4 %reduce-scatter.3.cloned.1.call-done = bf16[4,16,768]{2,1,0:T(8,128)(2,1)} async-done(((bf16[4,256,768]{2,1,0:T(8,128)(2,1)}), bf16[4,16,768]{2,1,0:T(8,128)(2,1)}) %reduce-scatter.3.cloned.1.call-update) | async-done | bytes 98320 | tf_op jit(solution)/shard_map/reduce_scatter | solution.py:871
  541.6 13.8 %collective-permute-done.51 = bf16[8,8,256]{2,0,1:T(8,128)(2,1)} collective-permute-done((bf16[8,8,256]{2,0,1:T(8,128)(2,1)}, bf16[8,8,256]{2,0,1:T(8,128)(2,1)}, u32[]{:S(2)}, u32[]{:S(2)}) %collective-permute-start.51) | collective-permute-done | bytes 32800 | tf_op jit(solution)/shard_map/ppermute | solution.py:27
  555.3 4.8 concatenate.72
  568.5 47.9 %reduce-scatter.5.cloned.1.call-done = bf16[2,144,1024]{2,1,0:T(8,128)(2,1)} async-done(((bf16[2,2304,1024]{2,1,0:T(8,128)(2,1)}), bf16[2,144,1024]{2,1,0:T(8,128)(2,1)}) %reduce-scatter.5.cloned.1.call-update) | async-done | bytes 589840 | tf_op jit(solution)/shard_map/reduce_scatter | solution.py:852
  620.3 5.0 collective-permute-done.77
  630.4 6.6 collective-permute-done.78
  644.9 10.1 %collective-permute-done.38.far = bf16[8,64,1024]{2,1,0:T(8,128)(2,1)S(1)} collective-permute-done((bf16[8,64,1024]{2,1,0:T(8,128)(2,1)}, bf16[8,64,1024]{2,1,0:T(8,128)(2,1)S(1)}, u32[]{:S(2)}, u32[]{:S(2)}) %collective-permute-start.38) | collective-permute-done | bytes 1048608 | tf_op jit(solution)/shard_map/ppermute | solution.py:27
  678.9 5.1 collective-permute-done.54
  689.9 5.5 collective-permute-done.57
  695.5 8.1 %collective-permute-done.58 = bf16[8,8,2432]{2,1,0:T(8,128)(2,1)S(1)} collective-permute-done((bf16[8,8,2432]{2,1,0:T(8,128)(2,1)S(1)}, bf16[8,8,2432]{2,1,0:T(8,128)(2,1)S(1)}, u32[]{:S(2)}, u32[]{:S(2)}) %collective-permute-start.58) | collective-permute-done | bytes 311328 | tf_op jit(solution)/shard_map/ppermute | solution.py:27
  706.7 5.0 convolution_bitcast_fusion
  715.2 6.7 all-gather.5.cloned.1.call-done
  721.9 4.9 slice_convert_fusion
  (385 shorter events, 235.9 us)
Async XLA Ops:
  7.2 493.3 %reduce-scatter.3.cloned.1.call-start = ((), (), s32[]{:S(2)}) async-start(), calls=%async_computation.2 | async-start | bytes 1671168 | tf_op jit(solution)/shard_map/reduce_scatter | solution.py:871
  36.9 50.4 %collective-permute-start.1 = (bf16[8,64,1024]{2,1,0:T(8,128)(2,1)S(1)}, bf16[8,64,1024]{2,1,0:T(8,128)(2,1)S(1)}, u32[]{:S(2)}, u32[]{:S(2)}) collective-permute-start(bf16[8,64,1024]{2,1,0:T(8,128)(2,1)S(1)} %copy-done.1), channel_id=1, source_target_pairs={{0,2},{1,3},{2,0},{3,1},{4,6},{5,7},{6,4},{7,5},{8,10},{9,11},{10,... | collective-permute-start | bytes 3145736 | tf_op jit(solution)/shard_map/ppermute | solution.py:27
  38.1 49.2 %collective-permute-start.12 = (bf16[7,64,1024]{2,1,0:T(8,128)(2,1)}, bf16[7,64,1024]{2,1,0:T(8,128)(2,1)}, u32[]{:S(2)}, u32[]{:S(2)}) collective-permute-start(bf16[7,64,1024]{2,1,0:T(8,128)(2,1)} %slice.93), channel_id=1, source_target_pairs={{0,4},{1,5},{2,6},{3,7},{4,8},{5,9},{6,10},{7,11},{8,12},{9,13},{1... | collective-permute-start | bytes 2752520 | tf_op jit(solution)/shard_map/ppermute | solution.py:32
  42.8 74.2 %collective-permute-start.9 = (bf16[256,768]{1,0:T(8,128)(2,1)}, bf16[256,768]{1,0:T(8,128)(2,1)}, u32[]{:S(2)}, u32[]{:S(2)}) collective-permute-start(bf16[256,768]{1,0:T(8,128)(2,1)} %copy.52), channel_id=1, source_target_pairs={{0,1},{1,0},{2,3},{3,2},{4,5},{5,4},{6,7},{7,6},{8,9},{9,8},{10,11... | collective-permute-start | bytes 1179656 | tf_op jit(solution)/shard_map/ppermute | solution.py:27
  42.9 74.7 %collective-permute-start.10 = (bf16[256,768]{1,0:T(8,128)(2,1)}, bf16[256,768]{1,0:T(8,128)(2,1)}, u32[]{:S(2)}, u32[]{:S(2)}) collective-permute-start(bf16[256,768]{1,0:T(8,128)(2,1)} %copy.53), channel_id=1, source_target_pairs={{0,66},{1,67},{2,64},{3,65},{4,70},{5,71},{6,68},{7,69},{8,74},{9,... | collective-permute-start | bytes 1179656 | tf_op jit(solution)/shard_map/ppermute | solution.py:27
  46.7 71.3 %collective-permute-start.11 = (bf16[256,768]{1,0:T(8,128)(2,1)}, bf16[256,768]{1,0:T(8,128)(2,1)}, u32[]{:S(2)}, u32[]{:S(2)}) collective-permute-start(bf16[256,768]{1,0:T(8,128)(2,1)} %copy.54), channel_id=1, source_target_pairs={{0,67},{1,66},{2,65},{3,64},{4,71},{5,70},{6,69},{7,68},{8,75},{9,... | collective-permute-start | bytes 1179656 | tf_op jit(solution)/shard_map/ppermute | solution.py:27
  117.6 37.6 %collective-permute-start.28 = (bf16[384,1024]{1,0:T(8,128)(2,1)S(1)}, bf16[384,1024]{1,0:T(8,128)(2,1)S(1)}, u32[]{:S(2)}, u32[]{:S(2)}) collective-permute-start(bf16[384,1024]{1,0:T(8,128)(2,1)S(1)} %slice.100), channel_id=1, source_target_pairs={{0,2},{1,3},{2,0},{3,1},{4,6},{5,7},{6,4},{7,5},{8,10},{9,11},{10,... | collective-permute-start | bytes 2359304 | tf_op jit(solution)/shard_map/ppermute | solution.py:27
  117.9 36.1 %collective-permute-start.24 = (bf16[96,4096]{1,0:T(8,128)(2,1)S(1)}, bf16[96,4096]{1,0:T(8,128)(2,1)S(1)}, u32[]{:S(2)}, u32[]{:S(2)}) collective-permute-start(bf16[96,4096]{1,0:T(8,128)(2,1)S(1)} %slice.97), channel_id=1, source_target_pairs={{0,2},{1,3},{2,0},{3,1},{4,6},{5,7},{6,4},{7,5},{8,10},{9,11},{10,... | collective-permute-start | bytes 2359304 | tf_op jit(solution)/shard_map/ppermute | solution.py:27
  119.7 36.5 %collective-permute-start.25 = (bf16[160,4096]{1,0:T(8,128)(2,1)S(1)}, bf16[160,4096]{1,0:T(8,128)(2,1)S(1)}, u32[]{:S(2)}, u32[]{:S(2)}) collective-permute-start(bf16[160,4096]{1,0:T(8,128)(2,1)S(1)} %slice.98), channel_id=1, source_target_pairs={{0,66},{1,67},{2,64},{3,65},{4,70},{5,71},{6,68},{7,69},{8,74},{9,... | collective-permute-start | bytes 3932168 | tf_op jit(solution)/shard_map/ppermute | solution.py:27
  121.0 60.9 %collective-permute-start.13 = (bf16[7,64,1024]{2,1,0:T(8,128)(2,1)}, bf16[7,64,1024]{2,1,0:T(8,128)(2,1)S(1)}, u32[]{:S(2)}, u32[]{:S(2)}) collective-permute-start(bf16[7,64,1024]{2,1,0:T(8,128)(2,1)} %collective-permute-done.12.refs_1_), channel_id=1, source_target_pairs={{0,1},{1,0},{2,3},{3,2},{4,5},{5,4},{6,7},{7,6},{8,9},{9,8},{10,11... | collective-permute-start | bytes 2752520 | tf_op jit(solution)/shard_map/ppermute | solution.py:27
  121.1 59.6 %collective-permute-start.29 = (bf16[640,1024]{1,0:T(8,128)(2,1)S(1)}, bf16[640,1024]{1,0:T(8,128)(2,1)S(1)}, u32[]{:S(2)}, u32[]{:S(2)}) collective-permute-start(bf16[640,1024]{1,0:T(8,128)(2,1)S(1)} %slice.101), channel_id=1, source_target_pairs={{0,66},{1,67},{2,64},{3,65},{4,70},{5,71},{6,68},{7,69},{8,74},{9,... | collective-permute-start | bytes 3932168 | tf_op jit(solution)/shard_map/ppermute | solution.py:27
  154.0 36.4 %collective-permute-start.15 = (bf16[7,64,1024]{2,1,0:T(8,128)(2,1)}, bf16[7,64,1024]{2,1,0:T(8,128)(2,1)S(1)}, u32[]{:S(2)}, u32[]{:S(2)}) collective-permute-start(bf16[7,64,1024]{2,1,0:T(8,128)(2,1)} %collective-permute-done.14.refs_3_), channel_id=1, source_target_pairs={{0,1},{1,0},{2,3},{3,2},{4,5},{5,4},{6,7},{7,6},{8,9},{9,8},{10,11... | collective-permute-start | bytes 2752520 | tf_op jit(solution)/shard_map/ppermute | solution.py:27
  156.2 43.4 %collective-permute-start.20 = (bf16[256,1024]{1,0:T(8,128)(2,1)S(1)}, bf16[256,1024]{1,0:T(8,128)(2,1)S(1)}, u32[]{:S(2)}, u32[]{:S(2)}) collective-permute-start(bf16[256,1024]{1,0:T(8,128)(2,1)S(1)} %copy-done.7), channel_id=1, source_target_pairs={{0,1},{1,0},{2,3},{3,2},{4,5},{5,4},{6,7},{7,6},{8,9},{9,8},{10,11... | collective-permute-start | bytes 1572872 | tf_op jit(solution)/shard_map/ppermute | solution.py:27
  180.7 70.4 %collective-permute-start.23 = (bf16[256,4096]{1,0:T(8,128)(2,1)}, bf16[256,4096]{1,0:T(8,128)(2,1)S(1)}, u32[]{:S(2)}, u32[]{:S(2)}) collective-permute-start(bf16[256,4096]{1,0:T(8,128)(2,1)} %u0.1), channel_id=1, source_target_pairs={{0,1},{1,0},{2,3},{3,2},{4,5},{5,4},{6,7},{7,6},{8,9},{9,8},{10,11... | collective-permute-start | bytes 6291464 | tf_op jit(solution)/shard_map/ppermute | solution.py:27
  181.9 70.6 %collective-permute-start.27 = (bf16[1024,1024]{1,0:T(8,128)(2,1)S(1)}, bf16[1024,1024]{1,0:T(8,128)(2,1)S(1)}, u32[]{:S(2)}, u32[]{:S(2)}) collective-permute-start(bf16[1024,1024]{1,0:T(8,128)(2,1)S(1)} %copy-done.35), channel_id=1, source_target_pairs={{0,1},{1,0},{2,3},{3,2},{4,5},{5,4},{6,7},{7,6},{8,9},{9,8},{10,11... | collective-permute-start | bytes 6291464 | tf_op jit(solution)/shard_map/ppermute | solution.py:27
  190.4 62.0 %collective-permute-start.26 = (bf16[256,4096]{1,0:T(8,128)(2,1)}, bf16[256,4096]{1,0:T(8,128)(2,1)}, u32[]{:S(2)}, u32[]{:S(2)}) collective-permute-start(bf16[256,4096]{1,0:T(8,128)(2,1)} %constant_dynamic-update-slice_fusion.u2), channel_id=1, source_target_pairs={{0,1},{1,0},{2,3},{3,2},{4,5},{5,4},{6,7},{7,6},{8,9},{9,8},{10,11... | collective-permute-start | bytes 6291464 | tf_op jit(solution)/shard_map/ppermute | solution.py:27
  190.4 62.0 %collective-permute-start.30 = (bf16[1024,1024]{1,0:T(8,128)(2,1)}, bf16[1024,1024]{1,0:T(8,128)(2,1)}, u32[]{:S(2)}, u32[]{:S(2)}) collective-permute-start(bf16[1024,1024]{1,0:T(8,128)(2,1)} %constant_dynamic-update-slice_fusion.2.d2), channel_id=1, source_target_pairs={{0,1},{1,0},{2,3},{3,2},{4,5},{5,4},{6,7},{7,6},{8,9},{9,8},{10,11... | collective-permute-start | bytes 6291464 | tf_op jit(solution)/shard_map/ppermute | solution.py:27
  289.4 77.9 %collective-permute-start.73 = (bf16[256,1024]{1,0:T(8,128)(2,1)}, bf16[256,1024]{1,0:T(8,128)(2,1)}, u32[]{:S(2)}, u32[]{:S(2)}) collective-permute-start(bf16[256,1024]{1,0:T(8,128)(2,1)} %fusion.5), channel_id=1, source_target_pairs={{0,1},{1,0},{2,3},{3,2},{4,5},{5,4},{6,7},{7,6},{8,9},{9,8},{10,11... | collective-permute-start | bytes 1572872 | tf_op jit(solution)/shard_map/ppermute | solution.py:27
  317.8 108.1 %collective-permute-start.71 = (bf16[4,256,1024]{2,1,0:T(8,128)(2,1)}, bf16[4,256,1024]{2,1,0:T(8,128)(2,1)}, u32[]{:S(2)}, u32[]{:S(2)}) collective-permute-start(bf16[4,256,1024]{2,1,0:T(8,128)(2,1)} %get-tuple-element.119), channel_id=1, source_target_pairs={{0,1},{1,0},{2,3},{3,2},{4,5},{5,4},{6,7},{7,6},{8,9},{9,8},{10,11... | collective-permute-start | bytes 6291464 | tf_op jit(solution)/shard_map/ppermute | solution.py:27
  366.9 62.4 %collective-permute-start.72 = (bf16[1024,1024]{1,0:T(8,128)(2,1)}, bf16[1024,1024]{1,0:T(8,128)(2,1)}, u32[]{:S(2)}, u32[]{:S(2)}) collective-permute-start(bf16[1024,1024]{1,0:T(8,128)(2,1)} %get-tuple-element.121), channel_id=1, source_target_pairs={{0,1},{1,0},{2,3},{3,2},{4,5},{5,4},{6,7},{7,6},{8,9},{9,8},{10,11... | collective-permute-start | bytes 6291464 | tf_op jit(solution)/shard_map/ppermute | solution.py:27
  367.2 41.0 %collective-permute-start.35 = (bf16[7,256,256]{2,1,0:T(8,128)(2,1)S(1)}, bf16[7,256,256]{2,1,0:T(8,128)(2,1)S(1)}, u32[]{:S(2)}, u32[]{:S(2)}) collective-permute-start(bf16[7,256,256]{2,1,0:T(8,128)(2,1)S(1)} %get-tuple-element.100), channel_id=1, source_target_pairs={{4,0},{5,1},{6,2},{7,3},{8,4},{9,5},{10,6},{11,7},{12,8},{13,9},{1... | collective-permute-start | bytes 2752520 | tf_op jit(solution)/shard_map/ppermute | solution.py:32
  369.2 62.9 %collective-permute-start.74 = (bf16[4,256,1024]{2,1,0:T(8,128)(2,1)}, bf16[4,256,1024]{2,1,0:T(8,128)(2,1)}, u32[]{:S(2)}, u32[]{:S(2)}) collective-permute-start(bf16[4,256,1024]{2,1,0:T(8,128)(2,1)} %get-tuple-element.124), channel_id=1, source_target_pairs={{0,1},{1,0},{2,3},{3,2},{4,5},{5,4},{6,7},{7,6},{8,9},{9,8},{10,11... | collective-permute-start | bytes 6291464 | tf_op jit(solution)/shard_map/ppermute | solution.py:27
  389.3 45.4 %collective-permute-start.75 = (bf16[1024,1024]{1,0:T(8,128)(2,1)}, bf16[1024,1024]{1,0:T(8,128)(2,1)}, u32[]{:S(2)}, u32[]{:S(2)}) collective-permute-start(bf16[1024,1024]{1,0:T(8,128)(2,1)} %get-tuple-element.126), channel_id=1, source_target_pairs={{0,1},{1,0},{2,3},{3,2},{4,5},{5,4},{6,7},{7,6},{8,9},{9,8},{10,11... | collective-permute-start | bytes 6291464 | tf_op jit(solution)/shard_map/ppermute | solution.py:27
  425.7 190.7 %reduce-scatter.5.cloned.1.call-start = ((), (), s32[]{:S(2)}) async-start(), calls=%async_computation.4 | async-start | bytes 10027008 | tf_op jit(solution)/shard_map/reduce_scatter | solution.py:852
  450.8 261.0 %all-gather.3.cloned.1.call-start = ((), (), s32[]{:S(2)}) async-start(), calls=%async_computation.3 | async-start | bytes 1671168 | tf_op jit(solution)/shard_map/all_gather | solution.py:879
  469.3 50.8 %collective-permute-start.63 = (bf16[2,8,4864]{2,1,0:T(8,128)(2,1)}, bf16[2,8,4864]{2,1,0:T(8,128)(2,1)}, u32[]{:S(2)}, u32[]{:S(2)}) collective-permute-start(bf16[2,8,4864]{2,1,0:T(8,128)(2,1)} %pad_maximum_fusion.3), channel_id=1, source_target_pairs={{0,48},{1,49},{2,50},{3,51},{4,52},{5,53},{6,54},{7,55},{8,56},{9,... | collective-permute-start | bytes 466952 | tf_op jit(solution)/shard_map/ppermute | solution.py:27
  469.3 40.4 %collective-permute-start.62 = (bf16[2,8,4864]{2,1,0:T(8,128)(2,1)}, bf16[2,8,4864]{2,1,0:T(8,128)(2,1)}, u32[]{:S(2)}, u32[]{:S(2)}) collective-permute-start(bf16[2,8,4864]{2,1,0:T(8,128)(2,1)} %pad_maximum_fusion.3), channel_id=1, source_target_pairs={{0,32},{1,33},{2,34},{3,35},{4,36},{5,37},{6,38},{7,39},{8,40},{9,... | collective-permute-start | bytes 466952 | tf_op jit(solution)/shard_map/ppermute | solution.py:27
  520.1 201.8 %all-gather.5.cloned.1.call-start = ((), (), s32[]{:S(2)}) async-start(), calls=%async_computation.5 | async-start | bytes 5013504 | tf_op jit(solution)/shard_map/all_gather | solution.py:855
  521.8 44.8 %collective-permute-start.64 = (bf16[8,8,4864]{2,1,0:T(8,128)(2,1)}, bf16[8,8,4864]{2,1,0:T(8,128)(2,1)}, u32[]{:S(2)}, u32[]{:S(2)}) collective-permute-start(bf16[8,8,4864]{2,1,0:T(8,128)(2,1)} %get-tuple-element.143), channel_id=1, source_target_pairs={{0,4},{1,5},{2,6},{3,7},{4,0},{5,1},{6,2},{7,3},{8,12},{9,13},{10,... | collective-permute-start | bytes 1867784 | tf_op jit(solution)/shard_map/ppermute | solution.py:27
  564.0 73.9 %collective-permute-start.66 = (bf16[8,8,4864]{2,1,0:T(8,128)(2,1)}, bf16[8,8,4864]{2,1,0:T(8,128)(2,1)}, u32[]{:S(2)}, u32[]{:S(2)}) collective-permute-start(bf16[8,8,4864]{2,1,0:T(8,128)(2,1)} %get-tuple-element.143), channel_id=1, source_target_pairs={{0,12},{1,13},{2,14},{3,15},{4,8},{5,9},{6,10},{7,11},{8,4},{9,5},... | collective-permute-start | bytes 1867784 | tf_op jit(solution)/shard_map/ppermute | solution.py:27
  565.6 52.7 %collective-permute-start.65 = (bf16[8,8,4864]{2,1,0:T(8,128)(2,1)}, bf16[8,8,4864]{2,1,0:T(8,128)(2,1)}, u32[]{:S(2)}, u32[]{:S(2)}) collective-permute-start(bf16[8,8,4864]{2,1,0:T(8,128)(2,1)} %get-tuple-element.143), channel_id=1, source_target_pairs={{0,8},{1,9},{2,10},{3,11},{4,12},{5,13},{6,14},{7,15},{8,0},{9,1},... | collective-permute-start | bytes 1867784 | tf_op jit(solution)/shard_map/ppermute | solution.py:27
  568.5 59.2 %collective-permute-start.37 = (bf16[8,64,1024]{2,1,0:T(8,128)(2,1)}, bf16[8,64,1024]{2,1,0:T(8,128)(2,1)}, u32[]{:S(2)}, u32[]{:S(2)}) collective-permute-start(bf16[8,64,1024]{2,1,0:T(8,128)(2,1)} %get-tuple-element.104), channel_id=1, source_target_pairs={{0,1},{1,0},{2,3},{3,2},{4,5},{5,4},{6,7},{7,6},{8,9},{9,8},{10,11... | collective-permute-start | bytes 3145736 | tf_op jit(solution)/shard_map/ppermute | solution.py:27
  (95 other events, 1520.9 us)
Sparse Core Ops, SparseCore 0:
  425.8 74.6 reduce-scatter.2
  504.0 112.3 reduce-scatter.4
  618.8 43.1 all-gather.2
  664.7 57.1 all-gather.4

commit v2 on v1

v2 whole, which is shorter than its diff:
```python
import math

import jax
import jax.numpy as jnp
from jax import lax
from jax.experimental import pallas as pl
from jax.experimental.pallas import tpu as pltpu
from jax.sharding import Mesh, PartitionSpec as P

F32 = jnp.float32
BF16 = jnp.bfloat16
HD = 64
GRID = 16
FPD = 8
PR = 64
D = 1024
FF = 4096
HC = 256
TOK = 256
PREV = 7
AXES = ("xh", "z", "y", "xl", "c")
CORE, DIRECT, OTHER, FAR = 1, 2, 66, 64
MB = 1024 * 1024


def swap(value, mask):
    return lax.ppermute(value, AXES, [(i, i ^ mask) for i in range(128)])


def shift(value, steps):
    first, last = max(0, -4 * steps), min(128, 128 - 4 * steps)
    return lax.ppermute(value, AXES, [(i, i + 4 * steps) for i in range(first, last)])


def after(value, *others):
    return lax.optimization_barrier((value,) + others)[0]


def nt(left, right):
    return lax.dot_general(left, right, (((1,), (1,)), ((), ())), preferred_element_type=F32)


def tn(left, right):
    return lax.dot_general(left, right, (((0,), (0,)), ((), ())), preferred_element_type=F32)


def nn(left, right):
    return jnp.dot(left, right, preferred_element_type=F32)


def norm(values):
    center = values - jnp.mean(values, axis=-1, keepdims=True)
    spread = jnp.mean(center * center, axis=-1, keepdims=True)
    rate = lax.rsqrt(spread + 1e-06)
    return center * rate, rate


def norm_back(normal, rate, grad):
    mean_grad = jnp.mean(grad, axis=-1, keepdims=True)
    mean_both = jnp.mean(grad * normal, axis=-1, keepdims=True)
    return rate * (grad - mean_grad - normal * mean_both)


def turn(values, cosine, sine):
    lanes = lax.broadcasted_iota(jnp.int32, values.shape, 1)
    other = jnp.where(
        lanes % HD < HD // 2, pltpu.roll(values, HC - HD // 2, 1), pltpu.roll(values, HD // 2, 1)
    )
    return values * cosine + other * sine


def params(mib):
    return pltpu.CompilerParams(
        dimension_semantics=("arbitrary",), vmem_limit_bytes=mib * MB
    )


def cost(flops, moved, exps=0):
    return pl.CostEstimate(flops=int(flops), bytes_accessed=int(moved), transcendentals=int(exps))


def whole(shape):
    return pl.BlockSpec(shape, lambda i, *_: (0,) * len(shape))


def columns(row, j):
    return pl.ds(pl.multiple_of((row ^ j) * HC, HC), HC)


def shape(dims, kind=BF16):
    return jax.ShapeDtypeStruct(dims, kind)


UB, QB, OB, DB, WIDE = 6144, 6656, 7168, 7296, 7424


def put(ref, start, at, value):
    cols = slice(start, start + value.shape[1])
    number = lax.broadcasted_iota(jnp.int32, (8, value.shape[1]), 0)
    ref[:, cols] = jnp.where(number == at, value, ref[:, cols])


def take(value, at):
    number = lax.broadcasted_iota(jnp.int32, value.shape, 0)
    return jnp.sum(jnp.where(number == at, value, 0.0), axis=0, keepdims=True)


def put_half(ref, start, value):
    cols = slice(start, start + value.shape[1])
    number = lax.broadcasted_iota(jnp.int32, (8, value.shape[1]), 0)
    both = jnp.concatenate([value, value], axis=0)
    ref[:, cols] = jnp.where(number // 4 == pl.program_id(0), both, ref[:, cols])


def unfold(ref, start, width):
    return jnp.concatenate([ref[i : i + 1, start : start + width] for i in range(8)], axis=1)


def prepare_kernel(row_ref, pos_ref, noise, ada, ab, qb, ob, ub, db, pack, silu, cp, sp, frames):
    row = row_ref[0]
    embed = noise[...].astype(F32)
    value = (embed / (1.0 + jnp.exp(-embed))).astype(BF16)
    own = jnp.where(
        row < 2,
        jnp.where(row == 0, value[:, :HC], value[:, HC : 2 * HC]),
        jnp.where(row == 2, value[:, 2 * HC : 3 * HC], value[:, 3 * HC :]),
    )
    silu[...] = own
    pack[:, UB:] = jnp.zeros((FPD, WIDE - UB), F32)
    for segment in range(6):
        cols = slice(segment * D, (segment + 1) * D)
        pack[:, cols] = nn(own, ada[:, cols])
    bias = pl.ds(pl.multiple_of(row * 1536, 512), 1536)
    pack[:, bias] = pack[:, bias] + ab[...].astype(F32)
    for i in range(2):
        at = 2 * row + i
        put(pack, UB, at, ub[:, i * 512 : (i + 1) * 512].astype(F32))
        put(pack, OB, at, ob[:, i * 128 : (i + 1) * 128].astype(F32))
        put(pack, DB, at, db[:, i * 128 : (i + 1) * 128].astype(F32))
    for i in range(3):
        chunk = 3 * row + i
        at = jnp.where(chunk < 4, chunk, chunk - 4)
        second = (chunk >= 4) & (chunk < 8)
        value = qb[:, i * HC : (i + 1) * HC].astype(F32)
        put(pack, QB, jnp.where(second, -1, at), value)
        put(pack, QB + HC, jnp.where(second, at, -1), value)

    def parts(dims):
        lane = lax.broadcasted_iota(jnp.int32, dims, 1)
        index = lane % (HD // 2)
        quarter, eighth = HD // 4, HD // 8
        in_frame = index < quarter
        in_row = (index >= quarter) & (index < quarter + eighth)
        offset = jnp.where(
            in_frame, index, jnp.where(in_row, index - quarter, index - quarter - eighth)
        ).astype(F32)
        length = jnp.where(in_frame, 1.0 * quarter, 1.0 * eighth)
        frequency = jnp.exp(-math.log(10000.0) * offset / length)
        sign = jnp.where(lane % HD < HD // 2, -1.0, 1.0)
        return in_frame, in_row, frequency, sign

    in_frame, in_row, frequency, sign = parts((TOK, HC))
    slot = lax.broadcasted_iota(jnp.int32, (TOK, HC), 0)
    patch = ((slot // PR) ^ row) * PR + slot % PR
    angle = jnp.where(in_row, patch // GRID, patch % GRID).astype(F32) * frequency
    cp[...] = jnp.where(in_frame, 0.0, jnp.cos(angle))
    sp[...] = jnp.where(in_frame, 0.0, jnp.sin(angle) * sign)
    in_frame, _, frequency, sign = parts((16, HC))
    slot = lax.broadcasted_iota(jnp.int32, (16, HC), 0)
    place = pos_ref[0] - PREV + (slot - FPD)
    for f in range(FPD):
        place = jnp.where(slot == f, pos_ref[f], place)
    angle = place.astype(F32) * frequency
    frames[:, :HC] = jnp.where(in_frame, jnp.cos(angle), 0.0)
    frames[:, HC:] = jnp.where(in_frame, jnp.sin(angle) * sign, 0.0)


def prepare(row, places, noise, ada, biases):
    return pl.pallas_call(
        prepare_kernel,
        out_shape=[
            shape((FPD, WIDE), F32),
            shape((FPD, HC)),
            shape((TOK, HC), F32),
            shape((TOK, HC), F32),
            shape((16, 2 * HC), F32),
        ],
        grid_spec=pltpu.PrefetchScalarGridSpec(
            num_scalar_prefetch=2,
            grid=(1,),
            in_specs=[whole((FPD, D)), whole((HC, 6 * D))]
            + [whole((1, b.shape[0])) for b in biases],
            out_specs=[
                whole((FPD, WIDE)),
                whole((FPD, HC)),
                whole((TOK, HC)),
                whole((TOK, HC)),
                whole((16, 2 * HC)),
            ],
        ),
        compiler_params=params(32),
        cost_estimate=cost(2 * 8 * HC * 6 * D, 4 * MB, 4 * TOK * HC),
        name="prepare",
    )(row, places, noise, ada, *[b[None] for b in biases])


def split_heads_kernel(row_ref, q, k, v, p0, p1, p2, p3):
    for j, p in enumerate((p0, p1, p2, p3)):

        @pl.when(pl.program_id(0) == j)
        def _():
            p[:, :HC] = q[...]
            p[:, HC : 2 * HC] = k[...]
            p[:, 2 * HC :] = v[...]


def split_heads(row, weight):
    return pl.pallas_call(
        split_heads_kernel,
        out_shape=[shape((HC, 3 * HC))] * 4,
        grid_spec=pltpu.PrefetchScalarGridSpec(
            num_scalar_prefetch=1,
            grid=(4,),
            in_specs=[
                pl.BlockSpec((HC, HC), lambda j, row, s=s: (0, 4 * s + (row[0] ^ j)))
                for s in range(3)
            ],
            out_specs=[whole((HC, 3 * HC))] * 4,
        ),
        compiler_params=params(16),
        cost_estimate=cost(0, 3 * MB),
        name="split_heads",
    )(row, weight, weight, weight)


def cosines(cp, sp, frames, at):
    both = frames[pl.ds(at, 1), :]
    return cp[...] + both[:, :HC], sp[...] + both[:, HC:]


def project_kernel(own, row_ref, x0, x1, x2, x3, table, mods, w0, w1, w2, w3, cp, sp, fr, *outs):
    row = row_ref[0]
    f = pl.program_id(0)
    if own:
        h_ref, q_ref, k_ref, v_ref = outs
        first, at, angle = 0, f, f
    else:
        k_ref, v_ref, h_ref = outs
        first, at, angle = HC, f + FPD - PREV, f + FPD
    x = jnp.concatenate([r[0] for r in (x0, x1, x2, x3)], axis=0).astype(F32)
    normal, _ = norm(x)
    shift_row = mods[pl.ds(at, 1), :D]
    scale_row = mods[pl.ds(at, 1), D : 2 * D]
    hidden = (normal * (1.0 + scale_row) + shift_row).astype(BF16)
    where = (0,) if own else ()
    h_ref[where + (slice(None), slice(None))] = hidden
    low, high = table[pl.ds(row, 1), QB : QB + 2 * HC], table[pl.ds(row + 4, 1), QB : QB + HC]
    total = jnp.concatenate([low, high], axis=1)[:, first:]
    for j, w in enumerate((w0, w1, w2, w3)):
        total = total + nn(h_ref[where + (slice(None), columns(row, j))], w[:, first:])
    cosine, sine = cosines(cp, sp, fr, angle)
    if own:
        q_ref[0] = (turn(total[:, :HC], cosine, sine).astype(BF16).astype(F32) * 0.125).astype(BF16)
        total = total[:, HC:]
    k_ref[0] = turn(total[:, :HC], cosine, sine).astype(BF16)
    v_ref[0] = total[:, HC:].astype(BF16)


def project(own, row, xs, table, mods, weights, tables):
    frames = xs[0].shape[0]
    x_spec = pl.BlockSpec((1, PR, D), lambda f, *_: (f, 0, 0))
    out_spec = pl.BlockSpec((1, TOK, HC), lambda f, *_: (f, 0, 0))
    out = shape((frames, TOK, HC))
    if own:
        out_specs = [pl.BlockSpec((1, TOK, D), lambda f, *_: (f, 0, 0)), out_spec, out_spec, out_spec]
        out_shape = [shape((frames, TOK, D)), out, out, out]
        scratch = []
    else:
        out_specs = [out_spec, out_spec]
        out_shape = [out, out]
        scratch = [pltpu.VMEM((TOK, D), BF16)]
    return pl.pallas_call(
        lambda *refs: project_kernel(own, *refs),
        out_shape=out_shape,
        grid_spec=pltpu.PrefetchScalarGridSpec(
            num_scalar_prefetch=1,
            grid=(frames,),
            in_specs=[x_spec] * 4
            + [whole((FPD, WIDE)), whole(mods.shape)]
            + [whole((HC, 3 * HC))] * 4
            + [whole((TOK, HC)), whole((TOK, HC)), whole((16, 2 * HC))],
            out_specs=out_specs,
            scratch_shapes=scratch,
        ),
        compiler_params=params(32),
        cost_estimate=cost(2 * frames * TOK * D * 3 * HC, frames * TOK * D * 4 + 4 * MB),
        name="project_own" if own else "project_prev",
    )(row, *xs, table, mods, *weights, *tables)


def head_lanes():
    return lax.broadcasted_iota(jnp.int32, (TOK, HC), 1) // HD


def attend_kernel(pos_ref, q, k, v, kp, vp, o0, o1, o2, o3, lse, qs, scores, acc, top, low):
    f = pl.program_id(0)
    place = pos_ref[f]
    lanes = head_lanes()
    query = q[0]
    for h in range(4):
        qs[pl.ds(h * TOK, TOK), :] = jnp.where(lanes == h, query, jnp.zeros_like(query))
    top[...] = jnp.full_like(top, -1e30)
    low[...] = jnp.zeros_like(low)
    acc[...] = jnp.zeros_like(acc)
    before = jnp.maximum(place - f, 0)
    start = jnp.maximum(f - place, 0)

    def score(keys, slot):
        for h in range(4):
            rows = pl.ds(h * TOK, TOK)
            s = nt(qs[rows, :], keys)
            scores[slot, rows, :] = s
            top[rows, :] = jnp.maximum(top[rows, :], jnp.maximum(s[:, :128], s[:, 128:]))

    def mix(values, slot):
        for h in range(4):
            rows = pl.ds(h * TOK, TOK)
            p = jnp.exp(scores[slot, rows, :] - jnp.concatenate([top[rows, :]] * 2, axis=1))
            low[rows, :] = low[rows, :] + (p[:, :128] + p[:, 128:])
            acc[rows, :] = acc[rows, :] + nn(p.astype(BF16), values)

    def run(step):
        def prev(i, _):
            at = PREV - before + i
            step(kp[at] if step is score else vp[at], i)
            return 0

        def own(g, _):
            step(k[g] if step is score else v[g], g - f + place)
            return 0

        lax.fori_loop(0, before, prev, 0)
        lax.fori_loop(start, f + 1, own, 0)

    run(score)
    for h in range(4):
        rows = pl.ds(h * TOK, TOK)
        top[rows, :] = jnp.broadcast_to(jnp.max(top[rows, :], axis=1, keepdims=True), (TOK, 128))
    run(mix)
    result = jnp.zeros((TOK, HC), F32)
    logs = jnp.zeros((TOK, 128), F32)
    narrow = lax.broadcasted_iota(jnp.int32, (TOK, 128), 1)
    for h in range(4):
        rows = pl.ds(h * TOK, TOK)
        total = jnp.sum(low[rows, :], axis=1, keepdims=True)
        result = jnp.where(lanes == h, acc[rows, :] / total, result)
        logs = jnp.where(narrow == h, top[rows, :] + jnp.log(total), logs)
    lse[0] = logs.T[:8]
    result = result.astype(BF16)
    for j, o in enumerate((o0, o1, o2, o3)):
        o[0] = result[j * PR : (j + 1) * PR]


def attend(places, q, k, v, kp, vp):
    block = pl.BlockSpec((1, TOK, HC), lambda f, *_: (f, 0, 0))
    piece = pl.BlockSpec((1, PR, HC), lambda f, *_: (f, 0, 0))
    return pl.pallas_call(
        attend_kernel,
        out_shape=[jax.ShapeDtypeStruct((FPD, PR, HC), BF16)] * 4
        + [jax.ShapeDtypeStruct((FPD, 8, TOK), F32)],
        grid_spec=pltpu.PrefetchScalarGridSpec(
            num_scalar_prefetch=1,
            grid=(FPD,),
            in_specs=[block]
            + [whole((FPD, TOK, HC))] * 2
            + [whole((PREV, TOK, HC))] * 2,
            out_specs=[piece] * 4 + [pl.BlockSpec((1, 8, TOK), lambda f, *_: (f, 0, 0))],
            scratch_shapes=[
                pltpu.VMEM((4 * TOK, HC), BF16),
                pltpu.VMEM((8, 4 * TOK, TOK), F32),
                pltpu.VMEM((4 * TOK, HC), F32),
                pltpu.VMEM((4 * TOK, 128), F32),
                pltpu.VMEM((4 * TOK, 128), F32),
            ],
        ),
        compiler_params=params(40),
        cost_estimate=cost(36 * 4 * 2 * 2 * TOK**3, 6 * MB, 36 * 4 * TOK * TOK),
        name="attend",
    )(places, q, k, v, kp, vp)


def attend_back_kernel(own, pos_ref, q, k, v, g0, g1, g2, g3, o0, o1, o2, o3, lse, *rest):
    if own:
        cp, sp, fr, before_ref, dq, dk, dv, qs, gs, ks, pl_scr, dl_scr, ds_scr, dq_acc = rest
        dk_acc, dv_acc = dk, dv
    else:
        dq, dk, dv, qs, gs, ks, pl_scr, dl_scr, ds_scr, dq_acc, dk_acc, dv_acc = rest
    f = pl.program_id(0)
    place = pos_ref[f]
    lanes = head_lanes()

    @pl.when(f == 0)
    def _():
        for ref in (dk_acc, dv_acc):
            ref[...] = jnp.zeros_like(ref)

    def prelude():
        query = q[0]
        grad = jnp.concatenate([r[0] for r in (g0, g1, g2, g3)], axis=0)
        mixed = jnp.concatenate([r[0] for r in (o0, o1, o2, o3)], axis=0)
        for h in range(4):
            rows = pl.ds(h * TOK, TOK)
            qs[rows, :] = jnp.where(lanes == h, query, jnp.zeros_like(query))
            gs[rows, :] = jnp.where(lanes == h, grad, jnp.zeros_like(grad))
        both = grad.astype(F32) * mixed.astype(F32)
        pick = (
            lax.broadcasted_iota(jnp.int32, (8, HC), 1) // HD
            == lax.broadcasted_iota(jnp.int32, (8, HC), 0)
        ).astype(F32)
        return lax.dot_general(
            pick, both, (((1,), (1,)), ((), ())),
            preferred_element_type=F32, precision=lax.Precision.HIGHEST,
        )

    def step(delta, logs, at):
        keys, values = k[at], v[at]
        for h in range(4):
            rows = pl.ds(h * TOK, TOK)
            ks[rows, :] = jnp.where(lanes == h, keys, jnp.zeros_like(keys))
            p = jnp.exp(nt(keys, qs[rows, :]) - logs[h : h + 1])
            ds = (p * (nt(values, gs[rows, :]) - delta[h : h + 1])).astype(BF16)
            pl_scr[:, rows] = p.astype(BF16)
            dl_scr[:, rows] = ds
            ds_scr[rows, :] = ds
        dv_acc[at] = dv_acc[at] + nn(pl_scr[...], gs[...])
        dk_acc[at] = dk_acc[at] + nn(dl_scr[...], qs[...])
        dq_acc[...] = dq_acc[...] + tn(ds_scr[...], ks[...])

    def sweep(low, high):
        delta = prelude()
        logs = lse[0]
        dq_acc[...] = jnp.zeros_like(dq_acc)

        def one(at, _):
            step(delta, logs, at)
            return 0

        lax.fori_loop(low, high, one, 0)

    if own:
        sweep(jnp.maximum(f - place, 0), f + 1)
        cosine, sine = cosines(cp, sp, fr, f)
        dq[0] = turn((dq_acc[...] + before_ref[0]) * 0.125, cosine, -sine).astype(BF16)
    else:
        count = jnp.maximum(place - f, 0)

        @pl.when(count > 0)
        def _():
            sweep(PREV - count, PREV)
            dq[0] = dq_acc[...]

        @pl.when(count == 0)
        def _():
            dq[0] = jnp.zeros_like(dq_acc)

        @pl.when(f == FPD - 1)
        def _():
            dk[...] = dk_acc[...].astype(BF16)
            dv[...] = dv_acc[...].astype(BF16)


def attend_back(own, places, q, k, v, grads, mixed, lse, tables=None, before=None):
    block = pl.BlockSpec((1, TOK, HC), lambda f, *_: (f, 0, 0))
    piece = pl.BlockSpec((1, PR, HC), lambda f, *_: (f, 0, 0))
    count = FPD if own else PREV
    wide = pltpu.VMEM((4 * TOK, HC), BF16)
    tall = pltpu.VMEM((TOK, 4 * TOK), BF16)
    scratch = [wide, wide, wide, tall, tall, wide, pltpu.VMEM((TOK, HC), F32)]
    specs = []
    extra = ()
    if own:
        specs = [whole((TOK, HC)), whole((TOK, HC)), whole((16, 2 * HC)), block]
        extra = tuple(tables) + (before,)
    else:
        scratch += [pltpu.VMEM((PREV, TOK, HC), F32)] * 2
    return pl.pallas_call(
        lambda *refs: attend_back_kernel(own, *refs),
        out_shape=[shape((FPD, TOK, HC), BF16 if own else F32)]
        + [shape((count, TOK, HC), F32 if own else BF16)] * 2,
        grid_spec=pltpu.PrefetchScalarGridSpec(
            num_scalar_prefetch=1,
            grid=(FPD,),
            in_specs=[block]
            + [whole((count, TOK, HC))] * 2
            + [piece] * 8
            + [pl.BlockSpec((1, 8, TOK), lambda f, *_: (f, 0, 0))]
            + specs,
            out_specs=[block] + [whole((count, TOK, HC))] * 2,
            scratch_shapes=scratch,
        ),
        compiler_params=params(40),
        cost_estimate=cost((30 if own else 12) * 4 * 5 * 2 * TOK**3, 12 * MB, 30 * 4 * TOK * TOK),
        name="attend_back_own" if own else "attend_back_prev",
    )(places, q, k, v, *grads, *mixed, lse, *extra)


HALF = 4
RAW = HALF * PR


def flat(ref):
    return ref[...].reshape(RAW, ref.shape[-1])


def frames_of(value):
    return value.reshape(HALF, PR, value.shape[-1])


def segment(table, s):
    both = table[:, s * D : (s + 1) * D]
    return jnp.where(pl.program_id(0) == 0, both[:HALF], both[HALF:])[:, None, :]


def fold(out, start, width, row):
    @pl.when(pl.program_id(0) == 0)
    def _():
        out[:, start : start + width] = jnp.zeros((8, width), F32)

    for i in range(8):
        at = (slice(i, i + 1), slice(start, start + width))
        out[at] = out[at] + row[:, i * width : (i + 1) * width]


def mid_kernel(o0, o1, o2, o3, w0, w1, w2, w3, table, x, cot, branch, middle, hidden, down, dsum):
    total = unfold(table, OB, 128)
    for o, w in zip((o0, o1, o2, o3), (w0, w1, w2, w3)):
        total = total + nn(flat(o), w[...])
    branched = frames_of(total)
    branch[...] = branched
    mid_value = x[...].astype(F32) + segment(table, 2) * branched
    middle[...] = mid_value
    normal, _ = norm(mid_value)
    hidden[...] = (normal * (1.0 + segment(table, 4)) + segment(table, 3)).astype(BF16)
    grad = (segment(table, 5) * cot[...].astype(F32)).astype(BF16)
    down[...] = grad
    fold(dsum, 0, 128, jnp.sum(grad.astype(F32).reshape(RAW, D), axis=0, keepdims=True))


def half_spec(width):
    return pl.BlockSpec((HALF, PR, width), lambda i, *_: (i, 0, 0))


def mid(pieces, weights, table, x, cot):
    return pl.pallas_call(
        mid_kernel,
        out_shape=[
            shape((FPD, PR, D), F32),
            shape((FPD, PR, D), F32),
            shape((FPD, PR, D)),
            shape((FPD, PR, D)),
            shape((8, 128), F32),
        ],
        grid=(FPD // HALF,),
        in_specs=[half_spec(HC)] * 4
        + [whole((HC, D))] * 4
        + [whole((FPD, WIDE)), half_spec(D), half_spec(D)],
        out_specs=[half_spec(D)] * 4 + [whole((8, 128))],
        compiler_params=params(40),
        cost_estimate=cost(2 * 512 * D * D, 12 * MB),
        name="mid",
    )(*pieces, *weights, table, x, cot)


def mid_back_kernel(hg, middle, branch, cot, table, w0, w1, w2, w3, mg, bg, a0, a1, a2, a3, sums):
    grad = hg[...]
    normal, rate = norm(middle[...])
    put_half(sums, D, jnp.sum(grad, axis=1))
    put_half(sums, 2 * D, jnp.sum(grad * normal, axis=1))
    total = cot[...].astype(F32) + norm_back(normal, rate, grad * (1.0 + segment(table, 4)))
    mg[...] = total
    put_half(sums, 0, jnp.sum(total * branch[...], axis=1))
    low = (segment(table, 2) * total).astype(BF16)
    bg[...] = low
    low = low.reshape(RAW, D)
    fold(sums, 3 * D, 128, jnp.sum(low.astype(F32), axis=0, keepdims=True))
    for a, w in zip((a0, a1, a2, a3), (w0, w1, w2, w3)):
        a[...] = frames_of(nt(low, w[...]).astype(BF16))


def mid_back(hg, middle, branch, cot, table, weights):
    return pl.pallas_call(
        mid_back_kernel,
        out_shape=[shape((FPD, PR, D), F32), shape((FPD, PR, D))]
        + [shape((FPD, PR, HC))] * 4
        + [shape((8, 3 * D + 128), F32)],
        grid=(FPD // HALF,),
        in_specs=[half_spec(D)] * 4
        + [whole((FPD, WIDE))]
        + [whole((HC, D))] * 4,
        out_specs=[half_spec(D)] * 2 + [half_spec(HC)] * 4 + [whole((8, 3 * D + 128))],
        compiler_params=params(40),
        cost_estimate=cost(2 * 512 * D * D, 12 * MB),
        name="mid_back",
    )(hg, middle, branch, cot, table, *weights)


NB = 512
STEPS = FF // NB
PER = D // NB
TOKENS = FPD * PR


def block_of(t):
    phase = t // PER
    return ((phase % 2) * 2) ^ (phase // 2)


def up_column(t, row):
    return (row ^ block_of(t)) * PER + t % PER


def down_row(t):
    return block_of(t) * PER + t % PER


def down_spec(j):
    phase = (0, 2, 1, 3)[j]
    return pl.BlockSpec((NB, D), lambda t, row: (jnp.clip(t - phase * PER, 0, PER - 1), 0))


def pick_down(d0, d1, d2, d3):
    phase = pl.program_id(0) // PER
    return jnp.where(
        phase < 2,
        jnp.where(phase == 0, d0[...], d2[...]),
        jnp.where(phase == 2, d1[...], d3[...]),
    )


def feed_kernel(row_ref, h2, dg, u0, u1, u2, u3, table, d0, d1, d2, d3, act, upg, hg, usum):
    row = row_ref[0]
    ups = (u0, u1, u2, u3)
    down = pick_down(d0, d1, d2, d3)
    at = pl.ds(up_column(pl.program_id(0), row), 1)
    u = table[at, UB : UB + NB]
    for j, w in enumerate(ups):
        u = u + nn(h2[:, columns(row, j)], w[...])
    rate = math.sqrt(2.0 / math.pi)
    square = u * u
    half = 0.5 + 0.5 * jnp.tanh(u * (rate + (rate * 0.044715) * square))
    active = u * half
    act[...] = active.astype(BF16)
    slope = half + active * (1.0 - half) * (2.0 * rate + (6.0 * rate * 0.044715) * square)
    grad = (nt(dg[...], down) * slope).astype(BF16)
    upg[...] = grad
    put(usum, 0, up_column(pl.program_id(0), row), jnp.sum(grad.astype(F32), axis=0, keepdims=True))

    @pl.when(pl.program_id(0) == 0)
    def _():
        hg[...] = jnp.zeros_like(hg)

    for j, w in enumerate(ups):
        hg[:, columns(row, j)] = hg[:, columns(row, j)] + nt(grad, w[...])


def feed(row, h2, dg, ups, table, downs):
    tok = whole((TOKENS, D))
    block = pl.BlockSpec((TOKENS, NB), lambda t, row: (0, t))
    return pl.pallas_call(
        feed_kernel,
        out_shape=[
            shape((TOKENS, FF)),
            shape((TOKENS, FF)),
            shape((TOKENS, D), F32),
            shape((8, NB), F32),
        ],
        grid_spec=pltpu.PrefetchScalarGridSpec(
            num_scalar_prefetch=1,
            grid=(STEPS,),
            in_specs=[tok, tok]
            + [pl.BlockSpec((HC, NB), lambda t, row: (0, up_column(t, row[0])))] * 4
            + [whole((FPD, WIDE))]
            + [down_spec(j) for j in range(4)],
            out_specs=[block, block, tok, whole((8, NB))],
        ),
        compiler_params=params(44),
        cost_estimate=cost(3 * 2 * TOKENS * D * FF, 30 * MB, TOKENS * FF),
        name="feed",
    )(row, h2, dg, *ups, table, *downs)


def feed_back_kernel(
    row_ref, h2, dg, act, upg, d0, d1, d2, d3, table, middle, cot,
    uk, us, dk, ds, out, gate, dn,
):
    row = row_ref[0]
    t = pl.program_id(0)
    down = pick_down(d0, d1, d2, d3)
    active = act[...]

    @pl.when(t == 0)
    def _():
        dn[...] = jnp.zeros_like(dn)

    dn[...] = dn[...] + nn(active, down)
    part = tn(active, dg[...]).astype(BF16)

    @pl.when(t < STEPS // 2)
    def _():
        dk[0] = part

    @pl.when(t >= STEPS // 2)
    def _():
        ds[0] = part

    grad = upg[...]
    for j, ref in enumerate((uk, us, uk, us)):
        ref[j // 2, 0] = tn(h2[:, columns(row, j)], grad).astype(BF16)

    @pl.when(t == STEPS - 1)
    def _():
        bias = unfold(table, DB, 128)
        for f in range(FPD):
            rows = slice(f * PR, (f + 1) * PR)
            value = dn[rows, :] + bias
            out[f] = (middle[f] + table[f : f + 1, 5 * D : 6 * D] * value).astype(BF16)
            gate[f : f + 1, :] = jnp.sum(cot[f].astype(F32) * value, axis=0, keepdims=True)


def feed_back(row, h2, dg, act, upg, downs, table, middle, cot):
    tok = whole((TOKENS, D))
    full = whole((FPD, PR, D))
    block = pl.BlockSpec((TOKENS, NB), lambda t, row: (0, t))
    up_out = pl.BlockSpec(
        (2, 1, HC, NB),
        lambda t, row: (0, up_column(t, row[0]) // PER, 0, up_column(t, row[0]) % PER),
    )

    def down_out(first):
        def index(t, row):
            at = jnp.clip(t - first, 0, STEPS // 2 - 1)
            return (at // PER, at % PER, 0)

        return pl.BlockSpec((1, NB, D), index)

    return pl.pallas_call(
        feed_back_kernel,
        out_shape=[shape((2, 4, HC, D))] * 2
        + [shape((2, D, D))] * 2
        + [shape((FPD, PR, D)), shape((8, D), F32)],
        grid_spec=pltpu.PrefetchScalarGridSpec(
            num_scalar_prefetch=1,
            grid=(STEPS,),
            in_specs=[tok, tok, block, block]
            + [down_spec(j) for j in range(4)]
            + [whole((FPD, WIDE)), full, full],
            out_specs=[up_out, up_out, down_out(0), down_out(STEPS // 2), full, whole((8, D))],
            scratch_shapes=[pltpu.VMEM((TOKENS, D), F32)],
        ),
        compiler_params=params(48),
        cost_estimate=cost(3 * 2 * TOKENS * D * FF, 40 * MB),
        name="feed_back",
    )(row, h2, dg, act, upg, *downs, table, middle, cot)


def out_weight_kernel(t0, t1, t2, t3, bg, keep, send):
    grad = bg[...].reshape(TOKENS, D)
    for j, t in enumerate((t0, t1, t2, t3)):
        ref = (keep, send)[j % 2]
        ref[j // 2] = tn(t[...].reshape(TOKENS, HC), grad).astype(BF16)


def out_weight_grad(pieces, bg):
    return pl.pallas_call(
        out_weight_kernel,
        out_shape=[shape((2, HC, D))] * 2,
        grid=(1,),
        in_specs=[whole((FPD, PR, HC))] * 4 + [whole((FPD, PR, D))],
        out_specs=[whole((2, HC, D))] * 2,
        compiler_params=params(24),
        cost_estimate=cost(2 * TOKENS * D * D, 4 * MB),
        name="out_weight_grad",
    )(*pieces, bg)


ROWS = 2 * D + HC
BLOCKS = ROWS // HC


def core_sum_kernel(ua, ub, da, db, oa, ob, out):
    i = pl.program_id(1)
    for low, high, a, b in ((0, 4, ua, ub), (4, 8, da, db), (8, 9, oa, ob)):

        @pl.when((i >= low) & (i < high))
        def _():
            out[0] = (a[0].astype(F32) + b[0].astype(F32)).astype(BF16)


def core_sum(up, down, out):
    def spec(low, count):
        return pl.BlockSpec((1, HC, D), lambda j, i: (j, jnp.clip(i - low, 0, count - 1), 0))

    up = [u.reshape(2, D, D) for u in up]
    return pl.pallas_call(
        core_sum_kernel,
        out_shape=shape((2, ROWS, D)),
        grid=(2, BLOCKS),
        in_specs=[spec(0, 4)] * 2 + [spec(4, 4)] * 2 + [spec(8, 1)] * 2,
        out_specs=pl.BlockSpec((1, HC, D), lambda j, i: (j, i, 0)),
        compiler_params=pltpu.CompilerParams(
            dimension_semantics=("arbitrary", "arbitrary"), vmem_limit_bytes=24 * MB
        ),
        cost_estimate=cost(2 * ROWS * D, 28 * MB),
        name="core_sum",
    )(*up, *down, *out)


def unpack_kernel(total, up, down, out):
    i = pl.program_id(0)
    value = total[...].astype(F32)
    for low, high, ref in ((0, 4, up), (4, 8, down), (8, 9, out)):

        @pl.when((i >= low) & (i < high))
        def _():
            ref[...] = value


def unpack(total):
    return pl.pallas_call(
        unpack_kernel,
        out_shape=[shape((HC, FF), F32), shape((D, D), F32), shape((HC, D), F32)],
        grid=(BLOCKS,),
        in_specs=[pl.BlockSpec((HC, D), lambda i: (i, 0))],
        out_specs=[
            pl.BlockSpec((HC, D), lambda i: (0, jnp.clip(i, 0, 3))),
            pl.BlockSpec((HC, D), lambda i: (jnp.clip(i - 4, 0, 3), 0)),
            pl.BlockSpec((HC, D), lambda i: (0, 0)),
        ],
        compiler_params=params(24),
        cost_estimate=cost(0, 14 * MB),
        name="unpack",
    )(total)


def project_back_kernel(row_ref, dq, dk, dv, rk, rv, w0, w1, w2, w3, cp, sp, fr, dp, h0, h2, hs, bsum):
    row = row_ref[0]
    f = pl.program_id(0)
    later = (f > 0).astype(F32)
    keys = dk[0] + later * rk[0].astype(F32)
    values = dv[0] + later * rv[0].astype(F32)
    cosine, sine = cosines(cp, sp, fr, f)
    dp[0, :, :HC] = dq[0]
    dp[0, :, HC : 2 * HC] = turn(keys, cosine, -sine).astype(BF16)
    dp[0, :, 2 * HC :] = values.astype(BF16)
    grad = dp[0]
    sums = jnp.sum(grad.astype(F32), axis=0, keepdims=True)

    @pl.when(f == 0)
    def _():
        bsum[...] = jnp.zeros_like(bsum)

    number = lax.broadcasted_iota(jnp.int32, (8, 2 * HC), 0)
    bsum[...] = bsum[...] + jnp.where(number == row, sums[:, : 2 * HC], 0.0)
    bsum[:, :HC] = bsum[:, :HC] + jnp.where(number[:, :HC] == row + 4, sums[:, 2 * HC :], 0.0)
    for j, w in enumerate((w0, w1, w2, w3)):
        part = nt(grad, w[...]).astype(BF16)
        at = (0, slice(None), columns(row, j))
        h0[at] = part[:PR]
        hs[(0,) + at] = part[PR : 2 * PR]
        h2[at] = part[2 * PR : 3 * PR]
        hs[(1,) + at] = part[3 * PR :]


def project_back(row, dq, dk, dv, rk, rv, weights, tables):
    block = pl.BlockSpec((1, TOK, HC), lambda f, *_: (f, 0, 0))
    late = pl.BlockSpec((1, TOK, HC), lambda f, *_: (jnp.maximum(f - 1, 0), 0, 0))
    piece = pl.BlockSpec((1, PR, D), lambda f, *_: (f, 0, 0))
    return pl.pallas_call(
        project_back_kernel,
        out_shape=[
            shape((FPD, TOK, 3 * HC)),
            shape((FPD, PR, D)),
            shape((FPD, PR, D)),
            shape((2, FPD, PR, D)),
            shape((8, 2 * HC), F32),
        ],
        grid_spec=pltpu.PrefetchScalarGridSpec(
            num_scalar_prefetch=1,
            grid=(FPD,),
            in_specs=[block] * 3
            + [late] * 2
            + [whole((HC, 3 * HC))] * 4
            + [whole((TOK, HC)), whole((TOK, HC)), whole((16, 2 * HC))],
            out_specs=[
                pl.BlockSpec((1, TOK, 3 * HC), lambda f, *_: (f, 0, 0)),
                piece,
                piece,
                pl.BlockSpec((2, 1, PR, D), lambda f, *_: (0, f, 0, 0)),
                whole((8, 2 * HC)),
            ],
        ),
        compiler_params=params(32),
        cost_estimate=cost(2 * FPD * TOK * D * 3 * HC, 14 * MB),
        name="project_back",
    )(row, dq, dk, dv, rk, rv, *weights, *tables)


def weight_kernel(row_ref, h, dp, w):
    w[0] = tn(h[...], dp[...]).astype(BF16)


def project_weight(row, hidden, dproj):
    tokens = FPD * TOK
    return pl.pallas_call(
        weight_kernel,
        out_shape=shape((4, HC, 3 * HC)),
        grid_spec=pltpu.PrefetchScalarGridSpec(
            num_scalar_prefetch=1,
            grid=(4,),
            in_specs=[
                pl.BlockSpec((tokens, HC), lambda j, row: (0, row[0] ^ j)),
                whole((tokens, 3 * HC)),
            ],
            out_specs=pl.BlockSpec((1, HC, 3 * HC), lambda j, row: (j, 0, 0)),
        ),
        compiler_params=params(32),
        cost_estimate=cost(2 * tokens * D * 3 * HC, 9 * MB),
        name="project_weight",
    )(row, hidden.reshape(tokens, D), dproj.reshape(tokens, 3 * HC))


def input_back_kernel(x, h0, near, far, table, mg, bsum, out, sums):
    grad = h0[...].astype(F32) + near[0].astype(F32) + far[...].astype(F32)
    normal, rate = norm(x[...].astype(F32))
    put_half(sums, 0, jnp.sum(grad, axis=1))
    put_half(sums, D, jnp.sum(grad * normal, axis=1))
    sums[:, 2 * D :] = bsum[...]
    out[...] = mg[...] + norm_back(normal, rate, grad * (1.0 + segment(table, 1)))


LATE = 2 * D + 2 * HC
EARLY = 4 * D + NB + 256


def input_back(x, h0, near, far, table, mg, bsum):
    return pl.pallas_call(
        input_back_kernel,
        out_shape=[shape((FPD, PR, D), F32), shape((8, LATE), F32)],
        grid=(FPD // HALF,),
        in_specs=[half_spec(D)] * 2
        + [pl.BlockSpec((1, HALF, PR, D), lambda i: (0, i, 0, 0))]
        + [half_spec(D), whole((FPD, WIDE)), half_spec(D), whole((8, 2 * HC))],
        out_specs=[half_spec(D), whole((8, LATE))],
        compiler_params=params(32),
        cost_estimate=cost(20 * 512 * D, 10 * MB),
        name="input_back",
    )(x, h0, near, far, table, mg, bsum)


def early_kernel(m, g, u, d, out):
    out[:, : 3 * D] = m[:, : 3 * D]
    out[:, 3 * D : 4 * D] = g[...]
    out[:, 4 * D : 4 * D + NB] = u[...]
    out[:, 4 * D + NB : 4 * D + NB + 128] = d[...]
    out[:, 4 * D + NB + 128 :] = m[:, 3 * D :]


def early_sums(sums, gate, usum, dsum):
    return pl.pallas_call(
        early_kernel,
        out_shape=shape((8, EARLY), F32),
        grid=(1,),
        in_specs=[whole(a.shape) for a in (sums, gate, usum, dsum)],
        out_specs=whole((8, EARLY)),
        cost_estimate=cost(0, MB),
        name="early_sums",
    )(sums, gate, usum, dsum)


def final_kernel(row_ref, *refs):
    row = row_ref[0]
    late, early, silu = refs[:4], refs[4:8], refs[8:12]
    ada, ab, qb, ob, ub, db, asum = refs[12:]

    def rows(ref, cols):
        value = ref[:, :, cols].astype(F32)
        return value.reshape(64, value.shape[-1])

    left = [rows(s, slice(None)).astype(BF16) for s in silu]
    for segment in range(6):
        source, start = (late, segment) if segment < 2 else (early, segment - 2)
        cols = slice(start * D, (start + 1) * D)
        product, total = 0.0, 0.0
        for s, ref in zip(left, source):
            right = rows(ref, cols)
            total = total + jnp.sum(right, axis=0, keepdims=True)
            product = product + tn(s, right.astype(BF16))
        at = segment * D
        ada[:, at : at + D] = product
        asum[0:1, at : at + D] = total

    def bias(source, start, stop):
        return sum(
            jnp.sum(ref[:, :, start:stop].astype(F32), axis=0) for ref in source
        )

    ab[...] = asum[0:1, pl.ds(pl.multiple_of(row * 1536, 512), 1536)]
    folded = bias(late, 2 * D, LATE)
    for i in range(3):
        chunk = 3 * row + i
        at = jnp.where(chunk < 4, chunk, chunk - 4)
        second = (chunk >= 4) & (chunk < 8)
        value = jnp.where(second, folded[:, HC:], folded[:, :HC])
        qb[:, i * HC : (i + 1) * HC] = take(value, at)
    folded = bias(early, 4 * D, EARLY)
    for i in range(2):
        at = 2 * row + i
        ub[:, i * NB : (i + 1) * NB] = take(folded[:, :NB], at)
        db[:, i * 128 : (i + 1) * 128] = take(folded[:, NB : NB + 128], at)
        ob[:, i * 128 : (i + 1) * 128] = take(folded[:, NB + 128 :], at)


def final_sums(row, late, early, silu):
    sizes = (1536, 768, 256, 1024, 256)
    return pl.pallas_call(
        final_kernel,
        out_shape=[shape((HC, 6 * D), F32)] + [shape((1, n), F32) for n in sizes],
        grid_spec=pltpu.PrefetchScalarGridSpec(
            num_scalar_prefetch=1,
            grid=(1,),
            in_specs=[whole((8, 8, LATE))] * 4
            + [whole((8, 8, EARLY))] * 4
            + [whole((8, 8, HC))] * 4,
            out_specs=[whole((HC, 6 * D))] + [whole((1, n)) for n in sizes],
            scratch_shapes=[pltpu.VMEM((8, 6 * D), F32)],
        ),
        compiler_params=params(44),
        cost_estimate=cost(2 * 256 * HC * 6 * D, 10 * MB),
        name="final_sums",
    )(row, *late, *early, *silu)


def row_sum(value):
    value = value + swap(value, CORE)
    return value + swap(value, DIRECT)


def row_pieces(value):
    return [value, swap(value, CORE), swap(value, DIRECT), swap(value, DIRECT ^ CORE)]


def seq_gather(value):
    value = jnp.stack([value, swap(value, FAR)])
    value = jnp.concatenate([value] + [swap(value, m) for m in (16, 32, 48)])
    return [value] + [swap(value, m) for m in (4, 8, 12)]


def by_row(pieces, row):
    a, b, c, d = pieces
    odd, high = row % 2 == 1, row >= 2
    a, b = jnp.where(odd, b, a), jnp.where(odd, a, b)
    c, d = jnp.where(odd, d, c), jnp.where(odd, c, d)
    return jnp.stack(
        [
            jnp.where(high, c, a),
            jnp.where(high, d, b),
            jnp.where(high, a, c),
            jnp.where(high, b, d),
        ]
    )


def turn_heads(pieces):
    return [pieces[0]] + [
        swap(piece, mask) for piece, mask in zip(pieces[1:], (CORE, DIRECT, DIRECT ^ CORE))
    ]


def per_device(
    activations,
    noise_embed,
    frame_position,
    cotangent,
    ada_weight,
    ada_bias,
    qkv_weight,
    qkv_bias,
    out_weight,
    out_bias,
    up_weight,
    up_bias,
    down_weight,
    down_bias,
):
    row = lax.axis_index(("xl", "c")).astype(jnp.int32)
    row_arg = row.reshape(1)

    x0 = activations
    x2 = swap(x0, DIRECT)
    x1 = swap(x0, CORE)
    x3 = swap(x2, CORE)
    p0 = after(shift(activations[1:], 1), x2)
    p2 = swap(p0, DIRECT)
    p1 = swap(p0, CORE)
    p3 = swap(p2, CORE)

    biases = (ada_bias, qkv_bias, out_bias, up_bias, down_bias)
    part, silu_own, *tables = prepare(row_arg, frame_position, noise_embed, ada_weight, biases)
    table = row_sum(part)
    before_mods = shift(table[:, : 2 * D], 1)
    heads = split_heads(row_arg, qkv_weight)
    qkv_pieces = [heads[0], swap(heads[1], CORE), swap(heads[2], OTHER), swap(heads[3], OTHER ^ CORE)]

    out_own = after(out_weight, qkv_pieces[3])
    up_own = after(up_weight, qkv_pieces[3])
    down_own = after(down_weight, p2)
    outs2 = swap(out_own, OTHER)
    ups2 = swap(up_own, OTHER)
    downs2 = swap(down_own, DIRECT)
    outs = [out_weight, swap(out_own, CORE), outs2, swap(outs2, CORE)]
    ups = [up_weight, swap(up_own, CORE), ups2, swap(ups2, CORE)]
    downs = [down_weight, swap(down_own, CORE), downs2, swap(downs2, CORE)]

    hidden1, q, k, v = project(True, row_arg, (x0, x1, x2, x3), table, table, qkv_pieces, tables)
    kp, vp = project(
        False, row_arg, (p0, p1, p2, p3), table, before_mods, qkv_pieces, tables
    )
    *mixed, lse = attend(frame_position, q, k, v, kp, vp)
    turned = turn_heads(mixed)
    branch, middle, hidden2, down_grad, dsum = mid(turned, outs, table, x0, cotangent)
    h2 = hidden2.reshape(TOKENS, D)
    dg = down_grad.reshape(TOKENS, D)
    act, upg, hg, usum = feed(row_arg, h2, dg, ups, table, downs)
    mg, bg, *ag, sums = mid_back(hg.reshape(FPD, PR, D), middle, branch, cotangent, table, outs)
    back = turn_heads(ag)

    uk, us, dk_part, ds_part, layer_output, gate = feed_back(
        row_arg, h2, dg, act, upg, downs, table, middle, cotangent
    )
    ok, os = out_weight_grad(turned, bg)
    back = list(lax.optimization_barrier(tuple(back) + (gate, ok))[:4])
    dq_before, dkp, dvp = attend_back(False, frame_position, q, kp, vp, back, mixed, lse)
    rk, rv = shift(dkp, -1), shift(dvp, -1)
    packed = core_sum(
        (uk, swap(us, CORE)), (dk_part, swap(ds_part, CORE)), (ok, swap(os, CORE))
    )
    dq_before = after(dq_before, packed)
    scattered = lax.psum_scatter(packed, ("z", "y"), scatter_dimension=1, tiled=True)
    dq, dk, dv = attend_back(
        True, frame_position, q, k, v, back, mixed, lse, tables, dq_before
    )
    share = scattered[0].astype(F32) + swap(scattered[1], DIRECT).astype(F32)
    share = (share + swap(share.astype(BF16), FAR).astype(F32)).astype(BF16)
    totals = lax.all_gather(share, ("z", "y"), axis=0, tiled=True)
    up_total, down_total, out_total = unpack(totals)

    early = row_sum(early_sums(sums, gate, usum, dsum))
    early_all = seq_gather(early.astype(BF16))
    silu_all = seq_gather(silu_own)

    dproj, h0, h2_part, send, bsum = project_back(row_arg, dq, dk, dv, rk, rv, qkv_pieces, tables)
    near = swap(send, CORE)
    far = swap((h2_part.astype(F32) + near[1].astype(F32)).astype(BF16), DIRECT)
    qkv_parts = project_weight(row_arg, hidden1, dproj)
    input_grad, late = input_back(x0, h0, near, far, table, mg, bsum)
    late = row_sum(late)
    late_all = seq_gather(late.astype(BF16))

    qkv_parts = lax.psum_scatter(qkv_parts, ("z", "y"), scatter_dimension=1, tiled=True)
    qkv_parts = (qkv_parts.astype(F32) + swap(qkv_parts, FAR).astype(F32)).astype(BF16)
    qkv_turned = turn_heads([qkv_parts[j] for j in range(4)])
    qkv_share = by_row(qkv_turned, row).reshape(4, 16, 3, HC).transpose(1, 2, 0, 3)
    qkv_total = lax.all_gather(
        qkv_share.reshape(16, 3 * D), ("z", "y"), axis=0, tiled=True
    ).astype(F32)

    ada_total, *bias_sums = final_sums(row_arg, late_all, early_all, silu_all)
    ada_sum, qkv_sum, out_sum, up_sum, down_sum = [b[0] for b in bias_sums]
    mod_own = jnp.concatenate([late[:, : 2 * D], early[:, : 4 * D]], axis=1).astype(BF16)
    silu_grad = nt(mod_own, ada_weight)
    silu_grad = by_row(row_pieces(silu_grad), row).transpose(1, 0, 2).reshape(FPD, D)
    embed = noise_embed.astype(F32)
    sigma = jax.nn.sigmoid(embed)
    embed_grad = silu_grad * (sigma * (1.0 + embed * (1.0 - sigma)))

    return (
        layer_output,
        input_grad,
        embed_grad,
        ada_total,
        ada_sum,
        qkv_total,
        qkv_sum,
        out_total,
        out_sum,
        up_total,
        up_sum,
        down_total,
        down_sum,
    )


def solution(mesh):
    fine = Mesh(mesh.devices.reshape(2, 4, 4, 2, 2), AXES)
    seq, row = ("xh", "z", "y"), ("xl", "c")
    token, weight, vector = P(seq, row, None), P(row, None), P(row)
    in_specs = (token, P(seq, None), P(seq), token) + (weight, vector) * 5
    out_specs = (token, token, P(seq, None)) + (weight, vector) * 5
    return jax.shard_map(
        per_device, mesh=fine, in_specs=in_specs, out_specs=out_specs, check_vma=False
    )
```

time: 747 us -> 736 us (0.985)
  waiting for transfers between devices: 329 us -> 405 us
  other arithmetic: 61.3 us -> 14.4 us
  local copies, waits for them, and re-layouts: 72.3 us -> 35.1 us
  Pallas kernels: 169 us -> 201 us
  starting transfers between devices: 74.5 us -> 57.8 us
  matrix products: 17.2 us -> 0.91 us
    reduce_scatter x1, waiting for transfers between devices: 26.4 us -> 70.6 us  [per_device(): lax.psum_scatter(qkv_parts, ('z', 'y'), scatter_dimension=1, tiled=True)]
    ppermute x74 -> x65, waiting for transfers between devices: 174 us -> 206 us  [swap(): return lax.ppermute(value, AXES, [(i, i ^ mask) for i in range(128)])]
    pallas_call x10 -> x18, Pallas kernels: 139 us -> 171 us  [the longest x2 43.7 us: attend_back(): pl.pallas_call(lambda *refs: attend_back_kernel(own, *refs), out_shape=[s...]
    reduce_scatter x1, waiting for transfers between devices: 47.9 us -> 72.6 us  [per_device(): lax.psum_scatter(packed, ('z', 'y'), scatter_dimension=1, tiled=True)]
    convert_element_type x13 -> x2, other arithmetic: 27.2 us -> 2.57 us  [the longest x1 1.65 us: per_device(): far = swap((h2_part.astype(F32) + near[1].astype(F32)).astype(BF16), DIRECT)]
    ppermute x5 -> x4, waiting for transfers between devices: 74.1 us -> 55.1 us  [shift(): lax.ppermute(value, AXES, [(i, i + 4 * steps) for i in range(first, last)])]
    dot_general x7 -> x0, matrix products: 14.4 us -> none  [the longest x5 10.5 us: tn(): lax.dot_general(left, right, (((0,), (0,)), ((), ())), preferred_element_...]
    another operation x3 -> x0, other arithmetic: 13.3 us -> none  [per_device(): jnp.stack([jnp.concatenate([core_sum(up_parts, j).reshape(D, D), core_sum...]
  transfers between devices with their start and end apart: 83 -> 73, of which waited for: 35 -> 38; matrix products, arithmetic and copies ran while one was open for 16% -> 3% of each run, Pallas kernels for 19% -> 17%
where the time goes in v2:
time: 736 us; the launch traced here: 729 us
  waiting for transfers between devices  405 us (55%)
  Pallas kernels  201 us (27%)
  starting transfers between devices  57.8 us (8%)
  local copies, waits for them, and re-layouts  35.1 us (5%)
  between operations  15.3 us (2%)
  other arithmetic  14.4 us (2%)
    ppermute x65, waiting for transfers between devices, swap(): return lax.ppermute(value, AXES, [(i, i ^ mask) for i in range(128)])  206 us
    reduce_scatter x1, waiting for transfers between devices, per_device(): lax.psum_scatter(packed, ('z', 'y'), scatter_dimension=1, tiled=True)  72.6 us
    reduce_scatter x1, waiting for transfers between devices, per_device(): lax.psum_scatter(qkv_parts, ('z', 'y'), scatter_dimension=1, tiled=True)  70.6 us
    ppermute x4, waiting for transfers between devices, shift(): lax.ppermute(value, AXES, [(i, i + 4 * steps) for i in range(first, last)])  55.1 us
    ppermute x65, starting transfers between devices, swap(): return lax.ppermute(value, AXES, [(i, i ^ mask) for i in range(128)])  48.1 us
    pallas_call x2, Pallas kernels, attend_back(): pl.pallas_call(lambda *refs: attend_back_kernel(own, *refs), out_shape=[s...  43.7 us
    pallas_call x1, Pallas kernels, attend(): pl.pallas_call(attend_kernel, out_shape=[jax.ShapeDtypeStruct((FPD, PR, H...  29.8 us
    pallas_call x1, Pallas kernels, feed_back(): pl.pallas_call(feed_back_kernel, out_shape=[shape((2, 4, HC, D))] * 2 + [...  28.7 us
  transfers between devices with their start and end apart: 73, of which 38 were waited for; matrix products, arithmetic and copies ran while one was open for 3% of the time, Pallas kernels for 17%

profile of v2, /device:TPU:6, one launch (start us, length us, event | category | flops | bytes accessed | tf_op | source)
XLA Modules:
  0.0 728.8 jit_solution(17277129111638403352)
XLA Ops:
  12.9 45.1 %collective-permute-done.8.refs_1_ = bf16[7,64,1024]{2,1,0:T(8,128)(2,1)} collective-permute-done((bf16[7,64,1024]{2,1,0:T(8,128)(2,1)S(1)}, bf16[7,64,1024]{2,1,0:T(8,128)(2,1)}, u32[]{:S(2)}, u32[]{:S(2)}) %collective-permute-start.8) | collective-permute-done | bytes 917536 | tf_op jit(solution)/shard_map/ppermute | solution.py:32
  59.8 11.4 %collective-permute-done.7.refs_10_.w3 = bf16[256,768]{1,0:T(8,128)(2,1)S(1)} collective-permute-done((bf16[256,768]{1,0:T(8,128)(2,1)S(1)}, bf16[256,768]{1,0:T(8,128)(2,1)S(1)}, u32[]{:S(2)}, u32[]{:S(2)}) %collective-permute-start.7) | collective-permute-done | bytes 393248 | tf_op jit(solution)/shard_map/ppermute | solution.py:27
  71.2 8.4 %collective-permute-done.10.refs_3_ = bf16[7,64,1024]{2,1,0:T(8,128)(2,1)} collective-permute-done((bf16[7,64,1024]{2,1,0:T(8,128)(2,1)}, bf16[7,64,1024]{2,1,0:T(8,128)(2,1)}, u32[]{:S(2)}, u32[]{:S(2)}) %collective-permute-start.10) | collective-permute-done | bytes 917536 | tf_op jit(solution)/shard_map/ppermute | solution.py:27
  85.9 44.6 %collective-permute-done.4 = f32[8,7424]{1,0:T(8,128)S(1)} collective-permute-done((f32[8,7424]{1,0:T(8,128)S(1)}, f32[8,7424]{1,0:T(8,128)S(1)}, u32[]{:S(2)}, u32[]{:S(2)}) %collective-permute-start.4) | collective-permute-done | bytes 237600 | tf_op jit(solution)/shard_map/ppermute | solution.py:27
  132.4 10.0 %collective-permute-done.12.refs_6_ = f32[8,2048]{1,0:T(8,128)S(1)} collective-permute-done((f32[8,2048]{1,0:T(8,128)S(1)}, f32[8,2048]{1,0:T(8,128)S(1)}, u32[]{:S(2)}, u32[]{:S(2)}) %collective-permute-start.12) | collective-permute-done | bytes 65568 | tf_op jit(solution)/shard_map/ppermute | solution.py:32
  148.4 11.0 %project_own.1 = (bf16[8,256,1024]{2,1,0:T(8,128)(2,1)S(1)}, bf16[8,256,256]{2,1,0:T(8,128)(2,1)S(1)}, bf16[8,256,256]{2,1,0:T(8,128)(2,1)S(1)}, bf16[8,256,256]{2,1,0:T(8,128)(2,1)S(1)}) custom-call(s32[1]{0:T(128)} %bitcast.row_ref.refs_0_, bf16[8,64,1024]{2,1,0:T(8,128)(2,1)S(1)} %copy-done.4, bf16[8,64,1024]{2,1,0:T(8,128)(2,1)S(1)} %collective-permute-done.refs_2_, ...), custom_call_target="tpu_custom_call" | custom-call | flops 3221225472 | bytes 12582912 | tf_op jit(solution)/shard_map/project_own/pallas_call | solution.py:282
  161.4 8.5 %project_prev.1 = (bf16[7,256,256]{2,1,0:T(8,128)(2,1)S(1)}, bf16[7,256,256]{2,1,0:T(8,128)(2,1)S(1)}) custom-call(s32[1]{0:T(128)} %bitcast.row_ref.refs_0_, bf16[7,64,1024]{2,1,0:T(8,128)(2,1)} %collective-permute-done.8.refs_1_, bf16[7,64,1024]{2,1,0:T(8,128)(2,1)S(1)} %collective-permute-done.9.refs_2_, ...), custom_call_target="tpu_custom_call" | custom-call | flops 2818572288 | bytes 11534336 | tf_op jit(solution)/shard_map/project_prev/pallas_call | solution.py:282
  170.2 29.8 %attend.1 = (bf16[8,64,256]{2,1,0:T(8,128)(2,1)S(1)}, bf16[8,64,256]{2,1,0:T(8,128)(2,1)S(1)}, bf16[8,64,256]{2,1,0:T(8,128)(2,1)S(1)}, bf16[8,64,256]{2,1,0:T(8,128)(2,1)S(1)}, f32[8,8,256]{2,1,0:T(8,128)S(1)}) custom-call(s32[8]{0:T(128)S(1)} %copy-done.21, bf16[8,256,256]{2,1,0:T(8,128)(2,1)S(1)} %get-tuple-element.96.q.refs_1_, ...), custom_call_target="tpu_custom_call" | custom-call | flops 9663676416 | bytes 6291456 | tf_op jit(solution)/shard_map/attend/pallas_call | solution.py:367
  202.7 7.7 %collective-permute-done.14.o2.t2 = bf16[8,64,256]{2,1,0:T(8,128)(2,1)S(1)} collective-permute-done((bf16[8,64,256]{2,1,0:T(8,128)(2,1)S(1)}, bf16[8,64,256]{2,1,0:T(8,128)(2,1)S(1)}, u32[]{:S(2)}, u32[]{:S(2)}) %collective-permute-start.14) | collective-permute-done | bytes 262176 | tf_op jit(solution)/shard_map/ppermute | solution.py:27
  210.4 8.3 %collective-permute-done.15.o3.t3 = bf16[8,64,256]{2,1,0:T(8,128)(2,1)S(1)} collective-permute-done((bf16[8,64,256]{2,1,0:T(8,128)(2,1)S(1)}, bf16[8,64,256]{2,1,0:T(8,128)(2,1)S(1)}, u32[]{:S(2)}, u32[]{:S(2)}) %collective-permute-start.15) | collective-permute-done | bytes 262176 | tf_op jit(solution)/shard_map/ppermute | solution.py:27
  222.9 25.5 %feed.1 = (bf16[512,4096]{1,0:T(8,128)(2,1)}, bf16[512,4096]{1,0:T(8,128)(2,1)}, f32[512,1024]{1,0:T(8,128)S(1)}, f32[8,512]{1,0:T(8,128)S(1)}) custom-call(s32[1]{0:T(128)} %bitcast.row_ref.refs_0_, bf16[512,1024]{1,0:T(8,128)(2,1)S(1)} %bitcast.74, bf16[512,1024]{1,0:T(8,128)(2,1)S(1)} %bitcast.76, bf16[256,4096]{1,0:T(8,128)(2,1)} %u0.1, ...), custom_call_target="tpu_custom_call" | custom-call | flops 12884901888 | bytes 31457280 | tf_op jit(solution)/shard_map/feed/pallas_call | solution.py:669
  251.5 28.7 %feed_back.1 = (bf16[2,4,256,1024]{3,2,1,0:T(8,128)(2,1)}, bf16[2,4,256,1024]{3,2,1,0:T(8,128)(2,1)}, bf16[2,1024,1024]{2,1,0:T(8,128)(2,1)}, bf16[2,1024,1024]{...) custom-call(s32[1]{0:T(128)} %bitcast.row_ref.refs_0_, bf16[512,1024]{1,0:T(8,128)(2,1)S(1)} %bitcast.75, ...), custom_call_target="tpu_custom_call" | custom-call | flops 12884901888 | bytes 41943040 | tf_op jit(solution)/shard_map/feed_back/pallas_call | solution.py:746
  289.0 6.7 collective-permute-done.26.refs_6_
  299.7 17.9 %attend_back_prev.1 = (f32[8,256,256]{2,1,0:T(8,128)S(1)}, bf16[7,256,256]{2,1,0:T(8,128)(2,1)}, bf16[7,256,256]{2,1,0:T(8,128)(2,1)}) custom-call(s32[8]{0:T(128)S(1)} %copy-done.21, bf16[8,256,256]{2,1,0:T(8,128)(2,1)S(1)} %copy-done.63, bf16[7,256,256]{2,1,0:T(8,128)(2,1)S(1)} %copy-done.59, bf16[7,256,256]{2,1,0:T(8,128)(2,1)S(1)} %copy-done.61, ...), custom_call_target="tpu_custom_call" | custom-call | flops 8053063680 | bytes 12582912 | tf_op jit(solution)/shard_map/attend_back_prev/pallas_call | solution.py:486
  323.1 10.6 %core_sum.1 = bf16[2,2304,1024]{2,1,0:T(8,128)(2,1)S(1)} custom-call(bf16[2,1024,1024]{2,1,0:T(8,128)(2,1)S(1)} %bitcast.71, bf16[2,1024,1024]{2,1,0:T(8,128)(2,1)} %bitcast.5.ub, bf16[2,1024,1024]{2,1,0:T(8,128)(2,1)S(1)} %copy-done.7, bf16[2,1024,1024]{2,1,0:T(8,128)(2,1)} %collective-permute-done.29.db, bf16[2,256,1024]{2,1,0:T(8,128)(2,1)S(1)} %get-tuple-element.123.oa, ...), custom_call_target="tpu_custom_call" | custom-call | flops 4718592 | bytes 29360128 | tf_op jit(solution)/shard_map/core_sum/pallas_call | solution.py:804
  348.4 25.8 %attend_back_own.1 = (bf16[8,256,256]{2,1,0:T(8,128)(2,1)S(1)}, f32[8,256,256]{2,1,0:T(8,128)S(1)}, f32[8,256,256]{2,1,0:T(8,128)S(1)}) custom-call(s32[8]{0:T(128)S(1)} %copy-done.21, bf16[8,256,256]{2,1,0:T(8,128)(2,1)S(1)} %copy-done.64, bf16[8,256,256]{2,1,0:T(8,128)(2,1)S(1)} %copy-done.66, bf16[8,256,256]{2,1,0:T(8,128)(2,1)S(1)} %copy-done.68, ...), custom_call_target="tpu_custom_call" | custom-call | flops 20132659200 | bytes 12582912 | tf_op jit(solution)/shard_map/attend_back_own/pallas_call | solution.py:486
  376.4 8.7 %project_back.1 = (bf16[8,256,768]{2,1,0:T(8,128)(2,1)S(1)}, bf16[8,64,1024]{2,1,0:T(8,128)(2,1)S(1)}, bf16[8,64,1024]{2,1,0:T(8,128)(2,1)S(1)}, bf16[2,8,64,1024]{3,2,1,0:T(8,128)(2,1)S(1)}, f32[8,512]{1,0:T(8,128)S(1)}) custom-call(s32[1]{0:T(128)} %bitcast.row_ref.refs_0_, bf16[8,256,256]{2,1,0:T(8,128)(2,1)S(1)} %get-tuple-element.136.dq, ...), custom_call_target="tpu_custom_call" | custom-call | flops 3221225472 | bytes 14680064 | tf_op jit(solution)/shard_map/project_back/pallas_call | solution.py:878
  386.4 5.5 project_weight.1
  392.7 70.6 %reduce-scatter.3.cloned.1.call-done = bf16[4,16,768]{2,1,0:T(8,128)(2,1)} async-done(((bf16[4,256,768]{2,1,0:T(8,128)(2,1)}), bf16[4,16,768]{2,1,0:T(8,128)(2,1)}) %reduce-scatter.3.cloned.1.call-update) | async-done | bytes 98320 | tf_op jit(solution)/shard_map/reduce_scatter | solution.py:1169
  464.8 4.9 collective-permute-done.63
  481.0 72.6 %reduce-scatter.5.cloned.1.call-done = bf16[2,144,1024]{2,1,0:T(8,128)(2,1)} async-done(((bf16[2,2304,1024]{2,1,0:T(8,128)(2,1)}), bf16[2,144,1024]{2,1,0:T(8,128)(2,1)}) %reduce-scatter.5.cloned.1.call-update) | async-done | bytes 589840 | tf_op jit(solution)/shard_map/reduce_scatter | solution.py:1148
  556.8 5.8 collective-permute-done.67
  576.9 5.8 collective-permute-done.38
  594.0 22.2 %collective-permute-done.34.far = bf16[8,64,1024]{2,1,0:T(8,128)(2,1)S(1)} collective-permute-done((bf16[8,64,1024]{2,1,0:T(8,128)(2,1)S(1)}, bf16[8,64,1024]{2,1,0:T(8,128)(2,1)S(1)}, u32[]{:S(2)}, u32[]{:S(2)}) %collective-permute-start.34) | collective-permute-done | bytes 1048608 | tf_op jit(solution)/shard_map/ppermute | solution.py:27
  618.5 4.2 input_back.1
  641.2 6.1 collective-permute-done.43
  647.9 7.1 collective-permute-done.44
  665.6 11.2 %collective-permute-done.55.refs_7_ = bf16[8,8,4864]{2,1,0:T(8,128)(2,1)S(1)} collective-permute-done((bf16[8,8,4864]{2,1,0:T(8,128)(2,1)S(1)}, bf16[8,8,4864]{2,1,0:T(8,128)(2,1)S(1)}, u32[]{:S(2)}, u32[]{:S(2)}) %collective-permute-start.55) | collective-permute-done | bytes 622624 | tf_op jit(solution)/shard_map/ppermute | solution.py:27
  677.8 13.6 %collective-permute-done.53.refs_5_ = bf16[8,8,4864]{2,1,0:T(8,128)(2,1)S(1)} collective-permute-done((bf16[8,8,4864]{2,1,0:T(8,128)(2,1)S(1)}, bf16[8,8,4864]{2,1,0:T(8,128)(2,1)S(1)}, u32[]{:S(2)}, u32[]{:S(2)}) %collective-permute-start.53) | collective-permute-done | bytes 622624 | tf_op jit(solution)/shard_map/ppermute | solution.py:27
  691.6 8.2 %collective-permute-done.47.refs_2_ = bf16[8,8,2560]{2,1,0:T(8,128)(2,1)S(1)} collective-permute-done((bf16[8,8,2560]{2,1,0:T(8,128)(2,1)S(1)}, bf16[8,8,2560]{2,1,0:T(8,128)(2,1)S(1)}, u32[]{:S(2)}, u32[]{:S(2)}) %collective-permute-start.47) | collective-permute-done | bytes 327712 | tf_op jit(solution)/shard_map/ppermute | solution.py:27
  702.5 6.1 final_sums.1
  715.6 6.2 unpack.1
  (347 shorter events, 154.7 us)
Async XLA Ops:
  7.2 456.1 %reduce-scatter.3.cloned.1.call-start = ((), (), s32[]{:S(2)}) async-start(), calls=%async_computation.2 | async-start | bytes 1671168 | tf_op jit(solution)/shard_map/reduce_scatter | solution.py:1169
  7.2 50.8 %collective-permute-start.1 = (bf16[8,64,1024]{2,1,0:T(8,128)(2,1)}, bf16[8,64,1024]{2,1,0:T(8,128)(2,1)}, u32[]{:S(2)}, u32[]{:S(2)}) collective-permute-start(bf16[8,64,1024]{2,1,0:T(8,128)(2,1)} %x.3), channel_id=1, source_target_pairs={{0,2},{1,3},{2,0},{3,1},{4,6},{5,7},{6,4},{7,5},{8,10},{9,11},{10,... | collective-permute-start | bytes 3145736 | tf_op jit(solution)/shard_map/ppermute | solution.py:27
  9.4 48.6 %collective-permute-start.8 = (bf16[7,64,1024]{2,1,0:T(8,128)(2,1)S(1)}, bf16[7,64,1024]{2,1,0:T(8,128)(2,1)}, u32[]{:S(2)}, u32[]{:S(2)}) collective-permute-start(bf16[7,64,1024]{2,1,0:T(8,128)(2,1)S(1)} %slice.35), channel_id=1, source_target_pairs={{0,4},{1,5},{2,6},{3,7},{4,8},{5,9},{6,10},{7,11},{8,12},{9,13},{1... | collective-permute-start | bytes 2752520 | tf_op jit(solution)/shard_map/ppermute | solution.py:32
  71.2 75.9 %collective-permute-start.20 = (bf16[256,4096]{1,0:T(8,128)(2,1)}, bf16[256,4096]{1,0:T(8,128)(2,1)S(1)}, u32[]{:S(2)}, u32[]{:S(2)}) collective-permute-start(bf16[256,4096]{1,0:T(8,128)(2,1)} %u0.1), channel_id=1, source_target_pairs={{0,66},{1,67},{2,64},{3,65},{4,70},{5,71},{6,68},{7,69},{8,74},{9,... | collective-permute-start | bytes 6291464 | tf_op jit(solution)/shard_map/ppermute | solution.py:27
  79.6 68.5 %collective-permute-start.23 = (bf16[1024,1024]{1,0:T(8,128)(2,1)}, bf16[1024,1024]{1,0:T(8,128)(2,1)S(1)}, u32[]{:S(2)}, u32[]{:S(2)}) collective-permute-start(bf16[1024,1024]{1,0:T(8,128)(2,1)} %d0.3), channel_id=1, source_target_pairs={{0,2},{1,3},{2,0},{3,1},{4,6},{5,7},{6,4},{7,5},{8,10},{9,11},{10,... | collective-permute-start | bytes 6291464 | tf_op jit(solution)/shard_map/ppermute | solution.py:27
  80.5 62.5 %collective-permute-start = (bf16[8,64,1024]{2,1,0:T(8,128)(2,1)S(1)}, bf16[8,64,1024]{2,1,0:T(8,128)(2,1)S(1)}, u32[]{:S(2)}, u32[]{:S(2)}) collective-permute-start(bf16[8,64,1024]{2,1,0:T(8,128)(2,1)S(1)} %copy-done.4), channel_id=1, source_target_pairs={{0,1},{1,0},{2,3},{3,2},{4,5},{5,4},{6,7},{7,6},{8,9},{9,8},{10,11... | collective-permute-start | bytes 3145736 | tf_op jit(solution)/shard_map/ppermute | solution.py:27
  84.6 45.8 %collective-permute-start.4 = (f32[8,7424]{1,0:T(8,128)S(1)}, f32[8,7424]{1,0:T(8,128)S(1)}, u32[]{:S(2)}, u32[]{:S(2)}) collective-permute-start(f32[8,7424]{1,0:T(8,128)S(1)} %add.49), channel_id=1, source_target_pairs={{0,2},{1,3},{2,0},{3,1},{4,6},{5,7},{6,4},{7,5},{8,10},{9,11},{10,... | collective-permute-start | bytes 712712 | tf_op jit(solution)/shard_map/ppermute | solution.py:27
  85.9 44.6 %collective-permute-start.6 = (bf16[256,768]{1,0:T(8,128)(2,1)S(1)}, bf16[256,768]{1,0:T(8,128)(2,1)S(1)}, u32[]{:S(2)}, u32[]{:S(2)}) collective-permute-start(bf16[256,768]{1,0:T(8,128)(2,1)S(1)} %get-tuple-element.91), channel_id=1, source_target_pairs={{0,66},{1,67},{2,64},{3,65},{4,70},{5,71},{6,68},{7,69},{8,74},{9,... | collective-permute-start | bytes 1179656 | tf_op jit(solution)/shard_map/ppermute | solution.py:27
  146.6 23.3 %collective-permute-start.16 = (bf16[256,1024]{1,0:T(8,128)(2,1)S(1)}, bf16[256,1024]{1,0:T(8,128)(2,1)S(1)}, u32[]{:S(2)}, u32[]{:S(2)}) collective-permute-start(bf16[256,1024]{1,0:T(8,128)(2,1)S(1)} %copy-done.13), channel_id=1, source_target_pairs={{0,1},{1,0},{2,3},{3,2},{4,5},{5,4},{6,7},{7,6},{8,9},{9,8},{10,11... | collective-permute-start | bytes 1572872 | tf_op jit(solution)/shard_map/ppermute | solution.py:27
  146.7 76.2 %collective-permute-start.19 = (bf16[256,4096]{1,0:T(8,128)(2,1)}, bf16[256,4096]{1,0:T(8,128)(2,1)}, u32[]{:S(2)}, u32[]{:S(2)}) collective-permute-start(bf16[256,4096]{1,0:T(8,128)(2,1)} %u0.1), channel_id=1, source_target_pairs={{0,1},{1,0},{2,3},{3,2},{4,5},{5,4},{6,7},{7,6},{8,9},{9,8},{10,11... | collective-permute-start | bytes 6291464 | tf_op jit(solution)/shard_map/ppermute | solution.py:27
  147.1 75.8 %collective-permute-start.22 = (bf16[1024,1024]{1,0:T(8,128)(2,1)}, bf16[1024,1024]{1,0:T(8,128)(2,1)}, u32[]{:S(2)}, u32[]{:S(2)}) collective-permute-start(bf16[1024,1024]{1,0:T(8,128)(2,1)} %d0.3), channel_id=1, source_target_pairs={{0,1},{1,0},{2,3},{3,2},{4,5},{5,4},{6,7},{7,6},{8,9},{9,8},{10,11... | collective-permute-start | bytes 6291464 | tf_op jit(solution)/shard_map/ppermute | solution.py:27
  147.9 75.0 %collective-permute-start.21 = (bf16[256,4096]{1,0:T(8,128)(2,1)S(1)}, bf16[256,4096]{1,0:T(8,128)(2,1)}, u32[]{:S(2)}, u32[]{:S(2)}) collective-permute-start(bf16[256,4096]{1,0:T(8,128)(2,1)S(1)} %collective-permute-done.20.u2), channel_id=1, source_target_pairs={{0,1},{1,0},{2,3},{3,2},{4,5},{5,4},{6,7},{7,6},{8,9},{9,8},{10,11... | collective-permute-start | bytes 6291464 | tf_op jit(solution)/shard_map/ppermute | solution.py:27
  148.0 74.9 %collective-permute-start.24 = (bf16[1024,1024]{1,0:T(8,128)(2,1)S(1)}, bf16[1024,1024]{1,0:T(8,128)(2,1)}, u32[]{:S(2)}, u32[]{:S(2)}) collective-permute-start(bf16[1024,1024]{1,0:T(8,128)(2,1)S(1)} %collective-permute-done.23.d2), channel_id=1, source_target_pairs={{0,1},{1,0},{2,3},{3,2},{4,5},{5,4},{6,7},{7,6},{8,9},{9,8},{10,11... | collective-permute-start | bytes 6291464 | tf_op jit(solution)/shard_map/ppermute | solution.py:27
  169.9 30.1 %collective-permute-start.18 = (bf16[256,1024]{1,0:T(8,128)(2,1)S(1)}, bf16[256,1024]{1,0:T(8,128)(2,1)S(1)}, u32[]{:S(2)}, u32[]{:S(2)}) collective-permute-start(bf16[256,1024]{1,0:T(8,128)(2,1)S(1)} %collective-permute-done.17.w2), channel_id=1, source_target_pairs={{0,1},{1,0},{2,3},{3,2},{4,5},{5,4},{6,7},{7,6},{8,9},{9,8},{10,11... | collective-permute-start | bytes 1572872 | tf_op jit(solution)/shard_map/ppermute | solution.py:27
  280.2 42.8 %collective-permute-start.28 = (bf16[2,4,256,1024]{3,2,1,0:T(8,128)(2,1)}, bf16[2,4,256,1024]{3,2,1,0:T(8,128)(2,1)}, u32[]{:S(2)}, u32[]{:S(2)}) collective-permute-start(bf16[2,4,256,1024]{3,2,1,0:T(8,128)(2,1)} %get-tuple-element.131), channel_id=1, source_target_pairs={{0,1},{1,0},{2,3},{3,2},{4,5},{5,4},{6,7},{7,6},{8,9},{9,8},{10,11... | collective-permute-start | bytes 12582920 | tf_op jit(solution)/shard_map/ppermute | solution.py:27
  280.3 42.7 %collective-permute-start.29 = (bf16[2,1024,1024]{2,1,0:T(8,128)(2,1)}, bf16[2,1024,1024]{2,1,0:T(8,128)(2,1)}, u32[]{:S(2)}, u32[]{:S(2)}) collective-permute-start(bf16[2,1024,1024]{2,1,0:T(8,128)(2,1)} %get-tuple-element.133), channel_id=1, source_target_pairs={{0,1},{1,0},{2,3},{3,2},{4,5},{5,4},{6,7},{7,6},{8,9},{9,8},{10,11... | collective-permute-start | bytes 12582920 | tf_op jit(solution)/shard_map/ppermute | solution.py:27
  286.1 37.0 %collective-permute-start.30 = (bf16[2,256,1024]{2,1,0:T(8,128)(2,1)S(1)}, bf16[2,256,1024]{2,1,0:T(8,128)(2,1)S(1)}, u32[]{:S(2)}, u32[]{:S(2)}) collective-permute-start(bf16[2,256,1024]{2,1,0:T(8,128)(2,1)S(1)} %get-tuple-element.134), channel_id=1, source_target_pairs={{0,1},{1,0},{2,3},{3,2},{4,5},{5,4},{6,7},{7,6},{8,9},{9,8},{10,11... | collective-permute-start | bytes 3145736 | tf_op jit(solution)/shard_map/ppermute | solution.py:27
  319.0 55.3 %collective-permute-start.31 = (bf16[7,256,256]{2,1,0:T(8,128)(2,1)}, bf16[7,256,256]{2,1,0:T(8,128)(2,1)S(1)}, u32[]{:S(2)}, u32[]{:S(2)}) collective-permute-start(bf16[7,256,256]{2,1,0:T(8,128)(2,1)} %get-tuple-element.139), channel_id=1, source_target_pairs={{4,0},{5,1},{6,2},{7,3},{8,4},{9,5},{10,6},{11,7},{12,8},{13,9},{1... | collective-permute-start | bytes 2752520 | tf_op jit(solution)/shard_map/ppermute | solution.py:32
  321.1 54.0 %collective-permute-start.32 = (bf16[7,256,256]{2,1,0:T(8,128)(2,1)}, bf16[7,256,256]{2,1,0:T(8,128)(2,1)}, u32[]{:S(2)}, u32[]{:S(2)}) collective-permute-start(bf16[7,256,256]{2,1,0:T(8,128)(2,1)} %get-tuple-element.140), channel_id=1, source_target_pairs={{4,0},{5,1},{6,2},{7,3},{8,4},{9,5},{10,6},{11,7},{12,8},{13,9},{1... | collective-permute-start | bytes 2752520 | tf_op jit(solution)/shard_map/ppermute | solution.py:32
  391.9 161.7 %reduce-scatter.5.cloned.1.call-start = ((), (), s32[]{:S(2)}) async-start(), calls=%async_computation.4 | async-start | bytes 10027008 | tf_op jit(solution)/shard_map/reduce_scatter | solution.py:1148
  392.7 317.2 %all-gather.3.cloned.1.call-start = ((), (), s32[]{:S(2)}) async-start(), calls=%async_computation.3 | async-start | bytes 1671168 | tf_op jit(solution)/shard_map/all_gather | solution.py:1173
  481.0 232.3 %all-gather.5.cloned.1.call-start = ((), (), s32[]{:S(2)}) async-start(), calls=%async_computation.5 | async-start | bytes 5013504 | tf_op jit(solution)/shard_map/all_gather | solution.py:1154
  584.2 72.0 %collective-permute-start.62 = (bf16[8,8,256]{2,1,0:T(8,128)(2,1)S(1)}, bf16[8,8,256]{2,1,0:T(8,128)(2,1)S(1)}, u32[]{:S(2)}, u32[]{:S(2)}) collective-permute-start(bf16[8,8,256]{2,1,0:T(8,128)(2,1)S(1)} %constant_dynamic-update-slice_fusion.10.refs_8_), channel_id=1, source_target_pairs={{0,12},{1,13},{2,14},{3,15},{4,8},{5,9},{6,10},{7,11},{8,4},{9,5},... | collective-permute-start | bytes 98312 | tf_op jit(solution)/shard_map/ppermute | solution.py:27
  586.4 75.3 %collective-permute-start.61 = (bf16[8,8,256]{2,1,0:T(8,128)(2,1)S(1)}, bf16[8,8,256]{2,1,0:T(8,128)(2,1)S(1)}, u32[]{:S(2)}, u32[]{:S(2)}) collective-permute-start(bf16[8,8,256]{2,1,0:T(8,128)(2,1)S(1)} %constant_dynamic-update-slice_fusion.10.refs_8_), channel_id=1, source_target_pairs={{0,8},{1,9},{2,10},{3,11},{4,12},{5,13},{6,14},{7,15},{8,0},{9,1},... | collective-permute-start | bytes 98312 | tf_op jit(solution)/shard_map/ppermute | solution.py:27
  588.7 41.6 %collective-permute-start.52 = (bf16[2,8,4864]{2,1,0:T(8,128)(2,1)S(1)}, bf16[2,8,4864]{2,1,0:T(8,128)(2,1)S(1)}, u32[]{:S(2)}, u32[]{:S(2)}) collective-permute-start(bf16[2,8,4864]{2,1,0:T(8,128)(2,1)S(1)} %pad_maximum_fusion), channel_id=1, source_target_pairs={{0,48},{1,49},{2,50},{3,51},{4,52},{5,53},{6,54},{7,55},{8,56},{9,... | collective-permute-start | bytes 466952 | tf_op jit(solution)/shard_map/ppermute | solution.py:27
  590.9 31.8 %collective-permute-start.50 = (bf16[2,8,4864]{2,1,0:T(8,128)(2,1)S(1)}, bf16[2,8,4864]{2,1,0:T(8,128)(2,1)S(1)}, u32[]{:S(2)}, u32[]{:S(2)}) collective-permute-start(bf16[2,8,4864]{2,1,0:T(8,128)(2,1)S(1)} %pad_maximum_fusion), channel_id=1, source_target_pairs={{0,16},{1,17},{2,18},{3,19},{4,20},{5,21},{6,22},{7,23},{8,24},{9,... | collective-permute-start | bytes 466952 | tf_op jit(solution)/shard_map/ppermute | solution.py:27
  631.5 31.4 %collective-permute-start.60 = (bf16[8,8,256]{2,1,0:T(8,128)(2,1)S(1)}, bf16[8,8,256]{2,1,0:T(8,128)(2,1)S(1)}, u32[]{:S(2)}, u32[]{:S(2)}) collective-permute-start(bf16[8,8,256]{2,1,0:T(8,128)(2,1)S(1)} %constant_dynamic-update-slice_fusion.10.refs_8_), channel_id=1, source_target_pairs={{0,4},{1,5},{2,6},{3,7},{4,0},{5,1},{6,2},{7,3},{8,12},{9,13},{10,... | collective-permute-start | bytes 98312 | tf_op jit(solution)/shard_map/ppermute | solution.py:27
  633.3 43.5 %collective-permute-start.55 = (bf16[8,8,4864]{2,1,0:T(8,128)(2,1)S(1)}, bf16[8,8,4864]{2,1,0:T(8,128)(2,1)S(1)}, u32[]{:S(2)}, u32[]{:S(2)}) collective-permute-start(bf16[8,8,4864]{2,1,0:T(8,128)(2,1)S(1)} %constant_dynamic-update-slice_fusion.5.refs_4_), channel_id=1, source_target_pairs={{0,12},{1,13},{2,14},{3,15},{4,8},{5,9},{6,10},{7,11},{8,4},{9,5},... | collective-permute-start | bytes 1867784 | tf_op jit(solution)/shard_map/ppermute | solution.py:27
  661.4 30.0 %collective-permute-start.53 = (bf16[8,8,4864]{2,1,0:T(8,128)(2,1)S(1)}, bf16[8,8,4864]{2,1,0:T(8,128)(2,1)S(1)}, u32[]{:S(2)}, u32[]{:S(2)}) collective-permute-start(bf16[8,8,4864]{2,1,0:T(8,128)(2,1)S(1)} %constant_dynamic-update-slice_fusion.5.refs_4_), channel_id=1, source_target_pairs={{0,4},{1,5},{2,6},{3,7},{4,0},{5,1},{6,2},{7,3},{8,12},{9,13},{10,... | collective-permute-start | bytes 1867784 | tf_op jit(solution)/shard_map/ppermute | solution.py:27
  661.6 30.0 %collective-permute-start.48 = (bf16[8,8,2560]{2,1,0:T(8,128)(2,1)S(1)}, bf16[8,8,2560]{2,1,0:T(8,128)(2,1)S(1)}, u32[]{:S(2)}, u32[]{:S(2)}) collective-permute-start(bf16[8,8,2560]{2,1,0:T(8,128)(2,1)S(1)} %constant_dynamic-update-slice_fusion.refs_0_), channel_id=1, source_target_pairs={{0,12},{1,13},{2,14},{3,15},{4,8},{5,9},{6,10},{7,11},{8,4},{9,5},... | collective-permute-start | bytes 983048 | tf_op jit(solution)/shard_map/ppermute | solution.py:27
  662.9 36.9 %collective-permute-start.47 = (bf16[8,8,2560]{2,1,0:T(8,128)(2,1)S(1)}, bf16[8,8,2560]{2,1,0:T(8,128)(2,1)S(1)}, u32[]{:S(2)}, u32[]{:S(2)}) collective-permute-start(bf16[8,8,2560]{2,1,0:T(8,128)(2,1)S(1)} %constant_dynamic-update-slice_fusion.refs_0_), channel_id=1, source_target_pairs={{0,8},{1,9},{2,10},{3,11},{4,12},{5,13},{6,14},{7,15},{8,0},{9,1},... | collective-permute-start | bytes 983048 | tf_op jit(solution)/shard_map/ppermute | solution.py:27
  676.8 25.7 %collective-permute-start.46 = (bf16[8,8,2560]{2,1,0:T(8,128)(2,1)S(1)}, bf16[8,8,2560]{2,1,0:T(8,128)(2,1)S(1)}, u32[]{:S(2)}, u32[]{:S(2)}) collective-permute-start(bf16[8,8,2560]{2,1,0:T(8,128)(2,1)S(1)} %constant_dynamic-update-slice_fusion.refs_0_), channel_id=1, source_target_pairs={{0,4},{1,5},{2,6},{3,7},{4,0},{5,1},{6,2},{7,3},{8,12},{9,13},{10,... | collective-permute-start | bytes 983048 | tf_op jit(solution)/shard_map/ppermute | solution.py:27
  (120 other events, 2065.4 us)
Sparse Core Ops, SparseCore 0:
  392.1 71.2 reduce-scatter.2
  466.8 86.8 reduce-scatter.4
  556.0 44.4 all-gather.2
  603.4 87.8 all-gather.4
